TPU v7x, 256 devices: a whole 4x4x8 slice. The times are simulated.
256 devices in a mesh: pair: 16 (over z_lo, y), aux: 16 (over z_hi, x, core).
Axes of the slice: x: 4, y: 4, z: 8 (z_hi: 2, z_lo: 4; z = z_hi * 4 + z_lo), core: 2. Of those that a mesh axis runs over, the one named last changes fastest.
Arguments:
- amplitudes: float32 [896, 16, 896], P('aux', 'pair'), may hold values from -6 to 6
- fitting: float32 [16, 896, 896], P('aux', 'pair'), may hold values from -0.09375 to 0.09375
Outputs:
- ladder: float32 [896, 16, 896], P('aux', 'pair')
All inputs are finite; a program needn't handle non-finite values.
Results may differ from a plain program's by a relative error of at most 0.0001.
Values sent between devices are 32-bit elements; how exact they have to be, the bound alone decides.
No kernel may reach another device: no remote copies, remote signals or barrier semaphores. Data moves between devices by JAX's collectives and lax.ppermute only.
A program may use at most 64 MiB of HBM per device.

v0:
```python
import jax
import jax.numpy as jnp
from jax import lax
from jax.sharding import PartitionSpec as P


def per_device(amplitudes, fitting):
    width = amplitudes.shape[2]
    pair_dev = amplitudes.shape[1]
    count_fit = fitting.shape[0]
    whole_fit = lax.all_gather(fitting, "pair", axis=1, tiled=True)
    whole_amp = lax.all_gather(amplitudes, "aux", axis=0, tiled=True)
    halves = jnp.einsum(
        "rpd,lbd->lrpb",
        whole_amp,
        whole_fit,
        precision=lax.Precision.HIGHEST,
        preferred_element_type=jnp.float32,
    )
    halves = halves.reshape(count_fit, width, pair_dev * width)
    term = jnp.einsum(
        "lac,lcx->ax",
        whole_fit,
        halves,
        precision=lax.Precision.HIGHEST,
        preferred_element_type=jnp.float32,
    )
    result = lax.psum_scatter(term, "aux", scatter_dimension=0, tiled=True)
    return result.reshape(result.shape[0], pair_dev, width)


def solution(mesh):
    in_specs = (P("aux", "pair", None), P("aux", "pair", None))
    out_specs = P("aux", "pair", None)
    return jax.shard_map(
        per_device, mesh=mesh, in_specs=in_specs, out_specs=out_specs, check_vma=False
    )
```

profile of v0, /device:TPU:32, one launch (start us, length us, event | category | flops | bytes accessed | tf_op | source)
XLA Modules:
  0.0 391.2 jit_solution(5764895174386948802)
XLA Ops:
  6.5 0.0 all-gather.3.cloned.1.call-start
  6.5 0.7 all-gather.3.cloned.1.call-update
  7.3 0.0 all-gather.5.cloned.1.call-start
  7.3 0.7 all-gather.5.cloned.1.call-update
  8.0 0.0 all-reduce.3.cloned.1.call-start
  8.1 83.3 %all-gather.3.cloned.1.call-done = f32[1,896,896]{2,1,0:T(8,128)} async-done(((f32[1,56,896]{2,1,0:T(8,128)}), f32[1,896,896]{2,1,0:T(8,128)}) %all-gather.3.cloned.1.call-update) | async-done | bytes 3211280 | tf_op jit(solution)/shard_map/all_gather | solution.py:11
  91.4 0.0 copy-start
  91.4 77.3 %all-gather.5.cloned.1.call-done = f32[896,1,896]{2,1,0:T(1,128)} async-done(((f32[56,1,896]{2,1,0:T(1,128)}), f32[896,1,896]{2,1,0:T(1,128)}) %all-gather.5.cloned.1.call-update) | async-done | bytes 3211280 | tf_op jit(solution)/shard_map/all_gather | solution.py:12
  168.7 14.7 %fusion = f32[896,896]{1,0:T(8,128)S(1)} fusion(f32[896,1,896]{2,1,0:T(1,128)} %all-gather.5.cloned.1.call-done, f32[1,896,896]{2,1,0:T(8,128)} %all-gather.3.cloned.1.call-done), kind=kOutput, calls=%fused_computation | convolution fusion | flops 8631877632 | bytes 9633792 | tf_op jit(solution)/shard_map/rpd,lbd->lrpb/dot_general | solution.py:13
  183.4 0.0 copy-done
  183.4 13.3 %fusion.7 = f32[896,896]{0,1:T(8,128)} fusion(f32[1,896,896]{2,1,0:T(8,128)S(1)} %copy-done, f32[896,896]{1,0:T(8,128)S(1)} %fusion), kind=kOutput, calls=%fused_computation.7 | convolution fusion | flops 8631877632 | bytes 9633792 | tf_op jit(solution)/shard_map/lac,lcx->ax/dot_general | solution.py:21
  196.8 0.0 copy-start.1
  196.8 0.0 all-reduce.3.cloned.1.call-update
  196.8 0.6 copy-done.1
  197.5 0.6 dynamic-slice
  198.7 183.7 %all-reduce.3.cloned.1.call-done = f32[896,896]{0,1:T(8,128)} async-done(((f32[896,896]{0,1:T(8,128)}), f32[896,896]{0,1:T(8,128)}) %all-reduce.3.cloned.1.call-update) | async-done | bytes 3211280
  382.4 1.4 dynamic-slice_bitcast_fusion
  383.8 0.9 copy.4
Async XLA Ops:
  6.5 84.8 %all-gather.3.cloned.1.call-start = ((), (), s32[]{:S(2)}) async-start(), calls=%async_computation | async-start | bytes 3411968 | tf_op jit(solution)/shard_map/all_gather | solution.py:11
  7.3 161.4 %all-gather.5.cloned.1.call-start = ((), (), s32[]{:S(2)}) async-start(), calls=%async_computation.1 | async-start | bytes 3411968 | tf_op jit(solution)/shard_map/all_gather | solution.py:12
  8.0 374.4 %all-reduce.3.cloned.1.call-start = ((), (), s32[]{:S(2)}) async-start(), calls=%async_computation.2 | async-start | bytes 6422528
  91.4 92.1 %copy-start = (f32[1,896,896]{2,1,0:T(8,128)S(1)}, f32[1,896,896]{2,1,0:T(8,128)}, u32[]{:S(2)}) copy-start(f32[1,896,896]{2,1,0:T(8,128)} %all-gather.3.cloned.1.call-done) | copy-start | bytes 9633796
  196.8 0.7 copy-start.1
Sparse Core Ops, SparseCore 0:
  9.1 82.1 all-gather.2
  94.0 74.6 all-gather.4
  196.9 185.4 all-reduce.2
where the time goes:
time: 392 us; the launch traced here: 391 us
  waiting for transfers between devices  346 us (88%)
  matrix products  28.1 us (7%)
  between operations  13.8 us (4%)
    unnamed x4, waiting for transfers between devices  185 us
    all_gather x1, waiting for transfers between devices, per_device(): whole_fit = lax.all_gather(fitting, 'pair', axis=1, tiled=True)  83.3 us
    all_gather x1, waiting for transfers between devices, per_device(): whole_amp = lax.all_gather(amplitudes, 'aux', axis=0, tiled=True)  77.3 us
    dot_general x1, matrix products, per_device(): jnp.einsum('rpd,lbd->lrpb', whole_amp, whole_fit, precision=lax.Precision...  14.7 us
    dot_general x1, matrix products, per_device(): jnp.einsum('lac,lcx->ax', whole_fit, halves, precision=lax.Precision.HIGH...  13.3 us
  transfers between devices with their start and end apart: 3, of which 3 were waited for; matrix products, arithmetic and copies ran while one was open for 0% of the time, Pallas kernels for 0%

commit v1 on v0

v1 whole, which is shorter than its diff:
```python
import jax
import jax.numpy as jnp
from jax import lax
from jax.experimental import pallas as pl
from jax.experimental.pallas import tpu as pltpu
from jax.sharding import PartitionSpec as P

NZL, NY, NZH, NX, NC = 4, 4, 2, 4, 2
V = 896
ROWS = 56
TILE = 128


def pair_permute(value, target):
    steps = []
    for zl in range(NZL):
        for y in range(NY):
            tz, ty = target(zl, y)
            steps.append((zl * NY + y, (tz % NZL) * NY + ty % NY))
    return lax.ppermute(value, "pair", steps)


def aux_permute(value, target):
    steps = []
    for zh in range(NZH):
        for x in range(NX):
            for c in range(NC):
                th, tx, tc = target(zh, x, c)
                steps.append(((zh * NX + x) * NC + c, ((th % NZH) * NX + tx % NX) * NC + tc % NC))
    return lax.ppermute(value, "aux", steps)


def split(value):
    high = value.astype(jnp.bfloat16)
    low = (value - high.astype(jnp.float32)).astype(jnp.bfloat16)
    return high, low


def ladder_kernel(place_ref, *refs):
    t_refs, b_refs = refs[:10], refs[10:26]
    keep_ref, send_ref = refs[26:28]
    t32, b32, t_hi, t_lo, b_hi, b_lo, sem = refs[28:]
    zl, y, zh, x, core = (place_ref[i] for i in range(5))
    copies = []
    for index in range(8):
        far, k = divmod(index, 4)
        block = ((zh + far) % NZH) * 8 + ((x - k + NX) % NX) * 2
        mine = pl.multiple_of((block + core) * ROWS, 8)
        other = pl.multiple_of((block + 1 - core) * ROWS, 8)
        copies.append(pltpu.make_async_copy(t_refs[index], t32.at[pl.ds(mine, ROWS)], sem.at[index]))
        copies.append(
            pltpu.make_async_copy(t_refs[8 + far].at[pl.ds(k * ROWS, ROWS)], t32.at[pl.ds(other, ROWS)], sem.at[8 + index])
        )
    for index in range(16):
        k, j = divmod(index, 4)
        row = pl.multiple_of(((zl ^ k) * NY + (y - j + NY) % NY) * ROWS, 8)
        copies.append(pltpu.make_async_copy(b_refs[index], b32.at[pl.ds(row, ROWS)], sem.at[16 + index]))
    for copy in copies:
        copy.start()
    for copy in copies:
        copy.wait()

    def load(i, carry):
        rows = pl.ds(pl.multiple_of(i * TILE, TILE), TILE)
        t_hi[rows], t_lo[rows] = split(t32[rows])
        b_hi[rows], b_lo[rows] = split(b32[rows])
        return carry

    lax.fori_loop(0, V // TILE, load, 0)

    def product(i, carry):
        rows = pl.ds(pl.multiple_of(i * TILE, TILE), TILE)
        nn = (((1,), (0,)), ((), ()))
        nt = (((1,), (1,)), ((), ()))

        def dot(left, right, dims):
            return lax.dot_general(left, right, dims, preferred_element_type=jnp.float32)

        high, low = b_hi[rows], b_lo[rows]
        g = dot(low, t_hi[...], nn) + dot(high, t_lo[...], nn) + dot(high, t_hi[...], nn)
        high, low = split(g)
        t32[rows] = dot(low, b_hi[...], nt) + dot(high, b_lo[...], nt) + dot(high, b_hi[...], nt)
        return carry

    lax.fori_loop(0, V // TILE, product, 0)

    copies = []
    for index in range(8):
        far, k = divmod(index, 4)
        block = ((zh + 1 - far) % NZH) * 8 + ((x + k) % NX) * 2
        mine = pl.multiple_of((block + core) * ROWS, 8)
        other = pl.multiple_of((block + 1 - core) * ROWS, 8)
        copies.append(pltpu.make_async_copy(t32.at[pl.ds(mine, ROWS)], keep_ref.at[index], sem.at[index]))
        copies.append(pltpu.make_async_copy(t32.at[pl.ds(other, ROWS)], send_ref.at[index], sem.at[8 + index]))
    for copy in copies:
        copy.start()
    for copy in copies:
        copy.wait()


def ladder_call(place, t_parts, b_parts):
    any_spec = pl.BlockSpec(memory_space=pl.ANY)
    out = jax.ShapeDtypeStruct((8, ROWS, V), jnp.float32)
    return pl.pallas_call(
        ladder_kernel,
        out_shape=(out, out),
        in_specs=[pl.BlockSpec(memory_space=pltpu.SMEM)] + [any_spec] * 26,
        out_specs=(any_spec, any_spec),
        scratch_shapes=[
            pltpu.VMEM((V, V), jnp.float32),
            pltpu.VMEM((V, V), jnp.float32),
            pltpu.VMEM((V, V), jnp.bfloat16),
            pltpu.VMEM((V, V), jnp.bfloat16),
            pltpu.VMEM((V, V), jnp.bfloat16),
            pltpu.VMEM((V, V), jnp.bfloat16),
            pltpu.SemaphoreType.DMA((32,)),
        ],
        compiler_params=pltpu.CompilerParams(vmem_limit_bytes=40 * 1024 * 1024),
        cost_estimate=pl.CostEstimate(flops=4 * 3 * V**3, bytes_accessed=4 * 4 * V * V, transcendentals=0),
        name="ladder",
    )(place, *t_parts, *b_parts)


def per_device(amplitudes, fitting):
    pair, aux = lax.axis_index("pair"), lax.axis_index("aux")
    place = jnp.stack([pair // NY, pair % NY, aux // 8, aux // 2 % NX, aux % 2]).astype(jnp.int32)
    amp = amplitudes.reshape(ROWS, V)
    fit = fitting.reshape(ROWS, V)

    with jax.named_scope("gather_fit"):
        shards = [fit] + [pair_permute(fit, lambda zl, y, k=k: (zl ^ k, y)) for k in (1, 2, 3)]
        b_parts = []
        for shard in shards:
            b_parts.append(shard)
            for j in (1, 2, 3):
                b_parts.append(pair_permute(shard, lambda zl, y, j=j: (zl, y + j)))

    with jax.named_scope("gather_amp"):
        far = aux_permute(amp, lambda zh, x, c: (zh + 1, x, c))
        t_parts, stacks = [], []
        for shard in (amp, far):
            parts = [shard] + [aux_permute(shard, lambda zh, x, c, k=k: (zh, x + k, c)) for k in (1, 2, 3)]
            t_parts += parts
            stacks.append(aux_permute(jnp.concatenate(parts), lambda zh, x, c: (zh, x, c + 1)))
        t_parts += stacks

    keep, send = ladder_call(place, t_parts, b_parts)

    with jax.named_scope("reduce"):
        halves = []
        for far in (0, 1):
            blocks = slice(4 * far, 4 * far + 4)
            got = aux_permute(send[blocks], lambda zh, x, c: (zh, x, c + 1))
            both = keep[blocks] + got
            total = both[0]
            for k in (1, 2, 3):
                total = total + aux_permute(both[k], lambda zh, x, c, k=k: (zh, x + k, c))
            halves.append(total)
        result = halves[1] + aux_permute(halves[0], lambda zh, x, c: (zh + 1, x, c))
    return result.reshape(ROWS, 1, V)


def solution(mesh):
    in_specs = (P("aux", "pair", None), P("aux", "pair", None))
    out_specs = P("aux", "pair", None)
    return jax.shard_map(
        per_device, mesh=mesh, in_specs=in_specs, out_specs=out_specs, check_vma=False
    )
```

time: 392 us -> 158 us (0.40)
  waiting for transfers between devices: 346 us -> 44.4 us
  starting transfers between devices: 0.08 us -> 58.6 us
  Pallas kernels: 0 us -> 32.6 us
  matrix products: 28.1 us -> 0 us
  local copies, waits for them, and re-layouts: 3.46 us -> 19.1 us
  between operations: 13.8 us -> 0.12 us
    unnamed x4 -> x0, waiting for transfers between devices: 185 us -> none
    all_gather x2 -> x0, waiting for transfers between devices: 161 us -> none  [the longest x1 83.3 us: per_device(): whole_fit = lax.all_gather(fitting, 'pair', axis=1, tiled=True)]
    ppermute x0 -> x33, starting transfers between devices: none -> 58.6 us  [the longest x18 36 us: aux_permute(): return lax.ppermute(value, 'aux', steps)]
    ppermute x0 -> x33, waiting for transfers between devices: none -> 44.4 us  [the longest x18 24.4 us: aux_permute(): return lax.ppermute(value, 'aux', steps)]
    pallas_call x0 -> x1, Pallas kernels: none -> 32.6 us  [ladder_call(): pl.pallas_call(ladder_kernel, out_shape=(out, out), in_specs=[pl.BlockSpe...]
    dot_general x2 -> x0, matrix products: 28.1 us -> none  [the longest x1 14.7 us: per_device(): jnp.einsum('rpd,lbd->lrpb', whole_amp, whole_fit, precision=lax.Precision...]
    unnamed x5 -> x47, local copies, waits for them, and re-layouts: 1.24 us -> 18 us
  transfers between devices with their start and end apart: 3 -> 33, of which waited for: 3 -> 20; matrix products, arithmetic and copies ran while one was open for 0% -> 1% of each run, Pallas kernels for 0% -> 0%
where the time goes in v1:
time: 158 us; the launch traced here: 157 us
  starting transfers between devices  58.6 us (37%)
  waiting for transfers between devices  44.4 us (28%)
  Pallas kernels  32.6 us (21%)
  local copies, waits for them, and re-layouts  19.1 us (12%)
  other arithmetic  2.3 us (1%)
    ppermute x18, starting transfers between devices, aux_permute(): return lax.ppermute(value, 'aux', steps)  36 us
    pallas_call x1, Pallas kernels, ladder_call(): pl.pallas_call(ladder_kernel, out_shape=(out, out), in_specs=[pl.BlockSpe...  32.6 us
    ppermute x18, waiting for transfers between devices, aux_permute(): return lax.ppermute(value, 'aux', steps)  24.4 us
    ppermute x15, starting transfers between devices, pair_permute(): return lax.ppermute(value, 'pair', steps)  22.6 us
    ppermute x15, waiting for transfers between devices, pair_permute(): return lax.ppermute(value, 'pair', steps)  20 us
    unnamed x47, local copies, waits for them, and re-layouts  18 us
  transfers between devices with their start and end apart: 33, of which 20 were waited for; matrix products, arithmetic and copies ran while one was open for 1% of the time, Pallas kernels for 0%

profile of v1, /device:TPU:32, one launch (start us, length us, event | category | flops | bytes accessed | tf_op | source)
XLA Modules:
  0.0 157.2 jit_solution(17383317516311421713)
XLA Ops:
  0.0 1.0 copy.6
  1.0 6.4 %collective-permute-start.3 = (f32[56,896]{1,0:T(8,128)S(1)}, f32[56,896]{1,0:T(8,128)S(1)}, u32[]{:S(2)}, u32[]{:S(2)}) collective-permute-start(f32[56,896]{1,0:T(8,128)S(1)} %bitcast.43), channel_id=1, source_target_pairs={{0,8},{1,9},{2,10},{3,11},{4,12},{5,13},{6,14},{7,15},{8,0},{9,1},... | collective-permute-start | bytes 602120 | tf_op jit(solution)/shard_map/gather_amp/ppermute | solution.py:30
  7.4 2.8 %collective-permute-start.2 = (f32[56,896]{1,0:T(8,128)S(1)}, f32[56,896]{1,0:T(8,128)S(1)}, u32[]{:S(2)}, u32[]{:S(2)}) collective-permute-start(f32[56,896]{1,0:T(8,128)S(1)} %bitcast.44), channel_id=1, source_target_pairs={{0,6},{1,7},{2,0},{3,1},{4,2},{5,3},{6,4},{7,5},{8,14},{9,15},{10,... | collective-permute-start | bytes 602120 | tf_op jit(solution)/shard_map/gather_amp/ppermute | solution.py:30
  10.1 0.8 collective-permute-start.1
  10.9 0.9 collective-permute-start
  11.8 1.0 collective-permute-start.20
  12.8 3.0 %collective-permute-done.3.refs_4_ = f32[56,896]{1,0:T(8,128)S(1)} collective-permute-done((f32[56,896]{1,0:T(8,128)S(1)}, f32[56,896]{1,0:T(8,128)S(1)}, u32[]{:S(2)}, u32[]{:S(2)}) %collective-permute-start.3) | collective-permute-done | bytes 200736 | tf_op jit(solution)/shard_map/gather_amp/ppermute | solution.py:30
  15.8 2.8 %collective-permute-start.6 = (f32[56,896]{1,0:T(8,128)S(1)}, f32[56,896]{1,0:T(8,128)S(1)}, u32[]{:S(2)}, u32[]{:S(2)}) collective-permute-start(f32[56,896]{1,0:T(8,128)S(1)} %collective-permute-done.3.refs_4_), channel_id=1, source_target_pairs={{0,6},{1,7},{2,0},{3,1},{4,2},{5,3},{6,4},{7,5},{8,14},{9,15},{10,... | collective-permute-start | bytes 602120 | tf_op jit(solution)/shard_map/gather_amp/ppermute | solution.py:30
  19.6 3.9 %collective-permute-start.4 = (f32[56,896]{1,0:T(8,128)S(1)}, f32[56,896]{1,0:T(8,128)S(1)}, u32[]{:S(2)}, u32[]{:S(2)}) collective-permute-start(f32[56,896]{1,0:T(8,128)S(1)} %collective-permute-done.3.refs_4_), channel_id=1, source_target_pairs={{0,2},{1,3},{2,4},{3,5},{4,6},{5,7},{6,0},{7,1},{8,10},{9,11},{10,... | collective-permute-start | bytes 602120 | tf_op jit(solution)/shard_map/gather_amp/ppermute | solution.py:30
  23.5 1.6 collective-permute-start.16
  25.3 3.0 %collective-permute-start.12 = (f32[56,896]{1,0:T(8,128)}, f32[56,896]{1,0:T(8,128)}, u32[]{:S(2)}, u32[]{:S(2)}) collective-permute-start(f32[56,896]{1,0:T(8,128)} %bitcast.51), channel_id=1, source_target_pairs={{0,64},{16,80},{32,96},{48,112},{64,0},{80,16},{96,32},{112,48},{1... | collective-permute-start | bytes 602120 | tf_op jit(solution)/shard_map/gather_fit/ppermute | solution.py:20
  28.3 1.0 pad_maximum_fusion
  29.3 3.0 %collective-permute-start.11 = (f32[56,896]{1,0:T(8,128)S(1)}, f32[56,896]{1,0:T(8,128)S(1)}, u32[]{:S(2)}, u32[]{:S(2)}) collective-permute-start(f32[56,896]{1,0:T(8,128)S(1)} %bitcast.52), channel_id=1, source_target_pairs={{0,48},{16,0},{32,16},{48,32},{64,112},{80,64},{96,80},{112,96},{1... | collective-permute-start | bytes 602120 | tf_op jit(solution)/shard_map/gather_fit/ppermute | solution.py:20
  32.9 1.0 collective-permute-start.9
  33.9 0.9 pad_maximum_fusion.1
  34.9 0.7 collective-permute-done.12.refs_14_
  35.5 2.6 %collective-permute-done.11.refs_13_ = f32[56,896]{1,0:T(8,128)S(1)} collective-permute-done((f32[56,896]{1,0:T(8,128)S(1)}, f32[56,896]{1,0:T(8,128)S(1)}, u32[]{:S(2)}, u32[]{:S(2)}) %collective-permute-start.11) | collective-permute-done | bytes 200736 | tf_op jit(solution)/shard_map/gather_fit/ppermute | solution.py:20
  38.1 0.7 copy-done.5
  38.8 3.7 %collective-permute-start.23 = (f32[56,896]{1,0:T(8,128)S(1)}, f32[56,896]{1,0:T(8,128)S(1)}, u32[]{:S(2)}, u32[]{:S(2)}) collective-permute-start(f32[56,896]{1,0:T(8,128)S(1)} %collective-permute-done.20.refs_22_), channel_id=1, source_target_pairs={{0,48},{16,0},{32,16},{48,32},{64,112},{80,64},{96,80},{112,96},{1... | collective-permute-start | bytes 602120 | tf_op jit(solution)/shard_map/gather_fit/ppermute | solution.py:20
  42.5 0.7 copy-done.7
  43.2 0.7 copy-done.9
  43.9 0.9 collective-permute-start.21
  44.7 3.2 %collective-permute-done.23.refs_25_ = f32[56,896]{1,0:T(8,128)S(1)} collective-permute-done((f32[56,896]{1,0:T(8,128)S(1)}, f32[56,896]{1,0:T(8,128)S(1)}, u32[]{:S(2)}, u32[]{:S(2)}) %collective-permute-start.23) | collective-permute-done | bytes 200736 | tf_op jit(solution)/shard_map/gather_fit/ppermute | solution.py:20
  47.9 0.7 copy-done.11
  48.6 4.2 %collective-permute-start.19 = (f32[56,896]{1,0:T(8,128)S(1)}, f32[56,896]{1,0:T(8,128)S(1)}, u32[]{:S(2)}, u32[]{:S(2)}) collective-permute-start(f32[56,896]{1,0:T(8,128)S(1)} %collective-permute-done.16.refs_18_), channel_id=1, source_target_pairs={{0,48},{16,0},{32,16},{48,32},{64,112},{80,64},{96,80},{112,96},{1... | collective-permute-start | bytes 602120 | tf_op jit(solution)/shard_map/gather_fit/ppermute | solution.py:20
  52.8 0.7 copy-done.13
  53.4 1.9 %collective-permute-done.21.refs_23_ = f32[56,896]{1,0:T(8,128)S(1)} collective-permute-done((f32[56,896]{1,0:T(8,128)S(1)}, f32[56,896]{1,0:T(8,128)S(1)}, u32[]{:S(2)}, u32[]{:S(2)}) %collective-permute-start.21) | collective-permute-done | bytes 200736 | tf_op jit(solution)/shard_map/gather_fit/ppermute | solution.py:20
  55.3 0.7 copy-done.15
  56.0 0.7 copy-done.3
  56.7 0.7 copy-done.17
  57.4 3.4 %collective-permute-start.15 = (f32[56,896]{1,0:T(8,128)}, f32[56,896]{1,0:T(8,128)}, u32[]{:S(2)}, u32[]{:S(2)}) collective-permute-start(f32[56,896]{1,0:T(8,128)} %collective-permute-done.12.refs_14_), channel_id=1, source_target_pairs={{0,48},{16,0},{32,16},{48,32},{64,112},{80,64},{96,80},{112,96},{1... | collective-permute-start | bytes 602120 | tf_op jit(solution)/shard_map/gather_fit/ppermute | solution.py:20
  60.8 0.7 copy-done.19
  61.7 4.3 %collective-permute-done.17.refs_19_ = f32[56,896]{1,0:T(8,128)S(1)} collective-permute-done((f32[56,896]{1,0:T(8,128)S(1)}, f32[56,896]{1,0:T(8,128)S(1)}, u32[]{:S(2)}, u32[]{:S(2)}) %collective-permute-start.17) | collective-permute-done | bytes 200736 | tf_op jit(solution)/shard_map/gather_fit/ppermute | solution.py:20
  66.0 0.7 copy-done.21
  66.8 2.7 %collective-permute-done.14.refs_16_ = f32[56,896]{1,0:T(8,128)} collective-permute-done((f32[56,896]{1,0:T(8,128)}, f32[56,896]{1,0:T(8,128)}, u32[]{:S(2)}, u32[]{:S(2)}) %collective-permute-start.14) | collective-permute-done | bytes 200736 | tf_op jit(solution)/shard_map/gather_fit/ppermute | solution.py:20
  69.5 4.5 %collective-permute-done.13.refs_15_ = f32[56,896]{1,0:T(8,128)} collective-permute-done((f32[56,896]{1,0:T(8,128)}, f32[56,896]{1,0:T(8,128)}, u32[]{:S(2)}, u32[]{:S(2)}) %collective-permute-start.13) | collective-permute-done | bytes 200736 | tf_op jit(solution)/shard_map/gather_fit/ppermute | solution.py:20
  74.0 0.9 copy-done.2
  74.9 0.9 copy-done.4
  75.8 0.9 copy-done.6
  76.7 0.9 copy-done.8
  77.7 0.9 copy-done.10
  78.6 0.9 copy-done.12
  79.5 0.9 copy-done.14
  80.5 0.9 copy-done.16
  81.4 0.9 copy-done.18
  82.3 0.9 copy-done.20
  83.2 0.9 copy-done.22
  84.2 32.6 %ladder.1 = (f32[8,56,896]{2,1,0:T(8,128)S(1)}, f32[8,56,896]{2,1,0:T(8,128)S(1)}) custom-call(s32[5]{0:T(128)S(1)} %stack.23.place_ref, f32[56,896]{1,0:T(8,128)S(1)} %bitcast.48, f32[56,896]{1,0:T(8,128)S(1)} %collective-permute-done.refs_1_, f32[56,896]{1,0:T(8,128)S(1)} %collective-permute-done.1.refs_2_, f32[56,896]{1,0:T(8,128)S(1)} %collective-permute-done.2.refs_3_, ...), custom_call_target="tpu_custom_call" | custom-call | flops 8631877632 | bytes 12845056 | tf_op jit(solution)/shard_map/ladder/pallas_call | solution.py:104
  117.5 1.8 %collective-permute-done.24 = f32[4,56,896]{2,1,0:T(8,128)S(1)} collective-permute-done((f32[4,56,896]{2,1,0:T(8,128)S(1)}, f32[4,56,896]{2,1,0:T(8,128)S(1)}, u32[]{:S(2)}, u32[]{:S(2)}) %collective-permute-start.24) | collective-permute-done | bytes 802848 | tf_op jit(solution)/shard_map/reduce/ppermute | solution.py:30
  119.3 1.1 collective-permute-done.28
  120.8 9.9 %collective-permute-start.29 = (f32[56,896]{1,0:T(8,128)S(1)}, f32[56,896]{1,0:T(8,128)S(1)}, u32[]{:S(2)}, u32[]{:S(2)}) collective-permute-start(f32[56,896]{1,0:T(8,128)S(1)} %get-tuple-element.16), channel_id=1, source_target_pairs={{0,2},{1,3},{2,4},{3,5},{4,6},{5,7},{6,0},{7,1},{8,10},{9,11},{10,... | collective-permute-start | bytes 602120 | tf_op jit(solution)/shard_map/reduce/ppermute | solution.py:30
  130.7 1.4 collective-permute-start.31
  132.0 1.4 collective-permute-start.30
  133.5 1.5 collective-permute-start.25
  135.0 1.8 %collective-permute-start.27 = (f32[56,896]{1,0:T(8,128)S(1)}, f32[56,896]{1,0:T(8,128)S(1)}, u32[]{:S(2)}, u32[]{:S(2)}) collective-permute-start(f32[56,896]{1,0:T(8,128)S(1)} %get-tuple-element.14), channel_id=1, source_target_pairs={{0,6},{1,7},{2,0},{3,1},{4,2},{5,3},{6,4},{7,5},{8,14},{9,15},{10,... | collective-permute-start | bytes 602120 | tf_op jit(solution)/shard_map/reduce/ppermute | solution.py:30
  136.8 0.7 collective-permute-done.29
  137.5 1.3 collective-permute-start.26
  138.8 2.2 %collective-permute-done.31 = f32[56,896]{1,0:T(8,128)S(1)} collective-permute-done((f32[56,896]{1,0:T(8,128)S(1)}, f32[56,896]{1,0:T(8,128)S(1)}, u32[]{:S(2)}, u32[]{:S(2)}) %collective-permute-start.31) | collective-permute-done | bytes 200736 | tf_op jit(solution)/shard_map/reduce/ppermute | solution.py:30
  141.0 2.6 %collective-permute-done.30 = f32[56,896]{1,0:T(8,128)S(1)} collective-permute-done((f32[56,896]{1,0:T(8,128)S(1)}, f32[56,896]{1,0:T(8,128)S(1)}, u32[]{:S(2)}, u32[]{:S(2)}) %collective-permute-start.30) | collective-permute-done | bytes 200736 | tf_op jit(solution)/shard_map/reduce/ppermute | solution.py:30
  143.7 2.1 %collective-permute-done.25 = f32[56,896]{1,0:T(8,128)S(1)} collective-permute-done((f32[56,896]{1,0:T(8,128)S(1)}, f32[56,896]{1,0:T(8,128)S(1)}, u32[]{:S(2)}, u32[]{:S(2)}) %collective-permute-start.25) | collective-permute-done | bytes 200736 | tf_op jit(solution)/shard_map/reduce/ppermute | solution.py:30
  145.9 1.4 collective-permute-done.27
  147.2 4.2 %collective-permute-done.26 = f32[56,896]{1,0:T(8,128)S(1)} collective-permute-done((f32[56,896]{1,0:T(8,128)S(1)}, f32[56,896]{1,0:T(8,128)S(1)}, u32[]{:S(2)}, u32[]{:S(2)}) %collective-permute-start.26) | collective-permute-done | bytes 200736 | tf_op jit(solution)/shard_map/reduce/ppermute | solution.py:30
  151.4 4.8 %collective-permute-done.32 = f32[56,896]{1,0:T(8,128)S(1)} collective-permute-done((f32[56,896]{1,0:T(8,128)S(1)}, f32[56,896]{1,0:T(8,128)S(1)}, u32[]{:S(2)}, u32[]{:S(2)}) %collective-permute-start.32) | collective-permute-done | bytes 200736 | tf_op jit(solution)/shard_map/reduce/ppermute | solution.py:30
  156.3 0.9 copy.3
  (60 shorter events, 3.6 us)
Async XLA Ops:
  0.0 29.3 %copy-start = (f32[1,56,896]{2,1,0:T(8,128)S(1)}, f32[1,56,896]{2,1,0:T(8,128)}, u32[]{:S(2)}) copy-start(f32[1,56,896]{2,1,0:T(8,128)} %param.3) | copy-start | bytes 602116
  1.0 14.8 %collective-permute-start.3 = (f32[56,896]{1,0:T(8,128)S(1)}, f32[56,896]{1,0:T(8,128)S(1)}, u32[]{:S(2)}, u32[]{:S(2)}) collective-permute-start(f32[56,896]{1,0:T(8,128)S(1)} %bitcast.43), channel_id=1, source_target_pairs={{0,8},{1,9},{2,10},{3,11},{4,12},{5,13},{6,14},{7,15},{8,0},{9,1},... | collective-permute-start | bytes 602120 | tf_op jit(solution)/shard_map/gather_amp/ppermute | solution.py:30
  7.4 11.4 %collective-permute-start.2 = (f32[56,896]{1,0:T(8,128)S(1)}, f32[56,896]{1,0:T(8,128)S(1)}, u32[]{:S(2)}, u32[]{:S(2)}) collective-permute-start(f32[56,896]{1,0:T(8,128)S(1)} %bitcast.44), channel_id=1, source_target_pairs={{0,6},{1,7},{2,0},{3,1},{4,2},{5,3},{6,4},{7,5},{8,14},{9,15},{10,... | collective-permute-start | bytes 602120 | tf_op jit(solution)/shard_map/gather_amp/ppermute | solution.py:30
  10.1 9.5 %collective-permute-start.1 = (f32[56,896]{1,0:T(8,128)S(1)}, f32[56,896]{1,0:T(8,128)S(1)}, u32[]{:S(2)}, u32[]{:S(2)}) collective-permute-start(f32[56,896]{1,0:T(8,128)S(1)} %bitcast.45), channel_id=1, source_target_pairs={{0,4},{1,5},{2,6},{3,7},{4,0},{5,1},{6,2},{7,3},{8,12},{9,13},{10,... | collective-permute-start | bytes 602120 | tf_op jit(solution)/shard_map/gather_amp/ppermute | solution.py:30
  10.9 12.6 %collective-permute-start = (f32[56,896]{1,0:T(8,128)S(1)}, f32[56,896]{1,0:T(8,128)S(1)}, u32[]{:S(2)}, u32[]{:S(2)}) collective-permute-start(f32[56,896]{1,0:T(8,128)S(1)} %bitcast.46), channel_id=1, source_target_pairs={{0,2},{1,3},{2,4},{3,5},{4,6},{5,7},{6,0},{7,1},{8,10},{9,11},{10,... | collective-permute-start | bytes 602120 | tf_op jit(solution)/shard_map/gather_amp/ppermute | solution.py:30
  11.8 13.5 %collective-permute-start.20 = (f32[56,896]{1,0:T(8,128)}, f32[56,896]{1,0:T(8,128)S(1)}, u32[]{:S(2)}, u32[]{:S(2)}) collective-permute-start(f32[56,896]{1,0:T(8,128)} %bitcast.49), channel_id=1, source_target_pairs={{0,192},{16,208},{32,224},{48,240},{64,128},{80,144},{96,160},{112... | collective-permute-start | bytes 602120 | tf_op jit(solution)/shard_map/gather_fit/ppermute | solution.py:20
  15.8 13.5 %collective-permute-start.6 = (f32[56,896]{1,0:T(8,128)S(1)}, f32[56,896]{1,0:T(8,128)S(1)}, u32[]{:S(2)}, u32[]{:S(2)}) collective-permute-start(f32[56,896]{1,0:T(8,128)S(1)} %collective-permute-done.3.refs_4_), channel_id=1, source_target_pairs={{0,6},{1,7},{2,0},{3,1},{4,2},{5,3},{6,4},{7,5},{8,14},{9,15},{10,... | collective-permute-start | bytes 602120 | tf_op jit(solution)/shard_map/gather_amp/ppermute | solution.py:30
  18.8 13.5 %collective-permute-start.5 = (f32[56,896]{1,0:T(8,128)S(1)}, f32[56,896]{1,0:T(8,128)S(1)}, u32[]{:S(2)}, u32[]{:S(2)}) collective-permute-start(f32[56,896]{1,0:T(8,128)S(1)} %collective-permute-done.3.refs_4_), channel_id=1, source_target_pairs={{0,4},{1,5},{2,6},{3,7},{4,0},{5,1},{6,2},{7,3},{8,12},{9,13},{10,... | collective-permute-start | bytes 602120 | tf_op jit(solution)/shard_map/gather_amp/ppermute | solution.py:30
  19.6 13.3 %collective-permute-start.4 = (f32[56,896]{1,0:T(8,128)S(1)}, f32[56,896]{1,0:T(8,128)S(1)}, u32[]{:S(2)}, u32[]{:S(2)}) collective-permute-start(f32[56,896]{1,0:T(8,128)S(1)} %collective-permute-done.3.refs_4_), channel_id=1, source_target_pairs={{0,2},{1,3},{2,4},{3,5},{4,6},{5,7},{6,0},{7,1},{8,10},{9,11},{10,... | collective-permute-start | bytes 602120 | tf_op jit(solution)/shard_map/gather_amp/ppermute | solution.py:30
  23.5 11.4 %collective-permute-start.16 = (f32[56,896]{1,0:T(8,128)}, f32[56,896]{1,0:T(8,128)S(1)}, u32[]{:S(2)}, u32[]{:S(2)}) collective-permute-start(f32[56,896]{1,0:T(8,128)} %bitcast.50), channel_id=1, source_target_pairs={{0,128},{16,144},{32,160},{48,176},{64,192},{80,208},{96,224},{112... | collective-permute-start | bytes 602120 | tf_op jit(solution)/shard_map/gather_fit/ppermute | solution.py:20
  25.3 17.9 %copy-start.1 = (f32[56,896]{1,0:T(8,128)}, f32[56,896]{1,0:T(8,128)S(1)}, u32[]{:S(2)}) copy-start(f32[56,896]{1,0:T(8,128)S(1)} %collective-permute-done.20.refs_22_) | copy-start | bytes 602116
  25.3 10.2 %collective-permute-start.12 = (f32[56,896]{1,0:T(8,128)}, f32[56,896]{1,0:T(8,128)}, u32[]{:S(2)}, u32[]{:S(2)}) collective-permute-start(f32[56,896]{1,0:T(8,128)} %bitcast.51), channel_id=1, source_target_pairs={{0,64},{16,80},{32,96},{48,112},{64,0},{80,16},{96,32},{112,48},{1... | collective-permute-start | bytes 602120 | tf_op jit(solution)/shard_map/gather_fit/ppermute | solution.py:20
  29.3 8.8 %collective-permute-start.11 = (f32[56,896]{1,0:T(8,128)S(1)}, f32[56,896]{1,0:T(8,128)S(1)}, u32[]{:S(2)}, u32[]{:S(2)}) collective-permute-start(f32[56,896]{1,0:T(8,128)S(1)} %bitcast.52), channel_id=1, source_target_pairs={{0,48},{16,0},{32,16},{48,32},{64,112},{80,64},{96,80},{112,96},{1... | collective-permute-start | bytes 602120 | tf_op jit(solution)/shard_map/gather_fit/ppermute | solution.py:20
  32.3 10.2 %collective-permute-start.10 = (f32[56,896]{1,0:T(8,128)S(1)}, f32[56,896]{1,0:T(8,128)S(1)}, u32[]{:S(2)}, u32[]{:S(2)}) collective-permute-start(f32[56,896]{1,0:T(8,128)S(1)} %bitcast.53), channel_id=1, source_target_pairs={{0,32},{16,48},{32,0},{48,16},{64,96},{80,112},{96,64},{112,80},{1... | collective-permute-start | bytes 602120 | tf_op jit(solution)/shard_map/gather_fit/ppermute | solution.py:20
  32.9 10.2 %collective-permute-start.9 = (f32[56,896]{1,0:T(8,128)S(1)}, f32[56,896]{1,0:T(8,128)S(1)}, u32[]{:S(2)}, u32[]{:S(2)}) collective-permute-start(f32[56,896]{1,0:T(8,128)S(1)} %bitcast.54), channel_id=1, source_target_pairs={{0,16},{16,32},{32,48},{48,0},{64,80},{80,96},{96,112},{112,64},{1... | collective-permute-start | bytes 602120 | tf_op jit(solution)/shard_map/gather_fit/ppermute | solution.py:20
  34.9 39.1 %collective-permute-start.7 = (f32[224,896]{1,0:T(8,128)}, f32[224,896]{1,0:T(8,128)S(1)}, u32[]{:S(2)}, u32[]{:S(2)}) collective-permute-start(f32[224,896]{1,0:T(8,128)} %pad_maximum_fusion), channel_id=1, source_target_pairs={{0,1},{1,0},{2,3},{3,2},{4,5},{5,4},{6,7},{7,6},{8,9},{9,8},{10,11... | collective-permute-start | bytes 2408456 | tf_op jit(solution)/shard_map/gather_amp/ppermute | solution.py:30
  35.5 38.4 %collective-permute-start.8 = (f32[224,896]{1,0:T(8,128)}, f32[224,896]{1,0:T(8,128)S(1)}, u32[]{:S(2)}, u32[]{:S(2)}) collective-permute-start(f32[224,896]{1,0:T(8,128)} %pad_maximum_fusion.1), channel_id=1, source_target_pairs={{0,1},{1,0},{2,3},{3,2},{4,5},{5,4},{6,7},{7,6},{8,9},{9,8},{10,11... | collective-permute-start | bytes 2408456 | tf_op jit(solution)/shard_map/gather_amp/ppermute | solution.py:30
  38.1 0.7 copy-start.5
  38.8 9.1 %collective-permute-start.23 = (f32[56,896]{1,0:T(8,128)S(1)}, f32[56,896]{1,0:T(8,128)S(1)}, u32[]{:S(2)}, u32[]{:S(2)}) collective-permute-start(f32[56,896]{1,0:T(8,128)S(1)} %collective-permute-done.20.refs_22_), channel_id=1, source_target_pairs={{0,48},{16,0},{32,16},{48,32},{64,112},{80,64},{96,80},{112,96},{1... | collective-permute-start | bytes 602120 | tf_op jit(solution)/shard_map/gather_fit/ppermute | solution.py:20
  42.5 0.7 copy-start.7
  43.2 9.6 %collective-permute-start.22 = (f32[56,896]{1,0:T(8,128)S(1)}, f32[56,896]{1,0:T(8,128)S(1)}, u32[]{:S(2)}, u32[]{:S(2)}) collective-permute-start(f32[56,896]{1,0:T(8,128)S(1)} %collective-permute-done.20.refs_22_), channel_id=1, source_target_pairs={{0,32},{16,48},{32,0},{48,16},{64,96},{80,112},{96,64},{112,80},{1... | collective-permute-start | bytes 602120 | tf_op jit(solution)/shard_map/gather_fit/ppermute | solution.py:20
  43.2 0.7 copy-start.9
  43.9 11.5 %collective-permute-start.21 = (f32[56,896]{1,0:T(8,128)S(1)}, f32[56,896]{1,0:T(8,128)S(1)}, u32[]{:S(2)}, u32[]{:S(2)}) collective-permute-start(f32[56,896]{1,0:T(8,128)S(1)} %collective-permute-done.20.refs_22_), channel_id=1, source_target_pairs={{0,16},{16,32},{32,48},{48,0},{64,80},{80,96},{96,112},{112,64},{1... | collective-permute-start | bytes 602120 | tf_op jit(solution)/shard_map/gather_fit/ppermute | solution.py:20
  47.9 0.7 copy-start.11
  48.6 8.1 %collective-permute-start.19 = (f32[56,896]{1,0:T(8,128)S(1)}, f32[56,896]{1,0:T(8,128)S(1)}, u32[]{:S(2)}, u32[]{:S(2)}) collective-permute-start(f32[56,896]{1,0:T(8,128)S(1)} %collective-permute-done.16.refs_18_), channel_id=1, source_target_pairs={{0,48},{16,0},{32,16},{48,32},{64,112},{80,64},{96,80},{112,96},{1... | collective-permute-start | bytes 602120 | tf_op jit(solution)/shard_map/gather_fit/ppermute | solution.py:20
  52.8 0.7 copy-start.13
  53.4 7.3 %collective-permute-start.18 = (f32[56,896]{1,0:T(8,128)S(1)}, f32[56,896]{1,0:T(8,128)S(1)}, u32[]{:S(2)}, u32[]{:S(2)}) collective-permute-start(f32[56,896]{1,0:T(8,128)S(1)} %collective-permute-done.16.refs_18_), channel_id=1, source_target_pairs={{0,32},{16,48},{32,0},{48,16},{64,96},{80,112},{96,64},{112,80},{1... | collective-permute-start | bytes 602120 | tf_op jit(solution)/shard_map/gather_fit/ppermute | solution.py:20
  55.3 0.7 copy-start.15
  56.0 10.0 %collective-permute-start.17 = (f32[56,896]{1,0:T(8,128)S(1)}, f32[56,896]{1,0:T(8,128)S(1)}, u32[]{:S(2)}, u32[]{:S(2)}) collective-permute-start(f32[56,896]{1,0:T(8,128)S(1)} %collective-permute-done.16.refs_18_), channel_id=1, source_target_pairs={{0,16},{16,32},{32,48},{48,0},{64,80},{80,96},{96,112},{112,64},{1... | collective-permute-start | bytes 602120 | tf_op jit(solution)/shard_map/gather_fit/ppermute | solution.py:20
  56.0 0.7 copy-start.3
  56.7 0.7 copy-start.17
  57.4 9.4 %collective-permute-start.15 = (f32[56,896]{1,0:T(8,128)}, f32[56,896]{1,0:T(8,128)}, u32[]{:S(2)}, u32[]{:S(2)}) collective-permute-start(f32[56,896]{1,0:T(8,128)} %collective-permute-done.12.refs_14_), channel_id=1, source_target_pairs={{0,48},{16,0},{32,16},{48,32},{64,112},{80,64},{96,80},{112,96},{1... | collective-permute-start | bytes 602120 | tf_op jit(solution)/shard_map/gather_fit/ppermute | solution.py:20
  60.8 0.7 copy-start.19
  61.5 8.0 %collective-permute-start.14 = (f32[56,896]{1,0:T(8,128)}, f32[56,896]{1,0:T(8,128)}, u32[]{:S(2)}, u32[]{:S(2)}) collective-permute-start(f32[56,896]{1,0:T(8,128)} %collective-permute-done.12.refs_14_), channel_id=1, source_target_pairs={{0,32},{16,48},{32,0},{48,16},{64,96},{80,112},{96,64},{112,80},{1... | collective-permute-start | bytes 602120 | tf_op jit(solution)/shard_map/gather_fit/ppermute | solution.py:20
  66.0 0.7 copy-start.21
  66.7 7.2 %collective-permute-start.13 = (f32[56,896]{1,0:T(8,128)}, f32[56,896]{1,0:T(8,128)}, u32[]{:S(2)}, u32[]{:S(2)}) collective-permute-start(f32[56,896]{1,0:T(8,128)} %collective-permute-done.12.refs_14_), channel_id=1, source_target_pairs={{0,16},{16,32},{32,48},{48,0},{64,80},{80,96},{96,112},{112,64},{1... | collective-permute-start | bytes 602120 | tf_op jit(solution)/shard_map/gather_fit/ppermute | solution.py:20
  73.9 0.9 copy-start.2
  74.9 0.9 copy-start.4
  75.8 0.9 copy-start.6
  76.7 0.9 copy-start.8
  77.7 0.9 copy-start.10
  78.6 0.9 copy-start.12
  79.5 0.9 copy-start.14
  80.5 0.9 copy-start.16
  81.4 0.9 copy-start.18
  82.3 0.9 copy-start.20
  83.2 0.9 copy-start.22
  116.9 2.4 %collective-permute-start.24 = (f32[4,56,896]{2,1,0:T(8,128)S(1)}, f32[4,56,896]{2,1,0:T(8,128)S(1)}, u32[]{:S(2)}, u32[]{:S(2)}) collective-permute-start(f32[4,56,896]{2,1,0:T(8,128)S(1)} %get-tuple-element.11), channel_id=1, source_target_pairs={{0,1},{1,0},{2,3},{3,2},{4,5},{5,4},{6,7},{7,6},{8,9},{9,8},{10,11... | collective-permute-start | bytes 2408456 | tf_op jit(solution)/shard_map/reduce/ppermute | solution.py:30
  117.0 3.4 %collective-permute-start.28 = (f32[4,56,896]{2,1,0:T(8,128)S(1)}, f32[4,56,896]{2,1,0:T(8,128)S(1)}, u32[]{:S(2)}, u32[]{:S(2)}) collective-permute-start(f32[4,56,896]{2,1,0:T(8,128)S(1)} %get-tuple-element.12), channel_id=1, source_target_pairs={{0,1},{1,0},{2,3},{3,2},{4,5},{5,4},{6,7},{7,6},{8,9},{9,8},{10,11... | collective-permute-start | bytes 2408456 | tf_op jit(solution)/shard_map/reduce/ppermute | solution.py:30
  120.8 16.7 %collective-permute-start.29 = (f32[56,896]{1,0:T(8,128)S(1)}, f32[56,896]{1,0:T(8,128)S(1)}, u32[]{:S(2)}, u32[]{:S(2)}) collective-permute-start(f32[56,896]{1,0:T(8,128)S(1)} %get-tuple-element.16), channel_id=1, source_target_pairs={{0,2},{1,3},{2,4},{3,5},{4,6},{5,7},{6,0},{7,1},{8,10},{9,11},{10,... | collective-permute-start | bytes 602120 | tf_op jit(solution)/shard_map/reduce/ppermute | solution.py:30
  130.7 10.3 %collective-permute-start.31 = (f32[56,896]{1,0:T(8,128)S(1)}, f32[56,896]{1,0:T(8,128)S(1)}, u32[]{:S(2)}, u32[]{:S(2)}) collective-permute-start(f32[56,896]{1,0:T(8,128)S(1)} %get-tuple-element.17), channel_id=1, source_target_pairs={{0,6},{1,7},{2,0},{3,1},{4,2},{5,3},{6,4},{7,5},{8,14},{9,15},{10,... | collective-permute-start | bytes 602120 | tf_op jit(solution)/shard_map/reduce/ppermute | solution.py:30
  132.0 11.5 %collective-permute-start.30 = (f32[56,896]{1,0:T(8,128)S(1)}, f32[56,896]{1,0:T(8,128)S(1)}, u32[]{:S(2)}, u32[]{:S(2)}) collective-permute-start(f32[56,896]{1,0:T(8,128)S(1)} %get-tuple-element.18), channel_id=1, source_target_pairs={{0,4},{1,5},{2,6},{3,7},{4,0},{5,1},{6,2},{7,3},{8,12},{9,13},{10,... | collective-permute-start | bytes 602120 | tf_op jit(solution)/shard_map/reduce/ppermute | solution.py:30
  133.5 12.4 %collective-permute-start.25 = (f32[56,896]{1,0:T(8,128)S(1)}, f32[56,896]{1,0:T(8,128)S(1)}, u32[]{:S(2)}, u32[]{:S(2)}) collective-permute-start(f32[56,896]{1,0:T(8,128)S(1)} %get-tuple-element.13), channel_id=1, source_target_pairs={{0,2},{1,3},{2,4},{3,5},{4,6},{5,7},{6,0},{7,1},{8,10},{9,11},{10,... | collective-permute-start | bytes 602120 | tf_op jit(solution)/shard_map/reduce/ppermute | solution.py:30
  135.0 12.2 %collective-permute-start.27 = (f32[56,896]{1,0:T(8,128)S(1)}, f32[56,896]{1,0:T(8,128)S(1)}, u32[]{:S(2)}, u32[]{:S(2)}) collective-permute-start(f32[56,896]{1,0:T(8,128)S(1)} %get-tuple-element.14), channel_id=1, source_target_pairs={{0,6},{1,7},{2,0},{3,1},{4,2},{5,3},{6,4},{7,5},{8,14},{9,15},{10,... | collective-permute-start | bytes 602120 | tf_op jit(solution)/shard_map/reduce/ppermute | solution.py:30
  137.5 13.9 %collective-permute-start.26 = (f32[56,896]{1,0:T(8,128)S(1)}, f32[56,896]{1,0:T(8,128)S(1)}, u32[]{:S(2)}, u32[]{:S(2)}) collective-permute-start(f32[56,896]{1,0:T(8,128)S(1)} %get-tuple-element.15), channel_id=1, source_target_pairs={{0,4},{1,5},{2,6},{3,7},{4,0},{5,1},{6,2},{7,3},{8,12},{9,13},{10,... | collective-permute-start | bytes 602120 | tf_op jit(solution)/shard_map/reduce/ppermute | solution.py:30
  143.6 12.6 %collective-permute-start.32 = (f32[56,896]{1,0:T(8,128)S(1)}, f32[56,896]{1,0:T(8,128)S(1)}, u32[]{:S(2)}, u32[]{:S(2)}) collective-permute-start(f32[56,896]{1,0:T(8,128)S(1)} %fusion.2), channel_id=1, source_target_pairs={{0,8},{1,9},{2,10},{3,11},{4,12},{5,13},{6,14},{7,15},{8,0},{9,1},... | collective-permute-start | bytes 602120 | tf_op jit(solution)/shard_map/reduce/ppermute | solution.py:30

commit v2 on v0

v2 whole, which is shorter than its diff:
```python
import jax
import jax.numpy as jnp
from jax import lax
from jax.experimental import pallas as pl
from jax.experimental.pallas import tpu as pltpu
from jax.sharding import PartitionSpec as P

NZL, NY, NZH, NX, NC = 4, 4, 2, 4, 2
V = 896
HALF = 448
ROWS = 56
NN = (((1,), (0,)), ((), ()))
NT = (((1,), (1,)), ((), ()))
ANY = pl.BlockSpec(memory_space=pl.ANY)
SMEM = pl.BlockSpec(memory_space=pltpu.SMEM)


def pair_permute(value, target):
    steps = []
    for zl in range(NZL):
        for y in range(NY):
            tz, ty = target(zl, y)
            steps.append((zl * NY + y, (tz % NZL) * NY + ty % NY))
    return lax.ppermute(value, "pair", steps)


def aux_permute(value, target):
    steps = []
    for zh in range(NZH):
        for x in range(NX):
            for c in range(NC):
                th, tx, tc = target(zh, x, c)
                steps.append(((zh * NX + x) * NC + c, ((th % NZH) * NX + tx % NX) * NC + tc % NC))
    return lax.ppermute(value, "aux", steps)


def swap_core(value):
    return aux_permute(value, lambda zh, x, c: (zh, x, 1 - c))


def split(value):
    high = value.astype(jnp.bfloat16)
    low = (value - high.astype(jnp.float32)).astype(jnp.bfloat16)
    return high, low


def product(left, right, dims):
    def dot(a, b):
        return lax.dot_general(a, b, dims, preferred_element_type=jnp.float32)

    return dot(left[1], right[0]) + dot(left[0], right[1]) + dot(left[0], right[0])


def run_copies(copies):
    for copy in copies:
        copy.start()
    for copy in copies:
        copy.wait()


def fit_copies(refs, target, zl, y, sem, first):
    both, below, above, low2, high2 = refs
    places = [(both, 0, 0, 0), (both, 1, 1, 0), (below, 0, 0, 3), (below, 1, 1, 3)]
    places += [(above, 0, 0, 1), (above, 1, 1, 1), (low2, 0, 0, 2), (high2, 0, 1, 2)]
    copies = []
    for index, (ref, part, k, j) in enumerate(places):
        row = pl.multiple_of(((zl + k) % 2) * 224 + ((y + j) % NY) * ROWS, 8)
        copies.append(
            pltpu.make_async_copy(ref.at[pl.ds(part * ROWS, ROWS)], target.at[pl.ds(row, ROWS)], sem.at[first + index])
        )
    return copies


def amp_copies(refs, target, zh, x, core, sem):
    mine, other, beside, across, relay, relay_other = refs
    step = 2 * core - 1
    places = []
    for far in (0, 1):
        places += [(mine, far, far, 0, core), (other, far, far, 0, 1 - core)]
        places += [(beside, far, far, step, core), (beside, 2 + far, far, step, 1 - core)]
        places += [(across, far, far, -step, 1 - core), (across, 2 + far, far, -step, core)]
        places += [(relay, far, far, 2, core), (relay_other, far, far, 2, 1 - core)]
    copies = []
    for index, (ref, part, far, dx, c) in enumerate(places):
        row = pl.multiple_of((((zh + far) % NZH) * 8 + ((x + dx + NX) % NX) * 2 + c) * ROWS, 8)
        copies.append(
            pltpu.make_async_copy(ref.at[pl.ds(part * ROWS, ROWS)], target.at[pl.ds(row, ROWS)], sem.at[index])
        )
    return copies


def first_kernel(place_ref, *refs):
    t_refs, b_refs = refs[:6], refs[6:11]
    t_hi, t_lo, b_hi, b_lo, g_hi, g_lo = refs[11:17]
    t32, b32, sem = refs[17:]
    zl, y, zh, x, core = (place_ref[i] for i in range(5))
    run_copies(amp_copies(t_refs, t32, zh, x, core, sem) + fit_copies(b_refs, b32, zl, y, sem, 16))
    for row in range(0, V, 128):
        rows = slice(row, row + 128)
        t_hi[rows], t_lo[rows] = split(t32[rows])
    for row in range(0, HALF, 64):
        rows = slice(row, row + 64)
        b_hi[rows], b_lo[rows] = split(b32[rows])
    g_hi[...], g_lo[...] = split(product((b_hi[...], b_lo[...]), (t_hi[...], t_lo[...]), NN))


def out_copies(total, keep_ref, send_ref, half, x, core, sem):
    copies = []
    for k in range(NX):
        block = ((x + k) % NX) * 2
        mine = pl.multiple_of((block + core) * ROWS, 8)
        other = pl.multiple_of((block + 1 - core) * ROWS, 8)
        copies.append(pltpu.make_async_copy(total.at[pl.ds(mine, ROWS)], keep_ref.at[k], sem.at[k]))
        copies.append(pltpu.make_async_copy(total.at[pl.ds(other, ROWS)], send_ref.at[k], sem.at[NX + k]))
    return copies


def second_kernel(place_ref, *refs):
    t_hi, t_lo, ba_hi, ba_lo, ga_hi, ga_lo = refs[:6]
    b_refs = refs[6:11]
    b_hi, b_lo, g_hi, g_lo, keep_ref, send_ref = refs[11:17]
    b32, total, sem = refs[17:]
    zl, y, zh, x, core = (place_ref[i] for i in range(5))
    run_copies(fit_copies(b_refs, b32, zl, y, sem, 0))
    upper = zl // 2
    rows_a = pl.ds(pl.multiple_of(upper * HALF, HALF), HALF)
    rows_b = pl.ds(pl.multiple_of((1 - upper) * HALF, HALF), HALF)
    high, low = split(b32[...])
    b_hi[rows_b], b_lo[rows_b] = high, low
    g_hi[rows_b], g_lo[rows_b] = split(product((high, low), (t_hi[...], t_lo[...]), NN))
    b_hi[rows_a], b_lo[rows_a] = ba_hi[...], ba_lo[...]
    g_hi[rows_a], g_lo[rows_a] = ga_hi[...], ga_lo[...]
    rows = pl.ds(pl.multiple_of((1 - zh) * HALF, HALF), HALF)
    total[...] = product((g_hi[rows], g_lo[rows]), (b_hi[...], b_lo[...]), NT)
    run_copies(out_copies(total, keep_ref, send_ref, 1 - zh, x, core, sem))


def third_kernel(place_ref, b_hi, b_lo, g_hi, g_lo, keep_ref, send_ref, total, sem):
    zh, x, core = (place_ref[i] for i in range(2, 5))
    rows = pl.ds(pl.multiple_of(zh * HALF, HALF), HALF)
    total[...] = product((g_hi[rows], g_lo[rows]), (b_hi[...], b_lo[...]), NT)
    run_copies(out_copies(total, keep_ref, send_ref, zh, x, core, sem))


def call(kernel, outs, out_specs, scratch, args, in_specs, flops, moved, name):
    return pl.pallas_call(
        kernel,
        out_shape=outs,
        in_specs=in_specs,
        out_specs=out_specs,
        scratch_shapes=scratch,
        compiler_params=pltpu.CompilerParams(vmem_limit_bytes=36 * 1024 * 1024),
        cost_estimate=pl.CostEstimate(flops=flops, bytes_accessed=moved, transcendentals=0),
        name=name,
    )(*args)


def per_device(amplitudes, fitting):
    pair, aux = lax.axis_index("pair"), lax.axis_index("aux")
    place = jnp.stack([pair // NY, pair % NY, aux // 8, aux // 2 % NX, aux % 2]).astype(jnp.int32)
    amp = amplitudes.reshape(ROWS, V)
    fit = fitting.reshape(ROWS, V)

    def spread(both):
        below = pair_permute(both, lambda zl, y: (zl, y + 1))
        above = pair_permute(both, lambda zl, y: (zl, y - 1))
        low2 = pair_permute(below[:ROWS], lambda zl, y: (zl, y + 1))
        high2 = pair_permute(above[ROWS:], lambda zl, y: (zl, y - 1))
        return [both, below, above, low2, high2]

    with jax.named_scope("gather_fit"):
        near = pair_permute(fit, lambda zl, y: (zl ^ 1, y))
        far = [pair_permute(fit, lambda zl, y, k=k: (zl ^ k, y)) for k in (2, 3)]
        fit_a = spread(jnp.concatenate([fit, near]))
        fit_b = spread(jnp.concatenate(far))

    with jax.named_scope("gather_amp"):
        mine = jnp.concatenate([amp, aux_permute(amp, lambda zh, x, c: (1 - zh, x, c))])
        other = swap_core(mine)
        chip = jnp.concatenate([mine, other])
        beside = aux_permute(chip, lambda zh, x, c: (zh, x + 1 - 2 * c, c))
        across = swap_core(beside)
        relay = aux_permute(beside[: 2 * ROWS], lambda zh, x, c: (zh, x + 1 - 2 * c, c))
        amps = [mine, other, beside, across, relay, swap_core(relay)]

    VMEM = pl.BlockSpec(memory_space=pltpu.VMEM)
    whole = jax.ShapeDtypeStruct((V, V), jnp.bfloat16)
    half = jax.ShapeDtypeStruct((HALF, V), jnp.bfloat16)
    blocks = jax.ShapeDtypeStruct((NX, ROWS, V), jnp.float32)
    cube = V**3
    first = call(
        first_kernel,
        (whole, whole, half, half, half, half),
        (VMEM,) * 6,
        [pltpu.VMEM((V, V), jnp.float32), pltpu.VMEM((HALF, V), jnp.float32), pltpu.SemaphoreType.DMA((24,))],
        (place, *amps, *fit_a),
        [SMEM] + [ANY] * 11,
        3 * cube,
        12 * V * V,
        "first_half",
    )
    second = call(
        second_kernel,
        (whole, whole, whole, whole, blocks, blocks),
        (VMEM,) * 4 + (ANY,) * 2,
        [pltpu.VMEM((HALF, V), jnp.float32), pltpu.VMEM((HALF, V), jnp.float32), pltpu.SemaphoreType.DMA((8,))],
        (place, *first, *fit_b),
        [SMEM] + [VMEM] * 6 + [ANY] * 5,
        6 * cube,
        20 * V * V,
        "second_half",
    )
    b_hi, b_lo, g_hi, g_lo, *far_rows = second
    near_rows = call(
        third_kernel,
        (blocks, blocks),
        (ANY,) * 2,
        [pltpu.VMEM((HALF, V), jnp.float32), pltpu.SemaphoreType.DMA((8,))],
        (place, b_hi, b_lo, g_hi, g_lo),
        [SMEM] + [VMEM] * 4,
        3 * cube,
        12 * V * V,
        "near_rows",
    )

    def reduce_x(keep, send):
        both = keep + swap_core(send)
        total = both[0]
        for k in (1, 2, 3):
            total = total + aux_permute(both[k], lambda zh, x, c, k=k: (zh, x + k, c))
        return total

    with jax.named_scope("reduce"):
        far_sum = aux_permute(reduce_x(*far_rows), lambda zh, x, c: (1 - zh, x, c))
        result = reduce_x(*near_rows) + far_sum
    return result.reshape(ROWS, 1, V)


def solution(mesh):
    in_specs = (P("aux", "pair", None), P("aux", "pair", None))
    out_specs = P("aux", "pair", None)
    return jax.shard_map(
        per_device, mesh=mesh, in_specs=in_specs, out_specs=out_specs, check_vma=False
    )
```

time: 392 us -> 117 us (0.30)
  waiting for transfers between devices: 346 us -> 47.1 us
  starting transfers between devices: 0.08 us -> 38.2 us
  matrix products: 28.1 us -> 0 us
  Pallas kernels: 0 us -> 25.3 us
  between operations: 13.8 us -> 0.15 us
    unnamed x4 -> x0, waiting for transfers between devices: 185 us -> none
    all_gather x2 -> x0, waiting for transfers between devices: 161 us -> none  [the longest x1 83.3 us: per_device(): whole_fit = lax.all_gather(fitting, 'pair', axis=1, tiled=True)]
    ppermute x0 -> x26, waiting for transfers between devices: none -> 47.1 us  [the longest x15 23.8 us: aux_permute(): return lax.ppermute(value, 'aux', steps)]
    ppermute x0 -> x26, starting transfers between devices: none -> 38.2 us  [the longest x15 22.2 us: aux_permute(): return lax.ppermute(value, 'aux', steps)]
    dot_general x2 -> x0, matrix products: 28.1 us -> none  [the longest x1 14.7 us: per_device(): jnp.einsum('rpd,lbd->lrpb', whole_amp, whole_fit, precision=lax.Precision...]
    pallas_call x0 -> x3, Pallas kernels: none -> 25.3 us  [call(): pl.pallas_call(kernel, out_shape=outs, in_specs=in_specs, out_specs=out_s...]
  transfers between devices with their start and end apart: 3 -> 26, of which waited for: 3 -> 14; matrix products, arithmetic and copies ran while one was open for 0% -> 4% of each run, Pallas kernels for 0% -> 12%
where the time goes in v2:
time: 117 us
  waiting for transfers between devices  47.1 us (40%)
  starting transfers between devices  38.2 us (33%)
  Pallas kernels  25.3 us (22%)
  local copies, waits for them, and re-layouts  5.78 us (5%)
    pallas_call x3, Pallas kernels, call(): pl.pallas_call(kernel, out_shape=outs, in_specs=in_specs, out_specs=out_s...  25.3 us
    ppermute x15, waiting for transfers between devices, aux_permute(): return lax.ppermute(value, 'aux', steps)  23.8 us
    ppermute x11, waiting for transfers between devices, pair_permute(): return lax.ppermute(value, 'pair', steps)  23.3 us
    ppermute x15, starting transfers between devices, aux_permute(): return lax.ppermute(value, 'aux', steps)  22.2 us
    ppermute x11, starting transfers between devices, pair_permute(): return lax.ppermute(value, 'pair', steps)  16 us
  transfers between devices with their start and end apart: 26, of which 14 were waited for; matrix products, arithmetic and copies ran while one was open for 4% of the time, Pallas kernels for 12%

profile of v2, /device:TPU:32, one launch (start us, length us, event | category | flops | bytes accessed | tf_op | source)
XLA Modules:
  0.0 117.0 jit_solution(945215469568502591)
XLA Ops:
  0.0 1.0 copy.6
  1.0 6.4 %collective-permute-start = (f32[56,896]{1,0:T(8,128)S(1)}, f32[56,896]{1,0:T(8,128)S(1)}, u32[]{:S(2)}, u32[]{:S(2)}) collective-permute-start(f32[56,896]{1,0:T(8,128)S(1)} %bitcast.43), channel_id=1, source_target_pairs={{0,8},{1,9},{2,10},{3,11},{4,12},{5,13},{6,14},{7,15},{8,0},{9,1},... | collective-permute-start | bytes 602120 | tf_op jit(solution)/shard_map/gather_amp/ppermute | solution.py:34
  7.4 9.4 %collective-permute-done = f32[56,896]{1,0:T(8,128)S(1)} collective-permute-done((f32[56,896]{1,0:T(8,128)S(1)}, f32[56,896]{1,0:T(8,128)S(1)}, u32[]{:S(2)}, u32[]{:S(2)}) %collective-permute-start) | collective-permute-done | bytes 200736 | tf_op jit(solution)/shard_map/gather_amp/ppermute | solution.py:34
  16.8 0.1 collective-permute-start.1
  16.9 1.7 %collective-permute-done.1.refs_1_ = f32[112,896]{1,0:T(8,128)S(1)} collective-permute-done((f32[112,896]{1,0:T(8,128)S(1)}, f32[112,896]{1,0:T(8,128)S(1)}, u32[]{:S(2)}, u32[]{:S(2)}) %collective-permute-start.1) | collective-permute-done | bytes 401440 | tf_op jit(solution)/shard_map/gather_amp/ppermute | solution.py:34
  18.6 0.1 pad_maximum_fusion
  18.7 1.6 %collective-permute-start.2 = (f32[224,896]{1,0:T(8,128)S(1)}, f32[224,896]{1,0:T(8,128)S(1)}, u32[]{:S(2)}, u32[]{:S(2)}) collective-permute-start(f32[224,896]{1,0:T(8,128)S(1)} %pad_maximum_fusion), channel_id=1, source_target_pairs={{0,2},{1,7},{2,4},{3,1},{4,6},{5,3},{6,0},{7,5},{8,10},{9,15},{10,... | collective-permute-start | bytes 2408456 | tf_op jit(solution)/shard_map/gather_amp/ppermute | solution.py:34
  20.2 0.0 collective-permute-start.6
  20.2 2.8 %collective-permute-start.11 = (f32[56,896]{1,0:T(8,128)S(1)}, f32[56,896]{1,0:T(8,128)S(1)}, u32[]{:S(2)}, u32[]{:S(2)}) collective-permute-start(f32[56,896]{1,0:T(8,128)S(1)} %bitcast.47), channel_id=1, source_target_pairs={{0,128},{16,144},{32,160},{48,176},{64,192},{80,208},{96,224},{112... | collective-permute-start | bytes 602120 | tf_op jit(solution)/shard_map/gather_fit/ppermute | solution.py:24
  23.0 0.7 collective-permute-start.12
  23.7 5.3 %collective-permute-done.6 = f32[56,896]{1,0:T(8,128)S(1)} collective-permute-done((f32[56,896]{1,0:T(8,128)S(1)}, f32[56,896]{1,0:T(8,128)S(1)}, u32[]{:S(2)}, u32[]{:S(2)}) %collective-permute-start.6) | collective-permute-done | bytes 200736 | tf_op jit(solution)/shard_map/gather_fit/ppermute | solution.py:24
  29.1 3.1 %collective-permute-start.8 = (f32[112,896]{1,0:T(8,128)S(1)}, f32[112,896]{1,0:T(8,128)S(1)}, u32[]{:S(2)}, u32[]{:S(2)}) collective-permute-start(f32[112,896]{1,0:T(8,128)S(1)} %pad_maximum_fusion.2.refs_6_), channel_id=1, source_target_pairs={{0,48},{16,0},{32,16},{48,32},{64,112},{80,64},{96,80},{112,96},{1... | collective-permute-start | bytes 1204232 | tf_op jit(solution)/shard_map/gather_fit/ppermute | solution.py:24
  32.2 0.0 collective-permute-start.7
  32.2 0.7 collective-permute-start.4
  32.9 4.2 %collective-permute-done.11 = f32[56,896]{1,0:T(8,128)S(1)} collective-permute-done((f32[56,896]{1,0:T(8,128)S(1)}, f32[56,896]{1,0:T(8,128)S(1)}, u32[]{:S(2)}, u32[]{:S(2)}) %collective-permute-start.11) | collective-permute-done | bytes 200736 | tf_op jit(solution)/shard_map/gather_fit/ppermute | solution.py:24
  37.0 0.0 collective-permute-start.3
  37.1 0.7 constant_dynamic-update-slice_fusion.1
  37.7 4.6 %collective-permute-done.12 = f32[56,896]{1,0:T(8,128)S(1)} collective-permute-done((f32[56,896]{1,0:T(8,128)S(1)}, f32[56,896]{1,0:T(8,128)S(1)}, u32[]{:S(2)}, u32[]{:S(2)}) %collective-permute-start.12) | collective-permute-done | bytes 200736 | tf_op jit(solution)/shard_map/gather_fit/ppermute | solution.py:24
  42.4 0.7 constant_dynamic-update-slice_fusion.refs_6_
  43.1 3.0 %collective-permute-start.14 = (f32[112,896]{1,0:T(8,128)}, f32[112,896]{1,0:T(8,128)S(1)}, u32[]{:S(2)}, u32[]{:S(2)}) collective-permute-start(f32[112,896]{1,0:T(8,128)} %constant_dynamic-update-slice_fusion.refs_6_), channel_id=1, source_target_pairs={{0,48},{16,0},{32,16},{48,32},{64,112},{80,64},{96,80},{112,96},{1... | collective-permute-start | bytes 1204232 | tf_op jit(solution)/shard_map/gather_fit/ppermute | solution.py:24
  46.1 0.1 collective-permute-start.5
  46.2 0.7 slice.54
  46.9 0.0 collective-permute-done.7.refs_7_
  46.9 3.1 %collective-permute-start.10 = (f32[56,896]{1,0:T(8,128)}, f32[56,896]{1,0:T(8,128)S(1)}, u32[]{:S(2)}, u32[]{:S(2)}) collective-permute-start(f32[56,896]{1,0:T(8,128)} %slice.54), channel_id=1, source_target_pairs={{0,48},{16,0},{32,16},{48,32},{64,112},{80,64},{96,80},{112,96},{1... | collective-permute-start | bytes 602120 | tf_op jit(solution)/shard_map/gather_fit/ppermute | solution.py:24
  50.0 0.7 slice.53
  50.7 5.4 %collective-permute-done.14.refs_8_ = f32[112,896]{1,0:T(8,128)S(1)} collective-permute-done((f32[112,896]{1,0:T(8,128)}, f32[112,896]{1,0:T(8,128)S(1)}, u32[]{:S(2)}, u32[]{:S(2)}) %collective-permute-start.14) | collective-permute-done | bytes 401440 | tf_op jit(solution)/shard_map/gather_fit/ppermute | solution.py:24
  56.1 0.9 collective-permute-start.9
  57.0 0.1 stack.23.place_ref
  57.1 1.4 %collective-permute-done.13.refs_7_ = f32[112,896]{1,0:T(8,128)} collective-permute-done((f32[112,896]{1,0:T(8,128)}, f32[112,896]{1,0:T(8,128)}, u32[]{:S(2)}, u32[]{:S(2)}) %collective-permute-start.13) | collective-permute-done | bytes 401440 | tf_op jit(solution)/shard_map/gather_fit/ppermute | solution.py:24
  58.5 1.3 %collective-permute-start.16 = (f32[56,896]{1,0:T(8,128)S(1)}, f32[56,896]{1,0:T(8,128)S(1)}, u32[]{:S(2)}, u32[]{:S(2)}) collective-permute-start(f32[56,896]{1,0:T(8,128)S(1)} %slice.56), channel_id=1, source_target_pairs={{0,48},{16,0},{32,16},{48,32},{64,112},{80,64},{96,80},{112,96},{1... | collective-permute-start | bytes 602120 | tf_op jit(solution)/shard_map/gather_fit/ppermute | solution.py:24
  59.9 0.9 slice.55
  60.8 0.0 collective-permute-done.10.refs_10_
  60.8 0.9 collective-permute-start.15
  61.7 2.4 %collective-permute-done.9.refs_9_ = f32[56,896]{1,0:T(8,128)} collective-permute-done((f32[56,896]{1,0:T(8,128)}, f32[56,896]{1,0:T(8,128)}, u32[]{:S(2)}, u32[]{:S(2)}) %collective-permute-start.9) | collective-permute-done | bytes 200736 | tf_op jit(solution)/shard_map/gather_fit/ppermute | solution.py:24
  64.2 0.0 collective-permute-done.5.refs_5_
  64.2 0.0 collective-permute-done.3.refs_3_
  64.2 8.9 %first_half.1 = (bf16[896,896]{1,0:T(8,128)(2,1)S(1)}, bf16[896,896]{1,0:T(8,128)(2,1)S(1)}, bf16[448,896]{1,0:T(8,128)(2,1)S(1)}, bf16[448,896]{1,0:T(8,128)(2,...) custom-call(s32[5]{0:T(128)S(1)} %stack.23.place_ref, f32[112,896]{1,0:T(8,128)S(1)} %pad_maximum_fusion.1.refs_0_, ...), custom_call_target="tpu_custom_call" | custom-call | flops 2157969408 | bytes 9633792 | tf_op jit(solution)/shard_map/first_half/pallas_call | solution.py:146
  73.1 0.0 collective-permute-done.16.refs_10_
  73.1 0.0 collective-permute-done.15.refs_9_
  73.1 10.8 %second_half.1 = (bf16[896,896]{1,0:T(8,128)(2,1)S(1)}, bf16[896,896]{1,0:T(8,128)(2,1)S(1)}, bf16[896,896]{1,0:T(8,128)(2,1)S(1)}, bf16[896,896]{1,0:T(8,128)(2...) custom-call(s32[5]{0:T(128)S(1)} %stack.23.place_ref, bf16[896,896]{1,0:T(8,128)(2,1)S(1)} %get-tuple-element.19.refs_0_, ...), custom_call_target="tpu_custom_call" | custom-call | flops 4315938816 | bytes 16056320 | tf_op jit(solution)/shard_map/second_half/pallas_call | solution.py:146
  83.9 0.1 collective-permute-start.21
  84.0 5.7 %near_rows.1 = (f32[4,56,896]{2,1,0:T(8,128)S(1)}, f32[4,56,896]{2,1,0:T(8,128)S(1)}) custom-call(s32[5]{0:T(128)S(1)} %stack.23.place_ref, bf16[896,896]{1,0:T(8,128)(2,1)S(1)} %get-tuple-element.25.b_hi, bf16[896,896]{1,0:T(8,128)(2,1)S(1)} %get-tuple-element.26.b_lo, bf16[896,896]{1,0:T(8,128)(2,1)S(1)} %get-tuple-element.27.g_hi, ...), custom_call_target="tpu_custom_call" | custom-call | flops 2157969408 | bytes 9633792 | tf_op jit(solution)/shard_map/near_rows/pallas_call | solution.py:146
  89.7 0.6 collective-permute-start.17
  90.3 0.0 collective-permute-done.21
  90.3 0.1 add.47
  90.5 0.1 collective-permute-start.22
  90.6 3.2 %collective-permute-start.24 = (f32[56,896]{1,0:T(8,128)S(1)}, f32[56,896]{1,0:T(8,128)S(1)}, u32[]{:S(2)}, u32[]{:S(2)}) collective-permute-start(f32[56,896]{1,0:T(8,128)S(1)} %get-tuple-element.37), channel_id=1, source_target_pairs={{0,6},{1,7},{2,0},{3,1},{4,2},{5,3},{6,4},{7,5},{8,14},{9,15},{10,... | collective-permute-start | bytes 602120 | tf_op jit(solution)/shard_map/reduce/ppermute | solution.py:34
  93.8 0.4 collective-permute-start.23
  94.2 0.0 collective-permute-done.17
  94.2 0.1 add.43
  94.3 1.5 %collective-permute-start.18 = (f32[56,896]{1,0:T(8,128)S(1)}, f32[56,896]{1,0:T(8,128)S(1)}, u32[]{:S(2)}, u32[]{:S(2)}) collective-permute-start(f32[56,896]{1,0:T(8,128)S(1)} %get-tuple-element.33), channel_id=1, source_target_pairs={{0,2},{1,3},{2,4},{3,5},{4,6},{5,7},{6,0},{7,1},{8,10},{9,11},{10,... | collective-permute-start | bytes 602120 | tf_op jit(solution)/shard_map/reduce/ppermute | solution.py:34
  95.8 1.8 %collective-permute-start.20 = (f32[56,896]{1,0:T(8,128)S(1)}, f32[56,896]{1,0:T(8,128)S(1)}, u32[]{:S(2)}, u32[]{:S(2)}) collective-permute-start(f32[56,896]{1,0:T(8,128)S(1)} %get-tuple-element.34), channel_id=1, source_target_pairs={{0,6},{1,7},{2,0},{3,1},{4,2},{5,3},{6,4},{7,5},{8,14},{9,15},{10,... | collective-permute-start | bytes 602120 | tf_op jit(solution)/shard_map/reduce/ppermute | solution.py:34
  97.7 5.8 %collective-permute-done.22 = f32[56,896]{1,0:T(8,128)S(1)} collective-permute-done((f32[56,896]{1,0:T(8,128)S(1)}, f32[56,896]{1,0:T(8,128)S(1)}, u32[]{:S(2)}, u32[]{:S(2)}) %collective-permute-start.22) | collective-permute-done | bytes 200736 | tf_op jit(solution)/shard_map/reduce/ppermute | solution.py:34
  103.4 0.0 collective-permute-start.19
  103.4 0.1 collective-permute-done.24
  103.5 0.9 collective-permute-done.23
  104.4 0.1 fusion.2
  104.4 5.7 %collective-permute-start.25 = (f32[56,896]{1,0:T(8,128)S(1)}, f32[56,896]{1,0:T(8,128)S(1)}, u32[]{:S(2)}, u32[]{:S(2)}) collective-permute-start(f32[56,896]{1,0:T(8,128)S(1)} %fusion.2), channel_id=1, source_target_pairs={{0,8},{1,9},{2,10},{3,11},{4,12},{5,13},{6,14},{7,15},{8,0},{9,1},... | collective-permute-start | bytes 602120 | tf_op jit(solution)/shard_map/reduce/ppermute | solution.py:34
  110.1 0.0 collective-permute-done.18
  110.1 0.8 collective-permute-done.20
  110.9 1.2 collective-permute-done.19
  112.0 4.0 %collective-permute-done.25 = f32[56,896]{1,0:T(8,128)S(1)} collective-permute-done((f32[56,896]{1,0:T(8,128)S(1)}, f32[56,896]{1,0:T(8,128)S(1)}, u32[]{:S(2)}, u32[]{:S(2)}) %collective-permute-start.25) | collective-permute-done | bytes 200736 | tf_op jit(solution)/shard_map/reduce/ppermute | solution.py:34
  116.1 0.1 fusion.7
  116.1 0.9 copy.3
  (12 shorter events, 0.2 us)
Async XLA Ops:
  0.0 20.2 %copy-start = (f32[1,56,896]{2,1,0:T(8,128)S(1)}, f32[1,56,896]{2,1,0:T(8,128)}, u32[]{:S(2)}) copy-start(f32[1,56,896]{2,1,0:T(8,128)} %param.3) | copy-start | bytes 602116
  1.0 15.8 %collective-permute-start = (f32[56,896]{1,0:T(8,128)S(1)}, f32[56,896]{1,0:T(8,128)S(1)}, u32[]{:S(2)}, u32[]{:S(2)}) collective-permute-start(f32[56,896]{1,0:T(8,128)S(1)} %bitcast.43), channel_id=1, source_target_pairs={{0,8},{1,9},{2,10},{3,11},{4,12},{5,13},{6,14},{7,15},{8,0},{9,1},... | collective-permute-start | bytes 602120 | tf_op jit(solution)/shard_map/gather_amp/ppermute | solution.py:34
  16.8 1.8 %collective-permute-start.1 = (f32[112,896]{1,0:T(8,128)S(1)}, f32[112,896]{1,0:T(8,128)S(1)}, u32[]{:S(2)}, u32[]{:S(2)}) collective-permute-start(f32[112,896]{1,0:T(8,128)S(1)} %pad_maximum_fusion.1.refs_0_), channel_id=1, source_target_pairs={{0,1},{1,0},{2,3},{3,2},{4,5},{5,4},{6,7},{7,6},{8,9},{9,8},{10,11... | collective-permute-start | bytes 1204232 | tf_op jit(solution)/shard_map/gather_amp/ppermute | solution.py:34
  18.7 13.5 %collective-permute-start.2 = (f32[224,896]{1,0:T(8,128)S(1)}, f32[224,896]{1,0:T(8,128)S(1)}, u32[]{:S(2)}, u32[]{:S(2)}) collective-permute-start(f32[224,896]{1,0:T(8,128)S(1)} %pad_maximum_fusion), channel_id=1, source_target_pairs={{0,2},{1,7},{2,4},{3,1},{4,6},{5,3},{6,0},{7,5},{8,10},{9,15},{10,... | collective-permute-start | bytes 2408456 | tf_op jit(solution)/shard_map/gather_amp/ppermute | solution.py:34
  20.2 8.8 %collective-permute-start.6 = (f32[56,896]{1,0:T(8,128)S(1)}, f32[56,896]{1,0:T(8,128)S(1)}, u32[]{:S(2)}, u32[]{:S(2)}) collective-permute-start(f32[56,896]{1,0:T(8,128)S(1)} %bitcast.46), channel_id=1, source_target_pairs={{0,64},{16,80},{32,96},{48,112},{64,0},{80,16},{96,32},{112,48},{1... | collective-permute-start | bytes 602120 | tf_op jit(solution)/shard_map/gather_fit/ppermute | solution.py:24
  20.2 16.8 %collective-permute-start.11 = (f32[56,896]{1,0:T(8,128)S(1)}, f32[56,896]{1,0:T(8,128)S(1)}, u32[]{:S(2)}, u32[]{:S(2)}) collective-permute-start(f32[56,896]{1,0:T(8,128)S(1)} %bitcast.47), channel_id=1, source_target_pairs={{0,128},{16,144},{32,160},{48,176},{64,192},{80,208},{96,224},{112... | collective-permute-start | bytes 602120 | tf_op jit(solution)/shard_map/gather_fit/ppermute | solution.py:24
  23.0 19.4 %collective-permute-start.12 = (f32[56,896]{1,0:T(8,128)S(1)}, f32[56,896]{1,0:T(8,128)S(1)}, u32[]{:S(2)}, u32[]{:S(2)}) collective-permute-start(f32[56,896]{1,0:T(8,128)S(1)} %bitcast.48), channel_id=1, source_target_pairs={{0,192},{16,208},{32,224},{48,240},{64,128},{80,144},{96,160},{112... | collective-permute-start | bytes 602120 | tf_op jit(solution)/shard_map/gather_fit/ppermute | solution.py:24
  29.1 17.0 %collective-permute-start.8 = (f32[112,896]{1,0:T(8,128)S(1)}, f32[112,896]{1,0:T(8,128)S(1)}, u32[]{:S(2)}, u32[]{:S(2)}) collective-permute-start(f32[112,896]{1,0:T(8,128)S(1)} %pad_maximum_fusion.2.refs_6_), channel_id=1, source_target_pairs={{0,48},{16,0},{32,16},{48,32},{64,112},{80,64},{96,80},{112,96},{1... | collective-permute-start | bytes 1204232 | tf_op jit(solution)/shard_map/gather_fit/ppermute | solution.py:24
  32.2 14.7 %collective-permute-start.7 = (f32[112,896]{1,0:T(8,128)S(1)}, f32[112,896]{1,0:T(8,128)S(1)}, u32[]{:S(2)}, u32[]{:S(2)}) collective-permute-start(f32[112,896]{1,0:T(8,128)S(1)} %pad_maximum_fusion.2.refs_6_), channel_id=1, source_target_pairs={{0,16},{16,32},{32,48},{48,0},{64,80},{80,96},{96,112},{112,64},{1... | collective-permute-start | bytes 1204232 | tf_op jit(solution)/shard_map/gather_fit/ppermute | solution.py:24
  32.2 13.9 %collective-permute-start.4 = (f32[112,896]{1,0:T(8,128)S(1)}, f32[112,896]{1,0:T(8,128)}, u32[]{:S(2)}, u32[]{:S(2)}) collective-permute-start(f32[112,896]{1,0:T(8,128)S(1)} %slice.52), channel_id=1, source_target_pairs={{0,2},{1,7},{2,4},{3,1},{4,6},{5,3},{6,0},{7,5},{8,10},{9,15},{10,... | collective-permute-start | bytes 1204232 | tf_op jit(solution)/shard_map/gather_amp/ppermute | solution.py:34
  37.0 27.1 %collective-permute-start.3 = (f32[224,896]{1,0:T(8,128)S(1)}, f32[224,896]{1,0:T(8,128)}, u32[]{:S(2)}, u32[]{:S(2)}) collective-permute-start(f32[224,896]{1,0:T(8,128)S(1)} %collective-permute-done.2.refs_2_), channel_id=1, source_target_pairs={{0,1},{1,0},{2,3},{3,2},{4,5},{5,4},{6,7},{7,6},{8,9},{9,8},{10,11... | collective-permute-start | bytes 2408456 | tf_op jit(solution)/shard_map/gather_amp/ppermute | solution.py:34
  43.1 13.0 %collective-permute-start.14 = (f32[112,896]{1,0:T(8,128)}, f32[112,896]{1,0:T(8,128)S(1)}, u32[]{:S(2)}, u32[]{:S(2)}) collective-permute-start(f32[112,896]{1,0:T(8,128)} %constant_dynamic-update-slice_fusion.refs_6_), channel_id=1, source_target_pairs={{0,48},{16,0},{32,16},{48,32},{64,112},{80,64},{96,80},{112,96},{1... | collective-permute-start | bytes 1204232 | tf_op jit(solution)/shard_map/gather_fit/ppermute | solution.py:24
  46.1 12.4 %collective-permute-start.13 = (f32[112,896]{1,0:T(8,128)}, f32[112,896]{1,0:T(8,128)}, u32[]{:S(2)}, u32[]{:S(2)}) collective-permute-start(f32[112,896]{1,0:T(8,128)} %constant_dynamic-update-slice_fusion.refs_6_), channel_id=1, source_target_pairs={{0,16},{16,32},{32,48},{48,0},{64,80},{80,96},{96,112},{112,64},{1... | collective-permute-start | bytes 1204232 | tf_op jit(solution)/shard_map/gather_fit/ppermute | solution.py:24
  46.1 18.1 %collective-permute-start.5 = (f32[112,896]{1,0:T(8,128)}, f32[112,896]{1,0:T(8,128)}, u32[]{:S(2)}, u32[]{:S(2)}) collective-permute-start(f32[112,896]{1,0:T(8,128)} %collective-permute-done.4.refs_4_), channel_id=1, source_target_pairs={{0,1},{1,0},{2,3},{3,2},{4,5},{5,4},{6,7},{7,6},{8,9},{9,8},{10,11... | collective-permute-start | bytes 1204232 | tf_op jit(solution)/shard_map/gather_amp/ppermute | solution.py:34
  46.9 13.9 %collective-permute-start.10 = (f32[56,896]{1,0:T(8,128)}, f32[56,896]{1,0:T(8,128)S(1)}, u32[]{:S(2)}, u32[]{:S(2)}) collective-permute-start(f32[56,896]{1,0:T(8,128)} %slice.54), channel_id=1, source_target_pairs={{0,48},{16,0},{32,16},{48,32},{64,112},{80,64},{96,80},{112,96},{1... | collective-permute-start | bytes 602120 | tf_op jit(solution)/shard_map/gather_fit/ppermute | solution.py:24
  56.1 8.1 %collective-permute-start.9 = (f32[56,896]{1,0:T(8,128)}, f32[56,896]{1,0:T(8,128)}, u32[]{:S(2)}, u32[]{:S(2)}) collective-permute-start(f32[56,896]{1,0:T(8,128)} %slice.53), channel_id=1, source_target_pairs={{0,16},{16,32},{32,48},{48,0},{64,80},{80,96},{96,112},{112,64},{1... | collective-permute-start | bytes 602120 | tf_op jit(solution)/shard_map/gather_fit/ppermute | solution.py:24
  58.5 14.6 %collective-permute-start.16 = (f32[56,896]{1,0:T(8,128)S(1)}, f32[56,896]{1,0:T(8,128)S(1)}, u32[]{:S(2)}, u32[]{:S(2)}) collective-permute-start(f32[56,896]{1,0:T(8,128)S(1)} %slice.56), channel_id=1, source_target_pairs={{0,48},{16,0},{32,16},{48,32},{64,112},{80,64},{96,80},{112,96},{1... | collective-permute-start | bytes 602120 | tf_op jit(solution)/shard_map/gather_fit/ppermute | solution.py:24
  60.8 12.3 %collective-permute-start.15 = (f32[56,896]{1,0:T(8,128)S(1)}, f32[56,896]{1,0:T(8,128)S(1)}, u32[]{:S(2)}, u32[]{:S(2)}) collective-permute-start(f32[56,896]{1,0:T(8,128)S(1)} %slice.55), channel_id=1, source_target_pairs={{0,16},{16,32},{32,48},{48,0},{64,80},{80,96},{96,112},{112,64},{1... | collective-permute-start | bytes 602120 | tf_op jit(solution)/shard_map/gather_fit/ppermute | solution.py:24
  83.9 6.4 %collective-permute-start.21 = (f32[4,56,896]{2,1,0:T(8,128)S(1)}, f32[4,56,896]{2,1,0:T(8,128)S(1)}, u32[]{:S(2)}, u32[]{:S(2)}) collective-permute-start(f32[4,56,896]{2,1,0:T(8,128)S(1)} %get-tuple-element.32), channel_id=1, source_target_pairs={{0,1},{1,0},{2,3},{3,2},{4,5},{5,4},{6,7},{7,6},{8,9},{9,8},{10,11... | collective-permute-start | bytes 2408456 | tf_op jit(solution)/shard_map/reduce/ppermute | solution.py:34
  89.7 4.5 %collective-permute-start.17 = (f32[4,56,896]{2,1,0:T(8,128)S(1)}, f32[4,56,896]{2,1,0:T(8,128)S(1)}, u32[]{:S(2)}, u32[]{:S(2)}) collective-permute-start(f32[4,56,896]{2,1,0:T(8,128)S(1)} %get-tuple-element.30), channel_id=1, source_target_pairs={{0,1},{1,0},{2,3},{3,2},{4,5},{5,4},{6,7},{7,6},{8,9},{9,8},{10,11... | collective-permute-start | bytes 2408456 | tf_op jit(solution)/shard_map/reduce/ppermute | solution.py:34
  90.5 13.0 %collective-permute-start.22 = (f32[56,896]{1,0:T(8,128)S(1)}, f32[56,896]{1,0:T(8,128)S(1)}, u32[]{:S(2)}, u32[]{:S(2)}) collective-permute-start(f32[56,896]{1,0:T(8,128)S(1)} %get-tuple-element.36), channel_id=1, source_target_pairs={{0,2},{1,3},{2,4},{3,5},{4,6},{5,7},{6,0},{7,1},{8,10},{9,11},{10,... | collective-permute-start | bytes 602120 | tf_op jit(solution)/shard_map/reduce/ppermute | solution.py:34
  90.6 12.9 %collective-permute-start.24 = (f32[56,896]{1,0:T(8,128)S(1)}, f32[56,896]{1,0:T(8,128)S(1)}, u32[]{:S(2)}, u32[]{:S(2)}) collective-permute-start(f32[56,896]{1,0:T(8,128)S(1)} %get-tuple-element.37), channel_id=1, source_target_pairs={{0,6},{1,7},{2,0},{3,1},{4,2},{5,3},{6,4},{7,5},{8,14},{9,15},{10,... | collective-permute-start | bytes 602120 | tf_op jit(solution)/shard_map/reduce/ppermute | solution.py:34
  93.8 10.6 %collective-permute-start.23 = (f32[56,896]{1,0:T(8,128)S(1)}, f32[56,896]{1,0:T(8,128)S(1)}, u32[]{:S(2)}, u32[]{:S(2)}) collective-permute-start(f32[56,896]{1,0:T(8,128)S(1)} %get-tuple-element.38), channel_id=1, source_target_pairs={{0,4},{1,5},{2,6},{3,7},{4,0},{5,1},{6,2},{7,3},{8,12},{9,13},{10,... | collective-permute-start | bytes 602120 | tf_op jit(solution)/shard_map/reduce/ppermute | solution.py:34
  94.3 15.7 %collective-permute-start.18 = (f32[56,896]{1,0:T(8,128)S(1)}, f32[56,896]{1,0:T(8,128)S(1)}, u32[]{:S(2)}, u32[]{:S(2)}) collective-permute-start(f32[56,896]{1,0:T(8,128)S(1)} %get-tuple-element.33), channel_id=1, source_target_pairs={{0,2},{1,3},{2,4},{3,5},{4,6},{5,7},{6,0},{7,1},{8,10},{9,11},{10,... | collective-permute-start | bytes 602120 | tf_op jit(solution)/shard_map/reduce/ppermute | solution.py:34
  95.8 15.0 %collective-permute-start.20 = (f32[56,896]{1,0:T(8,128)S(1)}, f32[56,896]{1,0:T(8,128)S(1)}, u32[]{:S(2)}, u32[]{:S(2)}) collective-permute-start(f32[56,896]{1,0:T(8,128)S(1)} %get-tuple-element.34), channel_id=1, source_target_pairs={{0,6},{1,7},{2,0},{3,1},{4,2},{5,3},{6,4},{7,5},{8,14},{9,15},{10,... | collective-permute-start | bytes 602120 | tf_op jit(solution)/shard_map/reduce/ppermute | solution.py:34
  103.4 8.6 %collective-permute-start.19 = (f32[56,896]{1,0:T(8,128)S(1)}, f32[56,896]{1,0:T(8,128)S(1)}, u32[]{:S(2)}, u32[]{:S(2)}) collective-permute-start(f32[56,896]{1,0:T(8,128)S(1)} %get-tuple-element.35), channel_id=1, source_target_pairs={{0,4},{1,5},{2,6},{3,7},{4,0},{5,1},{6,2},{7,3},{8,12},{9,13},{10,... | collective-permute-start | bytes 602120 | tf_op jit(solution)/shard_map/reduce/ppermute | solution.py:34
  104.4 11.6 %collective-permute-start.25 = (f32[56,896]{1,0:T(8,128)S(1)}, f32[56,896]{1,0:T(8,128)S(1)}, u32[]{:S(2)}, u32[]{:S(2)}) collective-permute-start(f32[56,896]{1,0:T(8,128)S(1)} %fusion.2), channel_id=1, source_target_pairs={{0,8},{1,9},{2,10},{3,11},{4,12},{5,13},{6,14},{7,15},{8,0},{9,1},... | collective-permute-start | bytes 602120 | tf_op jit(solution)/shard_map/reduce/ppermute | solution.py:34

commit v3 on v0

v3 whole, which is shorter than its diff:
```python
import jax
import jax.numpy as jnp
from jax import lax
from jax.experimental import pallas as pl
from jax.experimental.pallas import tpu as pltpu
from jax.sharding import PartitionSpec as P

NZL, NY, NZH, NX, NC = 4, 4, 2, 4, 2
V = 896
HALF = 448
ROWS = 56
NN = (((1,), (0,)), ((), ()))
NT = (((1,), (1,)), ((), ()))
ANY = pl.BlockSpec(memory_space=pl.ANY)
SMEM = pl.BlockSpec(memory_space=pltpu.SMEM)


def pair_permute(value, target):
    steps = []
    for zl in range(NZL):
        for y in range(NY):
            tz, ty = target(zl, y)
            steps.append((zl * NY + y, (tz % NZL) * NY + ty % NY))
    return lax.ppermute(value, "pair", steps)


def aux_permute(value, target):
    steps = []
    for zh in range(NZH):
        for x in range(NX):
            for c in range(NC):
                th, tx, tc = target(zh, x, c)
                steps.append(((zh * NX + x) * NC + c, ((th % NZH) * NX + tx % NX) * NC + tc % NC))
    return lax.ppermute(value, "aux", steps)


def swap_core(value):
    return aux_permute(value, lambda zh, x, c: (zh, x, 1 - c))


def split(value):
    high = value.astype(jnp.bfloat16)
    low = (value - high.astype(jnp.float32)).astype(jnp.bfloat16)
    return high, low


def product(left, right, dims):
    def dot(a, b):
        return lax.dot_general(a, b, dims, preferred_element_type=jnp.float32)

    return dot(left[1], right[0]) + dot(left[0], right[1]) + dot(left[0], right[0])


def run_copies(copies):
    for copy in copies:
        copy.start()
    for copy in copies:
        copy.wait()


def fit_copies(places, target, zl, y, sem, first):
    copies = []
    for index, (ref, part, k, j) in enumerate(places):
        row = pl.multiple_of(((zl ^ k) * NY + (y + j) % NY) * ROWS, 8)
        copies.append(
            pltpu.make_async_copy(ref.at[pl.ds(part * ROWS, ROWS)], target.at[pl.ds(row, ROWS)], sem.at[first + index])
        )
    return copies


def amp_copies(refs, target, zh, x, core, sem):
    own, far, beside, beside_far, across, across_far, relay, relay_other = refs
    step = 2 * core - 1
    places = []
    for f, here, there, back in ((0, own, beside, across), (1, far, beside_far, across_far)):
        places += [(here, 0, f, 0, core), (here, 1, f, 0, 1 - core)]
        places += [(there, 0, f, step, core), (there, 1, f, step, 1 - core)]
        places += [(back, 0, f, -step, 1 - core), (back, 1, f, -step, core)]
        places += [(relay, f, f, 2, core), (relay_other, f, f, 2, 1 - core)]
    copies = []
    for index, (ref, part, f, dx, c) in enumerate(places):
        row = pl.multiple_of((((zh + f) % NZH) * 8 + ((x + dx + NX) % NX) * 2 + c) * ROWS, 8)
        copies.append(
            pltpu.make_async_copy(ref.at[pl.ds(part * ROWS, ROWS)], target.at[pl.ds(row, ROWS)], sem.at[index])
        )
    return copies


def ladder_kernel(place_ref, *refs):
    t_refs, own = refs[:8], refs[8:12]
    both, below, above, three, up3, down3, across3 = refs[12:19]
    outs = refs[19:23]
    t32, b32, t_hi, t_lo, b_hi, b_lo, g_hi, g_lo, total, sem, out_sem = refs[23:]
    zl, y, zh, x, core = (place_ref[i] for i in range(5))
    places = [(ref, 0, 0, j) for ref, j in zip(own, (0, 3, 1, 2))]
    for part in (0, 1):
        places += [(both, part, part + 1, 0), (below, part, part + 1, 3), (above, part, part + 1, 1)]
    places += [(three, 0, 3, 0), (up3, 0, 3, 3), (up3, 1, 2, 2), (down3, 0, 3, 1), (down3, 1, 1, 2), (across3, 0, 3, 2)]
    amp = amp_copies(t_refs, t32, zh, x, core, sem)
    fit = fit_copies(places, b32, zl, y, sem, 16)
    for copy in amp + fit:
        copy.start()
    for copy in amp:
        copy.wait()
    for row in range(0, V, 128):
        rows = slice(row, row + 128)
        t_hi[rows], t_lo[rows] = split(t32[rows])
    for copy in fit:
        copy.wait()
    for row in (0, HALF):
        rows = slice(row, row + HALF)
        b_hi[rows], b_lo[rows] = split(b32[rows])
        g_hi[rows], g_lo[rows] = split(product((b_hi[rows], b_lo[rows]), (t_hi[...], t_lo[...]), NN))
    copies = []
    for far in (1, 0):
        half = (zh + far) % NZH
        rows = pl.ds(pl.multiple_of(half * HALF, HALF), HALF)
        total[far] = product((g_hi[rows], g_lo[rows]), (b_hi[...], b_lo[...]), NT)
        for k in range(NX):
            block = ((x + k) % NX) * 2
            for n, c in enumerate((core, 1 - core)):
                row = pl.multiple_of((block + c) * ROWS, 8)
                copies.append(
                    pltpu.make_async_copy(
                        total.at[far, pl.ds(row, ROWS)], outs[2 * (1 - far) + n].at[k], out_sem.at[far, n, k]
                    )
                )
                copies[-1].start()
    for copy in copies:
        copy.wait()


def call(kernel, outs, out_specs, scratch, args, in_specs, flops, moved, name):
    return pl.pallas_call(
        kernel,
        out_shape=outs,
        in_specs=in_specs,
        out_specs=out_specs,
        scratch_shapes=scratch,
        compiler_params=pltpu.CompilerParams(vmem_limit_bytes=52 * 1024 * 1024),
        cost_estimate=pl.CostEstimate(flops=flops, bytes_accessed=moved, transcendentals=0),
        name=name,
    )(*args)


def per_device(amplitudes, fitting):
    pair, aux = lax.axis_index("pair"), lax.axis_index("aux")
    place = jnp.stack([pair // NY, pair % NY, aux // 8, aux // 2 % NX, aux % 2]).astype(jnp.int32)
    fit = fitting.reshape(ROWS, V)

    def up(value):
        return pair_permute(value, lambda zl, y: (zl, y + 1))

    def down(value):
        return pair_permute(value, lambda zl, y: (zl, y - 1))

    def beside_x(value):
        return aux_permute(value, lambda zh, x, c: (zh, x + 1 - 2 * c, c))

    def pack(*parts):
        return jnp.concatenate(parts)

    tie = lax.optimization_barrier
    amp = amplitudes.reshape(ROWS, V)
    with jax.named_scope("gather"):
        near = pair_permute(fit, lambda zl, y: (zl ^ 1, y))
        two = pair_permute(fit, lambda zl, y: (zl ^ 2, y))
        own = pack(amp, swap_core(amp))
        fit_0 = up(fit), down(fit)
        beside = beside_x(own)
        amp_late, beside, fit_0, near, two = tie((amp, beside, fit_0, near, two))

        far = aux_permute(amp_late, lambda zh, x, c: (1 - zh, x, c))
        three = pair_permute(two, lambda zl, y: (zl ^ 1, y))
        both = pack(near, two)
        below, above = up(both), down(both)
        low = up(fit_0[0])
        low, below, above, three, far = tie((low, below, above, three, far))

        far_amp, far = far, pack(far, swap_core(far))
        beside_far, beside = tie((beside_x(far), beside))
        up3 = up(pack(three, below[ROWS:]))
        down3 = down(pack(three, above[:ROWS]))
        across3 = pair_permute(three, lambda zl, y: (zl, y + 2))
        relay = aux_permute(pack(amp, far_amp), lambda zh, x, c: (zh, x + 2, c))
        amps = [own, far, beside, beside_far, swap_core(beside), swap_core(beside_far), relay, swap_core(relay)]
        fits = [fit, *fit_0, low, both, below, above, three, up3, down3, across3]

    blocks = jax.ShapeDtypeStruct((NX, ROWS, V), jnp.float32)
    vmem = pltpu.VMEM
    sems = pltpu.SemaphoreType.DMA
    far_keep, far_send, near_keep, near_send = call(
        ladder_kernel,
        (blocks,) * 4,
        (ANY,) * 4,
        [vmem((V, V), jnp.float32)] * 2
        + [vmem((V, V), jnp.bfloat16)] * 6
        + [vmem((2, HALF, V), jnp.float32), sems((32,)), sems((2, 2, NX))],
        (place, *amps, *fits),
        [SMEM] + [ANY] * 19,
        12 * V**3,
        16 * V * V,
        "ladder",
    )

    def reduce_x(keep, send):
        both = keep + swap_core(send)
        total = both[0]
        for k in (1, 2, 3):
            total = total + aux_permute(both[k], lambda zh, x, c, k=k: (zh, x + k, c))
        return total

    with jax.named_scope("reduce"):
        far_sum = aux_permute(reduce_x(far_keep, far_send), lambda zh, x, c: (1 - zh, x, c))
        result = reduce_x(near_keep, near_send) + far_sum
    return result.reshape(ROWS, 1, V)


def solution(mesh):
    in_specs = (P("aux", "pair", None), P("aux", "pair", None))
    out_specs = P("aux", "pair", None)
    return jax.shard_map(
        per_device, mesh=mesh, in_specs=in_specs, out_specs=out_specs, check_vma=False
    )
```

time: 392 us -> 112 us (0.29)
  the two profiles are of different devices: /device:TPU:32 before, /device:TPU:2 now
where the time goes in v3:
time: 112 us; the launch traced here: 111 us
  waiting for transfers between devices  47.7 us (43%)
  starting transfers between devices  40.4 us (36%)
  Pallas kernels  17.7 us (16%)
  local copies, waits for them, and re-layouts  3.74 us (3%)
  other arithmetic  1.54 us (1%)
    ppermute x18, waiting for transfers between devices, aux_permute(): return lax.ppermute(value, 'aux', steps)  34.3 us
    ppermute x18, starting transfers between devices, aux_permute(): return lax.ppermute(value, 'aux', steps)  25.1 us
    pallas_call x1, Pallas kernels, call(): pl.pallas_call(kernel, out_shape=outs, in_specs=in_specs, out_specs=out_s...  17.7 us
    ppermute x11, starting transfers between devices, pair_permute(): return lax.ppermute(value, 'pair', steps)  15.3 us
    ppermute x11, waiting for transfers between devices, pair_permute(): return lax.ppermute(value, 'pair', steps)  13.4 us
  transfers between devices with their start and end apart: 29, of which 15 were waited for; matrix products, arithmetic and copies ran while one was open for 1% of the time, Pallas kernels for 0%

profile of v3, /device:TPU:2, one launch (start us, length us, event | category | flops | bytes accessed | tf_op | source)
XLA Modules:
  0.0 111.3 jit_solution(18305312933783231060)
XLA Ops:
  0.0 0.9 copy.6
  0.9 0.0 copy-start
  1.0 0.1 collective-permute-start
  1.1 1.4 %collective-permute-done = f32[56,896]{1,0:T(8,128)S(1)} collective-permute-done((f32[56,896]{1,0:T(8,128)S(1)}, f32[56,896]{1,0:T(8,128)S(1)}, u32[]{:S(2)}, u32[]{:S(2)}) %collective-permute-start) | collective-permute-done | bytes 200736 | tf_op jit(solution)/shard_map/gather/ppermute | solution.py:34
  2.5 1.6 %collective-permute-start.1 = (f32[112,896]{1,0:T(8,128)S(1)}, f32[112,896]{1,0:T(8,128)}, u32[]{:S(2)}, u32[]{:S(2)}) collective-permute-start(f32[112,896]{1,0:T(8,128)S(1)} %pad_maximum_fusion.1.refs_0_), channel_id=1, source_target_pairs={{0,2},{1,7},{2,4},{3,1},{4,6},{5,3},{6,0},{7,5},{8,10},{9,15},{10,... | collective-permute-start | bytes 1204232 | tf_op jit(solution)/shard_map/gather/ppermute | solution.py:34
  4.1 3.3 %collective-permute-start.5 = (f32[56,896]{1,0:T(8,128)S(1)}, f32[56,896]{1,0:T(8,128)S(1)}, u32[]{:S(2)}, u32[]{:S(2)}) collective-permute-start(f32[56,896]{1,0:T(8,128)S(1)} %bitcast.43), channel_id=1, source_target_pairs={{0,128},{16,144},{32,160},{48,176},{64,192},{80,208},{96,224},{112... | collective-permute-start | bytes 602120 | tf_op jit(solution)/shard_map/gather/ppermute | solution.py:24
  7.4 1.9 %collective-permute-start.4 = (f32[56,896]{1,0:T(8,128)S(1)}, f32[56,896]{1,0:T(8,128)S(1)}, u32[]{:S(2)}, u32[]{:S(2)}) collective-permute-start(f32[56,896]{1,0:T(8,128)S(1)} %bitcast.44), channel_id=1, source_target_pairs={{0,64},{16,80},{32,96},{48,112},{64,0},{80,16},{96,32},{112,48},{1... | collective-permute-start | bytes 602120 | tf_op jit(solution)/shard_map/gather/ppermute | solution.py:24
  9.3 3.0 %collective-permute-start.3 = (f32[56,896]{1,0:T(8,128)S(1)}, f32[56,896]{1,0:T(8,128)S(1)}, u32[]{:S(2)}, u32[]{:S(2)}) collective-permute-start(f32[56,896]{1,0:T(8,128)S(1)} %bitcast.45), channel_id=1, source_target_pairs={{0,48},{16,0},{32,16},{48,32},{64,112},{80,64},{96,80},{112,96},{1... | collective-permute-start | bytes 602120 | tf_op jit(solution)/shard_map/gather/ppermute | solution.py:24
  12.3 0.0 collective-permute-start.2
  12.3 4.6 %collective-permute-done.5 = f32[56,896]{1,0:T(8,128)S(1)} collective-permute-done((f32[56,896]{1,0:T(8,128)S(1)}, f32[56,896]{1,0:T(8,128)S(1)}, u32[]{:S(2)}, u32[]{:S(2)}) %collective-permute-start.5) | collective-permute-done | bytes 200736 | tf_op jit(solution)/shard_map/gather/ppermute | solution.py:24
  16.9 0.1 collective-permute-done.4
  17.0 0.0 collective-permute-done.3.refs_10_
  17.0 2.2 %collective-permute-done.2.refs_9_ = f32[56,896]{1,0:T(8,128)S(1)} collective-permute-done((f32[56,896]{1,0:T(8,128)S(1)}, f32[56,896]{1,0:T(8,128)S(1)}, u32[]{:S(2)}, u32[]{:S(2)}) %collective-permute-start.2) | collective-permute-done | bytes 200736 | tf_op jit(solution)/shard_map/gather/ppermute | solution.py:24
  19.2 0.0 collective-permute-done.1.refs_2_
  19.3 0.1 collective-permute-start.8
  19.4 2.0 %collective-permute-start.7 = (f32[112,896]{1,0:T(8,128)S(1)}, f32[112,896]{1,0:T(8,128)S(1)}, u32[]{:S(2)}, u32[]{:S(2)}) collective-permute-start(f32[112,896]{1,0:T(8,128)S(1)} %constant_dynamic-update-slice_fusion.refs_12_), channel_id=1, source_target_pairs={{0,16},{16,32},{32,48},{48,0},{64,80},{80,96},{96,112},{112,64},{1... | collective-permute-start | bytes 1204232 | tf_op jit(solution)/shard_map/gather/ppermute | solution.py:24
  21.4 4.5 %collective-permute-start.10 = (f32[56,896]{1,0:T(8,128)S(1)}, f32[56,896]{1,0:T(8,128)S(1)}, u32[]{:S(2)}, u32[]{:S(2)}) collective-permute-start(f32[56,896]{1,0:T(8,128)S(1)} %bitcast.50), channel_id=1, source_target_pairs={{0,8},{1,9},{2,10},{3,11},{4,12},{5,13},{6,14},{7,15},{8,0},{9,1},... | collective-permute-start | bytes 602120 | tf_op jit(solution)/shard_map/gather/ppermute | solution.py:34
  25.9 0.2 collective-permute-start.6
  26.0 0.8 collective-permute-start.9
  26.9 8.0 %collective-permute-done.10 = f32[56,896]{1,0:T(8,128)S(1)} collective-permute-done((f32[56,896]{1,0:T(8,128)S(1)}, f32[56,896]{1,0:T(8,128)S(1)}, u32[]{:S(2)}, u32[]{:S(2)}) %collective-permute-start.10) | collective-permute-done | bytes 200736 | tf_op jit(solution)/shard_map/gather/ppermute | solution.py:34
  34.9 2.9 %collective-permute-done.9.refs_15_ = f32[56,896]{1,0:T(8,128)S(1)} collective-permute-done((f32[56,896]{1,0:T(8,128)S(1)}, f32[56,896]{1,0:T(8,128)S(1)}, u32[]{:S(2)}, u32[]{:S(2)}) %collective-permute-start.9) | collective-permute-done | bytes 200736 | tf_op jit(solution)/shard_map/gather/ppermute | solution.py:24
  37.8 0.0 collective-permute-done.8.refs_14_
  37.8 0.1 collective-permute-start.11
  37.9 3.4 %collective-permute-start.15 = (f32[112,896]{1,0:T(8,128)S(1)}, f32[112,896]{1,0:T(8,128)}, u32[]{:S(2)}, u32[]{:S(2)}) collective-permute-start(f32[112,896]{1,0:T(8,128)S(1)} %pad_maximum_fusion), channel_id=1, source_target_pairs={{0,4},{1,5},{2,6},{3,7},{4,0},{5,1},{6,2},{7,3},{8,12},{9,13},{10,... | collective-permute-start | bytes 1204232 | tf_op jit(solution)/shard_map/gather/ppermute | solution.py:34
  41.4 2.3 %collective-permute-start.12 = (f32[112,896]{1,0:T(8,128)S(1)}, f32[112,896]{1,0:T(8,128)}, u32[]{:S(2)}, u32[]{:S(2)}) collective-permute-start(f32[112,896]{1,0:T(8,128)S(1)} %constant_dynamic-update-slice_fusion.2.refs_1_), channel_id=1, source_target_pairs={{0,2},{1,7},{2,4},{3,1},{4,6},{5,3},{6,0},{7,5},{8,10},{9,15},{10,... | collective-permute-start | bytes 1204232 | tf_op jit(solution)/shard_map/gather/ppermute | solution.py:34
  43.7 1.9 %collective-permute-start.19 = (f32[56,896]{1,0:T(8,128)S(1)}, f32[56,896]{1,0:T(8,128)S(1)}, u32[]{:S(2)}, u32[]{:S(2)}) collective-permute-start(f32[56,896]{1,0:T(8,128)S(1)} %collective-permute-done.9.refs_15_), channel_id=1, source_target_pairs={{0,32},{16,48},{32,0},{48,16},{64,96},{80,112},{96,64},{112,80},{1... | collective-permute-start | bytes 602120 | tf_op jit(solution)/shard_map/gather/ppermute | solution.py:24
  45.6 0.9 slice-done
  46.5 0.1 pad_maximum_fusion.2
  46.6 1.1 %collective-permute-start.18 = (f32[112,896]{1,0:T(8,128)S(1)}, f32[112,896]{1,0:T(8,128)S(1)}, u32[]{:S(2)}, u32[]{:S(2)}) collective-permute-start(f32[112,896]{1,0:T(8,128)S(1)} %get-tuple-element.45), channel_id=1, source_target_pairs={{0,48},{16,0},{32,16},{48,32},{64,112},{80,64},{96,80},{112,96},{1... | collective-permute-start | bytes 1204232 | tf_op jit(solution)/shard_map/gather/ppermute | solution.py:24
  47.7 1.0 collective-permute-start.17
  48.7 3.1 %collective-permute-done.15.refs_6_ = f32[112,896]{1,0:T(8,128)} collective-permute-done((f32[112,896]{1,0:T(8,128)S(1)}, f32[112,896]{1,0:T(8,128)}, u32[]{:S(2)}, u32[]{:S(2)}) %collective-permute-start.15) | collective-permute-done | bytes 401440 | tf_op jit(solution)/shard_map/gather/ppermute | solution.py:34
  51.8 4.7 %collective-permute-done.12.refs_3_ = f32[112,896]{1,0:T(8,128)} collective-permute-done((f32[112,896]{1,0:T(8,128)S(1)}, f32[112,896]{1,0:T(8,128)}, u32[]{:S(2)}, u32[]{:S(2)}) %collective-permute-start.12) | collective-permute-done | bytes 401440 | tf_op jit(solution)/shard_map/gather/ppermute | solution.py:34
  56.5 0.0 collective-permute-start.13
  56.5 0.0 collective-permute-done.19.refs_18_
  56.5 0.5 collective-permute-start.14
  57.0 0.1 stack.23.place_ref
  57.1 3.6 %collective-permute-done.18.refs_17_ = f32[112,896]{1,0:T(8,128)S(1)} collective-permute-done((f32[112,896]{1,0:T(8,128)S(1)}, f32[112,896]{1,0:T(8,128)S(1)}, u32[]{:S(2)}, u32[]{:S(2)}) %collective-permute-start.18) | collective-permute-done | bytes 401440 | tf_op jit(solution)/shard_map/gather/ppermute | solution.py:24
  60.7 0.0 collective-permute-done.17.refs_16_
  60.7 0.0 collective-permute-done.16.refs_7_
  60.7 0.0 collective-permute-done.14.refs_5_
  60.7 0.7 copy-done.5
  61.4 17.7 %ladder.1 = (f32[4,56,896]{2,1,0:T(8,128)}, f32[4,56,896]{2,1,0:T(8,128)}, f32[4,56,896]{2,1,0:T(8,128)}, f32[4,56,896]{2,1,0:T(8,128)}) custom-call(s32[5]{0:T(128)S(1)} %stack.23.place_ref, f32[112,896]{1,0:T(8,128)S(1)} %pad_maximum_fusion.1.refs_0_, f32[112,896]{1,0:T(8,128)S(1)} %constant_dynamic-update-slice_fusion.2.refs_1_, ...), custom_call_target="tpu_custom_call" | custom-call | flops 8631877632 | bytes 12845056 | tf_op jit(solution)/shard_map/ladder/pallas_call | solution.py:134
  79.1 0.1 collective-permute-start.24
  79.2 0.5 collective-permute-start.20
  79.7 2.0 %collective-permute-done.24 = f32[4,56,896]{2,1,0:T(8,128)S(1)} collective-permute-done((f32[4,56,896]{2,1,0:T(8,128)}, f32[4,56,896]{2,1,0:T(8,128)S(1)}, u32[]{:S(2)}, u32[]{:S(2)}) %collective-permute-start.24) | collective-permute-done | bytes 802848 | tf_op jit(solution)/shard_map/reduce/ppermute | solution.py:34
  81.7 1.2 %add.47 = f32[4,56,896]{2,1,0:T(8,128)S(1)} add(f32[4,56,896]{2,1,0:T(8,128)} %get-tuple-element.37, f32[4,56,896]{2,1,0:T(8,128)S(1)} %collective-permute-done.24) | non-fusion elementwise | flops 200704 | bytes 2408448 | tf_op jit(solution)/shard_map/reduce/add | solution.py:207
  83.0 0.9 collective-permute-start.25
  83.9 1.4 %collective-permute-start.27 = (f32[56,896]{1,0:T(8,128)S(1)}, f32[56,896]{1,0:T(8,128)S(1)}, u32[]{:S(2)}, u32[]{:S(2)}) collective-permute-start(f32[56,896]{1,0:T(8,128)S(1)} %get-tuple-element.43), channel_id=1, source_target_pairs={{0,6},{1,7},{2,0},{3,1},{4,2},{5,3},{6,4},{7,5},{8,14},{9,15},{10,... | collective-permute-start | bytes 602120 | tf_op jit(solution)/shard_map/reduce/ppermute | solution.py:34
  85.3 1.7 %collective-permute-start.26 = (f32[56,896]{1,0:T(8,128)S(1)}, f32[56,896]{1,0:T(8,128)S(1)}, u32[]{:S(2)}, u32[]{:S(2)}) collective-permute-start(f32[56,896]{1,0:T(8,128)S(1)} %get-tuple-element.44), channel_id=1, source_target_pairs={{0,4},{1,5},{2,6},{3,7},{4,0},{5,1},{6,2},{7,3},{8,12},{9,13},{10,... | collective-permute-start | bytes 602120 | tf_op jit(solution)/shard_map/reduce/ppermute | solution.py:34
  87.0 0.1 add.43
  87.2 1.9 %collective-permute-start.21 = (f32[56,896]{1,0:T(8,128)S(1)}, f32[56,896]{1,0:T(8,128)S(1)}, u32[]{:S(2)}, u32[]{:S(2)}) collective-permute-start(f32[56,896]{1,0:T(8,128)S(1)} %get-tuple-element.39), channel_id=1, source_target_pairs={{0,2},{1,3},{2,4},{3,5},{4,6},{5,7},{6,0},{7,1},{8,10},{9,11},{10,... | collective-permute-start | bytes 602120 | tf_op jit(solution)/shard_map/reduce/ppermute | solution.py:34
  89.1 0.2 collective-permute-start.23
  89.3 1.8 %collective-permute-done.25 = f32[56,896]{1,0:T(8,128)S(1)} collective-permute-done((f32[56,896]{1,0:T(8,128)S(1)}, f32[56,896]{1,0:T(8,128)S(1)}, u32[]{:S(2)}, u32[]{:S(2)}) %collective-permute-start.25) | collective-permute-done | bytes 200736 | tf_op jit(solution)/shard_map/reduce/ppermute | solution.py:34
  91.1 4.0 %collective-permute-start.22 = (f32[56,896]{1,0:T(8,128)S(1)}, f32[56,896]{1,0:T(8,128)S(1)}, u32[]{:S(2)}, u32[]{:S(2)}) collective-permute-start(f32[56,896]{1,0:T(8,128)S(1)} %get-tuple-element.41), channel_id=1, source_target_pairs={{0,4},{1,5},{2,6},{3,7},{4,0},{5,1},{6,2},{7,3},{8,12},{9,13},{10,... | collective-permute-start | bytes 602120 | tf_op jit(solution)/shard_map/reduce/ppermute | solution.py:34
  95.1 0.0 collective-permute-done.27
  95.1 2.1 %collective-permute-done.26 = f32[56,896]{1,0:T(8,128)S(1)} collective-permute-done((f32[56,896]{1,0:T(8,128)S(1)}, f32[56,896]{1,0:T(8,128)S(1)}, u32[]{:S(2)}, u32[]{:S(2)}) %collective-permute-start.26) | collective-permute-done | bytes 200736 | tf_op jit(solution)/shard_map/reduce/ppermute | solution.py:34
  97.2 0.1 fusion.2
  97.3 1.9 %collective-permute-start.28 = (f32[56,896]{1,0:T(8,128)S(1)}, f32[56,896]{1,0:T(8,128)S(1)}, u32[]{:S(2)}, u32[]{:S(2)}) collective-permute-start(f32[56,896]{1,0:T(8,128)S(1)} %fusion.2), channel_id=1, source_target_pairs={{0,8},{1,9},{2,10},{3,11},{4,12},{5,13},{6,14},{7,15},{8,0},{9,1},... | collective-permute-start | bytes 602120 | tf_op jit(solution)/shard_map/reduce/ppermute | solution.py:34
  99.2 0.6 collective-permute-done.21
  99.8 0.0 collective-permute-done.23
  99.8 4.9 %collective-permute-done.22 = f32[56,896]{1,0:T(8,128)S(1)} collective-permute-done((f32[56,896]{1,0:T(8,128)S(1)}, f32[56,896]{1,0:T(8,128)S(1)}, u32[]{:S(2)}, u32[]{:S(2)}) %collective-permute-start.22) | collective-permute-done | bytes 200736 | tf_op jit(solution)/shard_map/reduce/ppermute | solution.py:34
  104.7 5.7 %collective-permute-done.28 = f32[56,896]{1,0:T(8,128)S(1)} collective-permute-done((f32[56,896]{1,0:T(8,128)S(1)}, f32[56,896]{1,0:T(8,128)S(1)}, u32[]{:S(2)}, u32[]{:S(2)}) %collective-permute-start.28) | collective-permute-done | bytes 200736 | tf_op jit(solution)/shard_map/reduce/ppermute | solution.py:34
  110.4 0.1 fusion.7
  110.4 0.9 copy.3
  (26 shorter events, 0.3 us)
Async XLA Ops:
  0.9 3.2 %copy-start = (f32[1,56,896]{2,1,0:T(8,128)S(1)}, f32[1,56,896]{2,1,0:T(8,128)}, u32[]{:S(2)}) copy-start(f32[1,56,896]{2,1,0:T(8,128)} %param.3) | copy-start | bytes 602116
  1.0 1.5 %collective-permute-start = (f32[56,896]{1,0:T(8,128)S(1)}, f32[56,896]{1,0:T(8,128)S(1)}, u32[]{:S(2)}, u32[]{:S(2)}) collective-permute-start(f32[56,896]{1,0:T(8,128)S(1)} %bitcast.48), channel_id=1, source_target_pairs={{0,1},{1,0},{2,3},{3,2},{4,5},{5,4},{6,7},{7,6},{8,9},{9,8},{10,11... | collective-permute-start | bytes 602120 | tf_op jit(solution)/shard_map/gather/ppermute | solution.py:34
  2.5 16.7 %collective-permute-start.1 = (f32[112,896]{1,0:T(8,128)S(1)}, f32[112,896]{1,0:T(8,128)}, u32[]{:S(2)}, u32[]{:S(2)}) collective-permute-start(f32[112,896]{1,0:T(8,128)S(1)} %pad_maximum_fusion.1.refs_0_), channel_id=1, source_target_pairs={{0,2},{1,7},{2,4},{3,1},{4,6},{5,3},{6,0},{7,5},{8,10},{9,15},{10,... | collective-permute-start | bytes 1204232 | tf_op jit(solution)/shard_map/gather/ppermute | solution.py:34
  4.1 12.8 %collective-permute-start.5 = (f32[56,896]{1,0:T(8,128)S(1)}, f32[56,896]{1,0:T(8,128)S(1)}, u32[]{:S(2)}, u32[]{:S(2)}) collective-permute-start(f32[56,896]{1,0:T(8,128)S(1)} %bitcast.43), channel_id=1, source_target_pairs={{0,128},{16,144},{32,160},{48,176},{64,192},{80,208},{96,224},{112... | collective-permute-start | bytes 602120 | tf_op jit(solution)/shard_map/gather/ppermute | solution.py:24
  7.4 9.7 %collective-permute-start.4 = (f32[56,896]{1,0:T(8,128)S(1)}, f32[56,896]{1,0:T(8,128)S(1)}, u32[]{:S(2)}, u32[]{:S(2)}) collective-permute-start(f32[56,896]{1,0:T(8,128)S(1)} %bitcast.44), channel_id=1, source_target_pairs={{0,64},{16,80},{32,96},{48,112},{64,0},{80,16},{96,32},{112,48},{1... | collective-permute-start | bytes 602120 | tf_op jit(solution)/shard_map/gather/ppermute | solution.py:24
  9.3 7.8 %collective-permute-start.3 = (f32[56,896]{1,0:T(8,128)S(1)}, f32[56,896]{1,0:T(8,128)S(1)}, u32[]{:S(2)}, u32[]{:S(2)}) collective-permute-start(f32[56,896]{1,0:T(8,128)S(1)} %bitcast.45), channel_id=1, source_target_pairs={{0,48},{16,0},{32,16},{48,32},{64,112},{80,64},{96,80},{112,96},{1... | collective-permute-start | bytes 602120 | tf_op jit(solution)/shard_map/gather/ppermute | solution.py:24
  12.3 6.9 %collective-permute-start.2 = (f32[56,896]{1,0:T(8,128)S(1)}, f32[56,896]{1,0:T(8,128)S(1)}, u32[]{:S(2)}, u32[]{:S(2)}) collective-permute-start(f32[56,896]{1,0:T(8,128)S(1)} %bitcast.46), channel_id=1, source_target_pairs={{0,16},{16,32},{32,48},{48,0},{64,80},{80,96},{96,112},{112,64},{1... | collective-permute-start | bytes 602120 | tf_op jit(solution)/shard_map/gather/ppermute | solution.py:24
  19.3 18.7 %copy-start.4 = (f32[112,896]{1,0:T(8,128)}, f32[112,896]{1,0:T(8,128)S(1)}, u32[]{:S(2)}) copy-start(f32[112,896]{1,0:T(8,128)S(1)} %constant_dynamic-update-slice_fusion.refs_12_) | copy-start | bytes 1204228
  19.3 18.5 %collective-permute-start.8 = (f32[112,896]{1,0:T(8,128)S(1)}, f32[112,896]{1,0:T(8,128)S(1)}, u32[]{:S(2)}, u32[]{:S(2)}) collective-permute-start(f32[112,896]{1,0:T(8,128)S(1)} %constant_dynamic-update-slice_fusion.refs_12_), channel_id=1, source_target_pairs={{0,48},{16,0},{32,16},{48,32},{64,112},{80,64},{96,80},{112,96},{1... | collective-permute-start | bytes 1204232 | tf_op jit(solution)/shard_map/gather/ppermute | solution.py:24
  19.4 18.4 %collective-permute-start.7 = (f32[112,896]{1,0:T(8,128)S(1)}, f32[112,896]{1,0:T(8,128)S(1)}, u32[]{:S(2)}, u32[]{:S(2)}) collective-permute-start(f32[112,896]{1,0:T(8,128)S(1)} %constant_dynamic-update-slice_fusion.refs_12_), channel_id=1, source_target_pairs={{0,16},{16,32},{32,48},{48,0},{64,80},{80,96},{96,112},{112,64},{1... | collective-permute-start | bytes 1204232 | tf_op jit(solution)/shard_map/gather/ppermute | solution.py:24
  21.4 13.5 %collective-permute-start.10 = (f32[56,896]{1,0:T(8,128)S(1)}, f32[56,896]{1,0:T(8,128)S(1)}, u32[]{:S(2)}, u32[]{:S(2)}) collective-permute-start(f32[56,896]{1,0:T(8,128)S(1)} %bitcast.50), channel_id=1, source_target_pairs={{0,8},{1,9},{2,10},{3,11},{4,12},{5,13},{6,14},{7,15},{8,0},{9,1},... | collective-permute-start | bytes 602120 | tf_op jit(solution)/shard_map/gather/ppermute | solution.py:34
  25.9 9.0 %collective-permute-start.6 = (f32[56,896]{1,0:T(8,128)S(1)}, f32[56,896]{1,0:T(8,128)S(1)}, u32[]{:S(2)}, u32[]{:S(2)}) collective-permute-start(f32[56,896]{1,0:T(8,128)S(1)} %collective-permute-done.2.refs_9_), channel_id=1, source_target_pairs={{0,16},{16,32},{32,48},{48,0},{64,80},{80,96},{96,112},{112,64},{1... | collective-permute-start | bytes 602120 | tf_op jit(solution)/shard_map/gather/ppermute | solution.py:24
  26.0 11.7 %collective-permute-start.9 = (f32[56,896]{1,0:T(8,128)S(1)}, f32[56,896]{1,0:T(8,128)S(1)}, u32[]{:S(2)}, u32[]{:S(2)}) collective-permute-start(f32[56,896]{1,0:T(8,128)S(1)} %collective-permute-done.5), channel_id=1, source_target_pairs={{0,64},{16,80},{32,96},{48,112},{64,0},{80,16},{96,32},{112,48},{1... | collective-permute-start | bytes 602120 | tf_op jit(solution)/shard_map/gather/ppermute | solution.py:24
  37.8 7.8 %copy-start.3 = (f32[112,896]{1,0:T(8,128)}, f32[112,896]{1,0:T(8,128)S(1)}, u32[]{:S(2)}) copy-start(f32[112,896]{1,0:T(8,128)S(1)} %collective-permute-done.8.refs_14_) | copy-start | bytes 1204228
  37.8 7.8 %copy-start.2 = (f32[112,896]{1,0:T(8,128)}, f32[112,896]{1,0:T(8,128)S(1)}, u32[]{:S(2)}) copy-start(f32[112,896]{1,0:T(8,128)S(1)} %collective-permute-done.7.refs_13_) | copy-start | bytes 1204228
  37.8 3.6 %collective-permute-start.11 = (f32[56,896]{1,0:T(8,128)S(1)}, f32[56,896]{1,0:T(8,128)S(1)}, u32[]{:S(2)}, u32[]{:S(2)}) collective-permute-start(f32[56,896]{1,0:T(8,128)S(1)} %collective-permute-done.10), channel_id=1, source_target_pairs={{0,1},{1,0},{2,3},{3,2},{4,5},{5,4},{6,7},{7,6},{8,9},{9,8},{10,11... | collective-permute-start | bytes 602120 | tf_op jit(solution)/shard_map/gather/ppermute | solution.py:34
  37.9 13.8 %collective-permute-start.15 = (f32[112,896]{1,0:T(8,128)S(1)}, f32[112,896]{1,0:T(8,128)}, u32[]{:S(2)}, u32[]{:S(2)}) collective-permute-start(f32[112,896]{1,0:T(8,128)S(1)} %pad_maximum_fusion), channel_id=1, source_target_pairs={{0,4},{1,5},{2,6},{3,7},{4,0},{5,1},{6,2},{7,3},{8,12},{9,13},{10,... | collective-permute-start | bytes 1204232 | tf_op jit(solution)/shard_map/gather/ppermute | solution.py:34
  41.4 15.1 %collective-permute-start.12 = (f32[112,896]{1,0:T(8,128)S(1)}, f32[112,896]{1,0:T(8,128)}, u32[]{:S(2)}, u32[]{:S(2)}) collective-permute-start(f32[112,896]{1,0:T(8,128)S(1)} %constant_dynamic-update-slice_fusion.2.refs_1_), channel_id=1, source_target_pairs={{0,2},{1,7},{2,4},{3,1},{4,6},{5,3},{6,0},{7,5},{8,10},{9,15},{10,... | collective-permute-start | bytes 1204232 | tf_op jit(solution)/shard_map/gather/ppermute | solution.py:34
  43.7 12.8 %collective-permute-start.19 = (f32[56,896]{1,0:T(8,128)S(1)}, f32[56,896]{1,0:T(8,128)S(1)}, u32[]{:S(2)}, u32[]{:S(2)}) collective-permute-start(f32[56,896]{1,0:T(8,128)S(1)} %collective-permute-done.9.refs_15_), channel_id=1, source_target_pairs={{0,32},{16,48},{32,0},{48,16},{64,96},{80,112},{96,64},{112,80},{1... | collective-permute-start | bytes 602120 | tf_op jit(solution)/shard_map/gather/ppermute | solution.py:24
  45.6 0.9 slice-start
  46.6 14.1 %collective-permute-start.18 = (f32[112,896]{1,0:T(8,128)S(1)}, f32[112,896]{1,0:T(8,128)S(1)}, u32[]{:S(2)}, u32[]{:S(2)}) collective-permute-start(f32[112,896]{1,0:T(8,128)S(1)} %get-tuple-element.45), channel_id=1, source_target_pairs={{0,48},{16,0},{32,16},{48,32},{64,112},{80,64},{96,80},{112,96},{1... | collective-permute-start | bytes 1204232 | tf_op jit(solution)/shard_map/gather/ppermute | solution.py:24
  47.7 12.9 %collective-permute-start.17 = (f32[112,896]{1,0:T(8,128)S(1)}, f32[112,896]{1,0:T(8,128)}, u32[]{:S(2)}, u32[]{:S(2)}) collective-permute-start(f32[112,896]{1,0:T(8,128)S(1)} %get-tuple-element.46), channel_id=1, source_target_pairs={{0,16},{16,32},{32,48},{48,0},{64,80},{80,96},{96,112},{112,64},{1... | collective-permute-start | bytes 1204232 | tf_op jit(solution)/shard_map/gather/ppermute | solution.py:24
  51.8 8.9 %collective-permute-start.16 = (f32[112,896]{1,0:T(8,128)}, f32[112,896]{1,0:T(8,128)}, u32[]{:S(2)}, u32[]{:S(2)}) collective-permute-start(f32[112,896]{1,0:T(8,128)} %collective-permute-done.15.refs_6_), channel_id=1, source_target_pairs={{0,1},{1,0},{2,3},{3,2},{4,5},{5,4},{6,7},{7,6},{8,9},{9,8},{10,11... | collective-permute-start | bytes 1204232 | tf_op jit(solution)/shard_map/gather/ppermute | solution.py:34
  56.5 4.2 %collective-permute-start.13 = (f32[112,896]{1,0:T(8,128)}, f32[112,896]{1,0:T(8,128)}, u32[]{:S(2)}, u32[]{:S(2)}) collective-permute-start(f32[112,896]{1,0:T(8,128)} %collective-permute-done.1.refs_2_), channel_id=1, source_target_pairs={{0,1},{1,0},{2,3},{3,2},{4,5},{5,4},{6,7},{7,6},{8,9},{9,8},{10,11... | collective-permute-start | bytes 1204232 | tf_op jit(solution)/shard_map/gather/ppermute | solution.py:34
  56.5 4.2 %collective-permute-start.14 = (f32[112,896]{1,0:T(8,128)}, f32[112,896]{1,0:T(8,128)}, u32[]{:S(2)}, u32[]{:S(2)}) collective-permute-start(f32[112,896]{1,0:T(8,128)} %collective-permute-done.12.refs_3_), channel_id=1, source_target_pairs={{0,1},{1,0},{2,3},{3,2},{4,5},{5,4},{6,7},{7,6},{8,9},{9,8},{10,11... | collective-permute-start | bytes 1204232 | tf_op jit(solution)/shard_map/gather/ppermute | solution.py:34
  60.7 0.8 copy-start.5
  79.1 2.6 %collective-permute-start.24 = (f32[4,56,896]{2,1,0:T(8,128)}, f32[4,56,896]{2,1,0:T(8,128)S(1)}, u32[]{:S(2)}, u32[]{:S(2)}) collective-permute-start(f32[4,56,896]{2,1,0:T(8,128)} %get-tuple-element.38), channel_id=1, source_target_pairs={{0,1},{1,0},{2,3},{3,2},{4,5},{5,4},{6,7},{7,6},{8,9},{9,8},{10,11... | collective-permute-start | bytes 2408456 | tf_op jit(solution)/shard_map/reduce/ppermute | solution.py:34
  79.2 7.8 %collective-permute-start.20 = (f32[4,56,896]{2,1,0:T(8,128)}, f32[4,56,896]{2,1,0:T(8,128)S(1)}, u32[]{:S(2)}, u32[]{:S(2)}) collective-permute-start(f32[4,56,896]{2,1,0:T(8,128)} %get-tuple-element.36), channel_id=1, source_target_pairs={{0,1},{1,0},{2,3},{3,2},{4,5},{5,4},{6,7},{7,6},{8,9},{9,8},{10,11... | collective-permute-start | bytes 2408456 | tf_op jit(solution)/shard_map/reduce/ppermute | solution.py:34
  82.9 4.1 %copy-start.1 = (f32[4,56,896]{2,1,0:T(8,128)S(1)}, f32[4,56,896]{2,1,0:T(8,128)}, u32[]{:S(2)}) copy-start(f32[4,56,896]{2,1,0:T(8,128)} %get-tuple-element.35) | copy-start | bytes 2408452
  83.0 8.1 %collective-permute-start.25 = (f32[56,896]{1,0:T(8,128)S(1)}, f32[56,896]{1,0:T(8,128)S(1)}, u32[]{:S(2)}, u32[]{:S(2)}) collective-permute-start(f32[56,896]{1,0:T(8,128)S(1)} %get-tuple-element.42), channel_id=1, source_target_pairs={{0,2},{1,3},{2,4},{3,5},{4,6},{5,7},{6,0},{7,1},{8,10},{9,11},{10,... | collective-permute-start | bytes 602120 | tf_op jit(solution)/shard_map/reduce/ppermute | solution.py:34
  83.9 11.2 %collective-permute-start.27 = (f32[56,896]{1,0:T(8,128)S(1)}, f32[56,896]{1,0:T(8,128)S(1)}, u32[]{:S(2)}, u32[]{:S(2)}) collective-permute-start(f32[56,896]{1,0:T(8,128)S(1)} %get-tuple-element.43), channel_id=1, source_target_pairs={{0,6},{1,7},{2,0},{3,1},{4,2},{5,3},{6,4},{7,5},{8,14},{9,15},{10,... | collective-permute-start | bytes 602120 | tf_op jit(solution)/shard_map/reduce/ppermute | solution.py:34
  85.3 11.9 %collective-permute-start.26 = (f32[56,896]{1,0:T(8,128)S(1)}, f32[56,896]{1,0:T(8,128)S(1)}, u32[]{:S(2)}, u32[]{:S(2)}) collective-permute-start(f32[56,896]{1,0:T(8,128)S(1)} %get-tuple-element.44), channel_id=1, source_target_pairs={{0,4},{1,5},{2,6},{3,7},{4,0},{5,1},{6,2},{7,3},{8,12},{9,13},{10,... | collective-permute-start | bytes 602120 | tf_op jit(solution)/shard_map/reduce/ppermute | solution.py:34
  87.2 12.6 %collective-permute-start.21 = (f32[56,896]{1,0:T(8,128)S(1)}, f32[56,896]{1,0:T(8,128)S(1)}, u32[]{:S(2)}, u32[]{:S(2)}) collective-permute-start(f32[56,896]{1,0:T(8,128)S(1)} %get-tuple-element.39), channel_id=1, source_target_pairs={{0,2},{1,3},{2,4},{3,5},{4,6},{5,7},{6,0},{7,1},{8,10},{9,11},{10,... | collective-permute-start | bytes 602120 | tf_op jit(solution)/shard_map/reduce/ppermute | solution.py:34
  89.1 10.7 %collective-permute-start.23 = (f32[56,896]{1,0:T(8,128)S(1)}, f32[56,896]{1,0:T(8,128)S(1)}, u32[]{:S(2)}, u32[]{:S(2)}) collective-permute-start(f32[56,896]{1,0:T(8,128)S(1)} %get-tuple-element.40), channel_id=1, source_target_pairs={{0,6},{1,7},{2,0},{3,1},{4,2},{5,3},{6,4},{7,5},{8,14},{9,15},{10,... | collective-permute-start | bytes 602120 | tf_op jit(solution)/shard_map/reduce/ppermute | solution.py:34
  91.1 13.6 %collective-permute-start.22 = (f32[56,896]{1,0:T(8,128)S(1)}, f32[56,896]{1,0:T(8,128)S(1)}, u32[]{:S(2)}, u32[]{:S(2)}) collective-permute-start(f32[56,896]{1,0:T(8,128)S(1)} %get-tuple-element.41), channel_id=1, source_target_pairs={{0,4},{1,5},{2,6},{3,7},{4,0},{5,1},{6,2},{7,3},{8,12},{9,13},{10,... | collective-permute-start | bytes 602120 | tf_op jit(solution)/shard_map/reduce/ppermute | solution.py:34
  97.3 13.1 %collective-permute-start.28 = (f32[56,896]{1,0:T(8,128)S(1)}, f32[56,896]{1,0:T(8,128)S(1)}, u32[]{:S(2)}, u32[]{:S(2)}) collective-permute-start(f32[56,896]{1,0:T(8,128)S(1)} %fusion.2), channel_id=1, source_target_pairs={{0,8},{1,9},{2,10},{3,11},{4,12},{5,13},{6,14},{7,15},{8,0},{9,1},... | collective-permute-start | bytes 602120 | tf_op jit(solution)/shard_map/reduce/ppermute | solution.py:34

commit v4 on v3

--- a/solution.py
+++ b/solution.py
@@ -168,10 +168,11 @@
         own = pack(amp, swap_core(amp))
         fit_0 = up(fit), down(fit)
         beside = beside_x(own)
-        amp_late, beside, fit_0, near, two = tie((amp, beside, fit_0, near, two))
-
+        amp_late, near, two = tie((amp, near, two))
         far = aux_permute(amp_late, lambda zh, x, c: (1 - zh, x, c))
         three = pair_permute(two, lambda zl, y: (zl ^ 1, y))
+        beside, fit_0, near, two = tie((beside, fit_0, near, two))
+
         both = pack(near, two)
         below, above = up(both), down(both)
         low = up(fit_0[0])

time: 112 us -> 110 us (0.982)
  the two profiles are of different devices: /device:TPU:2 before, /device:TPU:32 now
where the time goes in v4:
time: 110 us; the launch traced here: 109 us
  waiting for transfers between devices  54.8 us (50%)
  starting transfers between devices  32.2 us (29%)
  Pallas kernels  17.7 us (16%)
  local copies, waits for them, and re-layouts  3 us (3%)
  other arithmetic  1.54 us (1%)
    ppermute x18, waiting for transfers between devices, aux_permute(): return lax.ppermute(value, 'aux', steps)  45.2 us
    pallas_call x1, Pallas kernels, call(): pl.pallas_call(kernel, out_shape=outs, in_specs=in_specs, out_specs=out_s...  17.7 us
    ppermute x18, starting transfers between devices, aux_permute(): return lax.ppermute(value, 'aux', steps)  17.3 us
    ppermute x11, starting transfers between devices, pair_permute(): return lax.ppermute(value, 'pair', steps)  14.9 us
    ppermute x11, waiting for transfers between devices, pair_permute(): return lax.ppermute(value, 'pair', steps)  9.58 us
  transfers between devices with their start and end apart: 29, of which 18 were waited for; matrix products, arithmetic and copies ran while one was open for 2% of the time, Pallas kernels for 0%

profile of v4, /device:TPU:32, one launch (start us, length us, event | category | flops | bytes accessed | tf_op | source)
XLA Modules:
  0.0 109.3 jit_solution(10722354244748352384)
XLA Ops:
  0.0 0.9 copy.6
  0.9 0.0 copy-start
  1.0 0.1 collective-permute-start
  1.1 1.4 %collective-permute-done = f32[56,896]{1,0:T(8,128)S(1)} collective-permute-done((f32[56,896]{1,0:T(8,128)S(1)}, f32[56,896]{1,0:T(8,128)S(1)}, u32[]{:S(2)}, u32[]{:S(2)}) %collective-permute-start) | collective-permute-done | bytes 200736 | tf_op jit(solution)/shard_map/gather/ppermute | solution.py:34
  2.5 1.6 %collective-permute-start.1 = (f32[112,896]{1,0:T(8,128)S(1)}, f32[112,896]{1,0:T(8,128)}, u32[]{:S(2)}, u32[]{:S(2)}) collective-permute-start(f32[112,896]{1,0:T(8,128)S(1)} %pad_maximum_fusion.1.refs_0_), channel_id=1, source_target_pairs={{0,2},{1,7},{2,4},{3,1},{4,6},{5,3},{6,0},{7,5},{8,10},{9,15},{10,... | collective-permute-start | bytes 1204232 | tf_op jit(solution)/shard_map/gather/ppermute | solution.py:34
  4.1 3.3 %collective-permute-start.5 = (f32[56,896]{1,0:T(8,128)S(1)}, f32[56,896]{1,0:T(8,128)S(1)}, u32[]{:S(2)}, u32[]{:S(2)}) collective-permute-start(f32[56,896]{1,0:T(8,128)S(1)} %bitcast.43), channel_id=1, source_target_pairs={{0,128},{16,144},{32,160},{48,176},{64,192},{80,208},{96,224},{112... | collective-permute-start | bytes 602120 | tf_op jit(solution)/shard_map/gather/ppermute | solution.py:24
  7.4 0.1 collective-permute-start.4
  7.5 3.0 %collective-permute-start.3 = (f32[56,896]{1,0:T(8,128)S(1)}, f32[56,896]{1,0:T(8,128)S(1)}, u32[]{:S(2)}, u32[]{:S(2)}) collective-permute-start(f32[56,896]{1,0:T(8,128)S(1)} %bitcast.45), channel_id=1, source_target_pairs={{0,48},{16,0},{32,16},{48,32},{64,112},{80,64},{96,80},{112,96},{1... | collective-permute-start | bytes 602120 | tf_op jit(solution)/shard_map/gather/ppermute | solution.py:24
  10.5 6.1 %collective-permute-done.5 = f32[56,896]{1,0:T(8,128)S(1)} collective-permute-done((f32[56,896]{1,0:T(8,128)S(1)}, f32[56,896]{1,0:T(8,128)S(1)}, u32[]{:S(2)}, u32[]{:S(2)}) %collective-permute-start.5) | collective-permute-done | bytes 200736 | tf_op jit(solution)/shard_map/gather/ppermute | solution.py:24
  16.6 0.9 collective-permute-done.4
  17.5 0.0 collective-permute-done.3.refs_10_
  17.5 1.6 %collective-permute-done.2.refs_9_ = f32[56,896]{1,0:T(8,128)S(1)} collective-permute-done((f32[56,896]{1,0:T(8,128)S(1)}, f32[56,896]{1,0:T(8,128)S(1)}, u32[]{:S(2)}, u32[]{:S(2)}) %collective-permute-start.2) | collective-permute-done | bytes 200736 | tf_op jit(solution)/shard_map/gather/ppermute | solution.py:24
  19.1 0.0 collective-permute-done.1.refs_2_
  19.1 1.5 %collective-permute-start.8 = (f32[112,896]{1,0:T(8,128)S(1)}, f32[112,896]{1,0:T(8,128)S(1)}, u32[]{:S(2)}, u32[]{:S(2)}) collective-permute-start(f32[112,896]{1,0:T(8,128)S(1)} %constant_dynamic-update-slice_fusion.refs_12_), channel_id=1, source_target_pairs={{0,48},{16,0},{32,16},{48,32},{64,112},{80,64},{96,80},{112,96},{1... | collective-permute-start | bytes 1204232 | tf_op jit(solution)/shard_map/gather/ppermute | solution.py:24
  20.7 0.6 collective-permute-start.7
  21.2 1.7 %collective-permute-start.9 = (f32[56,896]{1,0:T(8,128)S(1)}, f32[56,896]{1,0:T(8,128)S(1)}, u32[]{:S(2)}, u32[]{:S(2)}) collective-permute-start(f32[56,896]{1,0:T(8,128)S(1)} %collective-permute-done.5), channel_id=1, source_target_pairs={{0,64},{16,80},{32,96},{48,112},{64,0},{80,16},{96,32},{112,48},{1... | collective-permute-start | bytes 602120 | tf_op jit(solution)/shard_map/gather/ppermute | solution.py:24
  23.0 4.5 %collective-permute-start.10 = (f32[56,896]{1,0:T(8,128)S(1)}, f32[56,896]{1,0:T(8,128)S(1)}, u32[]{:S(2)}, u32[]{:S(2)}) collective-permute-start(f32[56,896]{1,0:T(8,128)S(1)} %bitcast.50), channel_id=1, source_target_pairs={{0,8},{1,9},{2,10},{3,11},{4,12},{5,13},{6,14},{7,15},{8,0},{9,1},... | collective-permute-start | bytes 602120 | tf_op jit(solution)/shard_map/gather/ppermute | solution.py:34
  27.5 0.6 collective-permute-start.6
  28.1 12.7 %collective-permute-done.10 = f32[56,896]{1,0:T(8,128)S(1)} collective-permute-done((f32[56,896]{1,0:T(8,128)S(1)}, f32[56,896]{1,0:T(8,128)S(1)}, u32[]{:S(2)}, u32[]{:S(2)}) %collective-permute-start.10) | collective-permute-done | bytes 200736 | tf_op jit(solution)/shard_map/gather/ppermute | solution.py:34
  40.8 0.0 collective-permute-done.9.refs_15_
  40.8 0.0 collective-permute-done.6.refs_11_
  40.8 0.1 collective-permute-start.11
  41.0 0.6 collective-permute-start.15
  41.6 0.8 collective-permute-done.11
  42.4 0.3 collective-permute-start.12
  42.7 1.9 %collective-permute-start.19 = (f32[56,896]{1,0:T(8,128)S(1)}, f32[56,896]{1,0:T(8,128)S(1)}, u32[]{:S(2)}, u32[]{:S(2)}) collective-permute-start(f32[56,896]{1,0:T(8,128)S(1)} %collective-permute-done.9.refs_15_), channel_id=1, source_target_pairs={{0,32},{16,48},{32,0},{48,16},{64,96},{80,112},{96,64},{112,80},{1... | collective-permute-start | bytes 602120 | tf_op jit(solution)/shard_map/gather/ppermute | solution.py:24
  44.6 0.9 slice-done
  45.5 0.1 pad_maximum_fusion.2
  45.6 1.1 %collective-permute-start.18 = (f32[112,896]{1,0:T(8,128)S(1)}, f32[112,896]{1,0:T(8,128)S(1)}, u32[]{:S(2)}, u32[]{:S(2)}) collective-permute-start(f32[112,896]{1,0:T(8,128)S(1)} %get-tuple-element.49), channel_id=1, source_target_pairs={{0,48},{16,0},{32,16},{48,32},{64,112},{80,64},{96,80},{112,96},{1... | collective-permute-start | bytes 1204232 | tf_op jit(solution)/shard_map/gather/ppermute | solution.py:24
  46.7 1.0 collective-permute-start.17
  47.7 6.8 %collective-permute-done.15.refs_6_ = f32[112,896]{1,0:T(8,128)} collective-permute-done((f32[112,896]{1,0:T(8,128)S(1)}, f32[112,896]{1,0:T(8,128)}, u32[]{:S(2)}, u32[]{:S(2)}) %collective-permute-start.15) | collective-permute-done | bytes 401440 | tf_op jit(solution)/shard_map/gather/ppermute | solution.py:34
  54.5 0.0 collective-permute-start.16
  54.5 4.2 %collective-permute-done.12.refs_3_ = f32[112,896]{1,0:T(8,128)} collective-permute-done((f32[112,896]{1,0:T(8,128)S(1)}, f32[112,896]{1,0:T(8,128)}, u32[]{:S(2)}, u32[]{:S(2)}) %collective-permute-start.12) | collective-permute-done | bytes 401440 | tf_op jit(solution)/shard_map/gather/ppermute | solution.py:34
  58.7 0.0 collective-permute-start.13
  58.7 0.0 collective-permute-done.19.refs_18_
  58.7 0.5 collective-permute-start.14
  59.2 0.1 stack.23.place_ref
  59.3 1.0 collective-permute-done.18.refs_17_
  60.3 0.5 collective-permute-done.13.refs_4_
  60.7 0.6 collective-permute-done.14.refs_5_
  61.3 17.7 %ladder.1 = (f32[4,56,896]{2,1,0:T(8,128)}, f32[4,56,896]{2,1,0:T(8,128)}, f32[4,56,896]{2,1,0:T(8,128)}, f32[4,56,896]{2,1,0:T(8,128)}) custom-call(s32[5]{0:T(128)S(1)} %stack.23.place_ref, f32[112,896]{1,0:T(8,128)S(1)} %pad_maximum_fusion.1.refs_0_, f32[112,896]{1,0:T(8,128)S(1)} %constant_dynamic-update-slice_fusion.2.refs_1_, ...), custom_call_target="tpu_custom_call" | custom-call | flops 8631877632 | bytes 12845056 | tf_op jit(solution)/shard_map/ladder/pallas_call | solution.py:134
  79.0 0.2 collective-permute-start.24
  79.2 0.4 collective-permute-start.20
  79.6 2.0 %collective-permute-done.24 = f32[4,56,896]{2,1,0:T(8,128)S(1)} collective-permute-done((f32[4,56,896]{2,1,0:T(8,128)}, f32[4,56,896]{2,1,0:T(8,128)S(1)}, u32[]{:S(2)}, u32[]{:S(2)}) %collective-permute-start.24) | collective-permute-done | bytes 802848 | tf_op jit(solution)/shard_map/reduce/ppermute | solution.py:34
  81.6 1.2 %add.47 = f32[4,56,896]{2,1,0:T(8,128)S(1)} add(f32[4,56,896]{2,1,0:T(8,128)} %get-tuple-element.41, f32[4,56,896]{2,1,0:T(8,128)S(1)} %collective-permute-done.24) | non-fusion elementwise | flops 200704 | bytes 2408448 | tf_op jit(solution)/shard_map/reduce/add | solution.py:208
  82.9 1.4 %collective-permute-start.25 = (f32[56,896]{1,0:T(8,128)S(1)}, f32[56,896]{1,0:T(8,128)S(1)}, u32[]{:S(2)}, u32[]{:S(2)}) collective-permute-start(f32[56,896]{1,0:T(8,128)S(1)} %get-tuple-element.46), channel_id=1, source_target_pairs={{0,2},{1,3},{2,4},{3,5},{4,6},{5,7},{6,0},{7,1},{8,10},{9,11},{10,... | collective-permute-start | bytes 602120 | tf_op jit(solution)/shard_map/reduce/ppermute | solution.py:34
  84.3 2.1 %collective-permute-start.27 = (f32[56,896]{1,0:T(8,128)S(1)}, f32[56,896]{1,0:T(8,128)S(1)}, u32[]{:S(2)}, u32[]{:S(2)}) collective-permute-start(f32[56,896]{1,0:T(8,128)S(1)} %get-tuple-element.47), channel_id=1, source_target_pairs={{0,6},{1,7},{2,0},{3,1},{4,2},{5,3},{6,4},{7,5},{8,14},{9,15},{10,... | collective-permute-start | bytes 602120 | tf_op jit(solution)/shard_map/reduce/ppermute | solution.py:34
  86.4 0.6 collective-permute-start.26
  87.0 0.0 collective-permute-done.20
  87.0 0.1 add.43
  87.1 1.1 %collective-permute-start.21 = (f32[56,896]{1,0:T(8,128)S(1)}, f32[56,896]{1,0:T(8,128)S(1)}, u32[]{:S(2)}, u32[]{:S(2)}) collective-permute-start(f32[56,896]{1,0:T(8,128)S(1)} %get-tuple-element.43), channel_id=1, source_target_pairs={{0,2},{1,3},{2,4},{3,5},{4,6},{5,7},{6,0},{7,1},{8,10},{9,11},{10,... | collective-permute-start | bytes 602120 | tf_op jit(solution)/shard_map/reduce/ppermute | solution.py:34
  88.3 2.2 %collective-permute-start.23 = (f32[56,896]{1,0:T(8,128)S(1)}, f32[56,896]{1,0:T(8,128)S(1)}, u32[]{:S(2)}, u32[]{:S(2)}) collective-permute-start(f32[56,896]{1,0:T(8,128)S(1)} %get-tuple-element.44), channel_id=1, source_target_pairs={{0,6},{1,7},{2,0},{3,1},{4,2},{5,3},{6,4},{7,5},{8,14},{9,15},{10,... | collective-permute-start | bytes 602120 | tf_op jit(solution)/shard_map/reduce/ppermute | solution.py:34
  90.5 5.8 %collective-permute-done.25 = f32[56,896]{1,0:T(8,128)S(1)} collective-permute-done((f32[56,896]{1,0:T(8,128)S(1)}, f32[56,896]{1,0:T(8,128)S(1)}, u32[]{:S(2)}, u32[]{:S(2)}) %collective-permute-start.25) | collective-permute-done | bytes 200736 | tf_op jit(solution)/shard_map/reduce/ppermute | solution.py:34
  96.2 0.0 collective-permute-start.22
  96.2 0.0 collective-permute-done.27
  96.2 0.5 collective-permute-done.26
  96.8 0.1 fusion.2
  96.8 1.6 %collective-permute-start.28 = (f32[56,896]{1,0:T(8,128)S(1)}, f32[56,896]{1,0:T(8,128)S(1)}, u32[]{:S(2)}, u32[]{:S(2)}) collective-permute-start(f32[56,896]{1,0:T(8,128)S(1)} %fusion.2), channel_id=1, source_target_pairs={{0,8},{1,9},{2,10},{3,11},{4,12},{5,13},{6,14},{7,15},{8,0},{9,1},... | collective-permute-start | bytes 602120 | tf_op jit(solution)/shard_map/reduce/ppermute | solution.py:34
  98.5 2.1 %collective-permute-done.21 = f32[56,896]{1,0:T(8,128)S(1)} collective-permute-done((f32[56,896]{1,0:T(8,128)S(1)}, f32[56,896]{1,0:T(8,128)S(1)}, u32[]{:S(2)}, u32[]{:S(2)}) %collective-permute-start.21) | collective-permute-done | bytes 200736 | tf_op jit(solution)/shard_map/reduce/ppermute | solution.py:34
  100.5 3.1 %collective-permute-done.23 = f32[56,896]{1,0:T(8,128)S(1)} collective-permute-done((f32[56,896]{1,0:T(8,128)S(1)}, f32[56,896]{1,0:T(8,128)S(1)}, u32[]{:S(2)}, u32[]{:S(2)}) %collective-permute-start.23) | collective-permute-done | bytes 200736 | tf_op jit(solution)/shard_map/reduce/ppermute | solution.py:34
  103.6 1.0 collective-permute-done.22
  104.6 3.8 %collective-permute-done.28 = f32[56,896]{1,0:T(8,128)S(1)} collective-permute-done((f32[56,896]{1,0:T(8,128)S(1)}, f32[56,896]{1,0:T(8,128)S(1)}, u32[]{:S(2)}, u32[]{:S(2)}) %collective-permute-start.28) | collective-permute-done | bytes 200736 | tf_op jit(solution)/shard_map/reduce/ppermute | solution.py:34
  108.4 0.1 fusion.7
  108.4 0.9 copy.3
  (26 shorter events, 0.3 us)
Async XLA Ops:
  0.9 3.2 %copy-start = (f32[1,56,896]{2,1,0:T(8,128)S(1)}, f32[1,56,896]{2,1,0:T(8,128)}, u32[]{:S(2)}) copy-start(f32[1,56,896]{2,1,0:T(8,128)} %param.3) | copy-start | bytes 602116
  1.0 1.5 %collective-permute-start = (f32[56,896]{1,0:T(8,128)S(1)}, f32[56,896]{1,0:T(8,128)S(1)}, u32[]{:S(2)}, u32[]{:S(2)}) collective-permute-start(f32[56,896]{1,0:T(8,128)S(1)} %bitcast.48), channel_id=1, source_target_pairs={{0,1},{1,0},{2,3},{3,2},{4,5},{5,4},{6,7},{7,6},{8,9},{9,8},{10,11... | collective-permute-start | bytes 602120 | tf_op jit(solution)/shard_map/gather/ppermute | solution.py:34
  2.5 16.5 %collective-permute-start.1 = (f32[112,896]{1,0:T(8,128)S(1)}, f32[112,896]{1,0:T(8,128)}, u32[]{:S(2)}, u32[]{:S(2)}) collective-permute-start(f32[112,896]{1,0:T(8,128)S(1)} %pad_maximum_fusion.1.refs_0_), channel_id=1, source_target_pairs={{0,2},{1,7},{2,4},{3,1},{4,6},{5,3},{6,0},{7,5},{8,10},{9,15},{10,... | collective-permute-start | bytes 1204232 | tf_op jit(solution)/shard_map/gather/ppermute | solution.py:34
  4.1 12.5 %collective-permute-start.5 = (f32[56,896]{1,0:T(8,128)S(1)}, f32[56,896]{1,0:T(8,128)S(1)}, u32[]{:S(2)}, u32[]{:S(2)}) collective-permute-start(f32[56,896]{1,0:T(8,128)S(1)} %bitcast.43), channel_id=1, source_target_pairs={{0,128},{16,144},{32,160},{48,176},{64,192},{80,208},{96,224},{112... | collective-permute-start | bytes 602120 | tf_op jit(solution)/shard_map/gather/ppermute | solution.py:24
  7.4 10.1 %collective-permute-start.4 = (f32[56,896]{1,0:T(8,128)S(1)}, f32[56,896]{1,0:T(8,128)S(1)}, u32[]{:S(2)}, u32[]{:S(2)}) collective-permute-start(f32[56,896]{1,0:T(8,128)S(1)} %bitcast.44), channel_id=1, source_target_pairs={{0,64},{16,80},{32,96},{48,112},{64,0},{80,16},{96,32},{112,48},{1... | collective-permute-start | bytes 602120 | tf_op jit(solution)/shard_map/gather/ppermute | solution.py:24
  7.5 10.0 %collective-permute-start.3 = (f32[56,896]{1,0:T(8,128)S(1)}, f32[56,896]{1,0:T(8,128)S(1)}, u32[]{:S(2)}, u32[]{:S(2)}) collective-permute-start(f32[56,896]{1,0:T(8,128)S(1)} %bitcast.45), channel_id=1, source_target_pairs={{0,48},{16,0},{32,16},{48,32},{64,112},{80,64},{96,80},{112,96},{1... | collective-permute-start | bytes 602120 | tf_op jit(solution)/shard_map/gather/ppermute | solution.py:24
  10.5 8.6 %collective-permute-start.2 = (f32[56,896]{1,0:T(8,128)S(1)}, f32[56,896]{1,0:T(8,128)S(1)}, u32[]{:S(2)}, u32[]{:S(2)}) collective-permute-start(f32[56,896]{1,0:T(8,128)S(1)} %bitcast.46), channel_id=1, source_target_pairs={{0,16},{16,32},{32,48},{48,0},{64,80},{80,96},{96,112},{112,64},{1... | collective-permute-start | bytes 602120 | tf_op jit(solution)/shard_map/gather/ppermute | solution.py:24
  19.1 21.9 %copy-start.4 = (f32[112,896]{1,0:T(8,128)}, f32[112,896]{1,0:T(8,128)S(1)}, u32[]{:S(2)}) copy-start(f32[112,896]{1,0:T(8,128)S(1)} %constant_dynamic-update-slice_fusion.refs_12_) | copy-start | bytes 1204228
  19.1 21.7 %collective-permute-start.8 = (f32[112,896]{1,0:T(8,128)S(1)}, f32[112,896]{1,0:T(8,128)S(1)}, u32[]{:S(2)}, u32[]{:S(2)}) collective-permute-start(f32[112,896]{1,0:T(8,128)S(1)} %constant_dynamic-update-slice_fusion.refs_12_), channel_id=1, source_target_pairs={{0,48},{16,0},{32,16},{48,32},{64,112},{80,64},{96,80},{112,96},{1... | collective-permute-start | bytes 1204232 | tf_op jit(solution)/shard_map/gather/ppermute | solution.py:24
  20.7 20.1 %collective-permute-start.7 = (f32[112,896]{1,0:T(8,128)S(1)}, f32[112,896]{1,0:T(8,128)S(1)}, u32[]{:S(2)}, u32[]{:S(2)}) collective-permute-start(f32[112,896]{1,0:T(8,128)S(1)} %constant_dynamic-update-slice_fusion.refs_12_), channel_id=1, source_target_pairs={{0,16},{16,32},{32,48},{48,0},{64,80},{80,96},{96,112},{112,64},{1... | collective-permute-start | bytes 1204232 | tf_op jit(solution)/shard_map/gather/ppermute | solution.py:24
  21.2 19.6 %collective-permute-start.9 = (f32[56,896]{1,0:T(8,128)S(1)}, f32[56,896]{1,0:T(8,128)S(1)}, u32[]{:S(2)}, u32[]{:S(2)}) collective-permute-start(f32[56,896]{1,0:T(8,128)S(1)} %collective-permute-done.5), channel_id=1, source_target_pairs={{0,64},{16,80},{32,96},{48,112},{64,0},{80,16},{96,32},{112,48},{1... | collective-permute-start | bytes 602120 | tf_op jit(solution)/shard_map/gather/ppermute | solution.py:24
  23.0 17.8 %collective-permute-start.10 = (f32[56,896]{1,0:T(8,128)S(1)}, f32[56,896]{1,0:T(8,128)S(1)}, u32[]{:S(2)}, u32[]{:S(2)}) collective-permute-start(f32[56,896]{1,0:T(8,128)S(1)} %bitcast.50), channel_id=1, source_target_pairs={{0,8},{1,9},{2,10},{3,11},{4,12},{5,13},{6,14},{7,15},{8,0},{9,1},... | collective-permute-start | bytes 602120 | tf_op jit(solution)/shard_map/gather/ppermute | solution.py:34
  27.5 13.3 %collective-permute-start.6 = (f32[56,896]{1,0:T(8,128)S(1)}, f32[56,896]{1,0:T(8,128)S(1)}, u32[]{:S(2)}, u32[]{:S(2)}) collective-permute-start(f32[56,896]{1,0:T(8,128)S(1)} %collective-permute-done.2.refs_9_), channel_id=1, source_target_pairs={{0,16},{16,32},{32,48},{48,0},{64,80},{80,96},{96,112},{112,64},{1... | collective-permute-start | bytes 602120 | tf_op jit(solution)/shard_map/gather/ppermute | solution.py:24
  40.8 3.8 %copy-start.3 = (f32[112,896]{1,0:T(8,128)}, f32[112,896]{1,0:T(8,128)S(1)}, u32[]{:S(2)}) copy-start(f32[112,896]{1,0:T(8,128)S(1)} %collective-permute-done.8.refs_14_) | copy-start | bytes 1204228
  40.8 3.8 %copy-start.2 = (f32[112,896]{1,0:T(8,128)}, f32[112,896]{1,0:T(8,128)S(1)}, u32[]{:S(2)}) copy-start(f32[112,896]{1,0:T(8,128)S(1)} %collective-permute-done.7.refs_13_) | copy-start | bytes 1204228
  40.8 1.5 %collective-permute-start.11 = (f32[56,896]{1,0:T(8,128)S(1)}, f32[56,896]{1,0:T(8,128)S(1)}, u32[]{:S(2)}, u32[]{:S(2)}) collective-permute-start(f32[56,896]{1,0:T(8,128)S(1)} %collective-permute-done.10), channel_id=1, source_target_pairs={{0,1},{1,0},{2,3},{3,2},{4,5},{5,4},{6,7},{7,6},{8,9},{9,8},{10,11... | collective-permute-start | bytes 602120 | tf_op jit(solution)/shard_map/gather/ppermute | solution.py:34
  41.0 13.5 %collective-permute-start.15 = (f32[112,896]{1,0:T(8,128)S(1)}, f32[112,896]{1,0:T(8,128)}, u32[]{:S(2)}, u32[]{:S(2)}) collective-permute-start(f32[112,896]{1,0:T(8,128)S(1)} %pad_maximum_fusion), channel_id=1, source_target_pairs={{0,4},{1,5},{2,6},{3,7},{4,0},{5,1},{6,2},{7,3},{8,12},{9,13},{10,... | collective-permute-start | bytes 1204232 | tf_op jit(solution)/shard_map/gather/ppermute | solution.py:34
  42.4 16.3 %collective-permute-start.12 = (f32[112,896]{1,0:T(8,128)S(1)}, f32[112,896]{1,0:T(8,128)}, u32[]{:S(2)}, u32[]{:S(2)}) collective-permute-start(f32[112,896]{1,0:T(8,128)S(1)} %constant_dynamic-update-slice_fusion.2.refs_1_), channel_id=1, source_target_pairs={{0,2},{1,7},{2,4},{3,1},{4,6},{5,3},{6,0},{7,5},{8,10},{9,15},{10,... | collective-permute-start | bytes 1204232 | tf_op jit(solution)/shard_map/gather/ppermute | solution.py:34
  42.7 16.0 %collective-permute-start.19 = (f32[56,896]{1,0:T(8,128)S(1)}, f32[56,896]{1,0:T(8,128)S(1)}, u32[]{:S(2)}, u32[]{:S(2)}) collective-permute-start(f32[56,896]{1,0:T(8,128)S(1)} %collective-permute-done.9.refs_15_), channel_id=1, source_target_pairs={{0,32},{16,48},{32,0},{48,16},{64,96},{80,112},{96,64},{112,80},{1... | collective-permute-start | bytes 602120 | tf_op jit(solution)/shard_map/gather/ppermute | solution.py:24
  44.6 0.9 slice-start
  45.6 14.7 %collective-permute-start.18 = (f32[112,896]{1,0:T(8,128)S(1)}, f32[112,896]{1,0:T(8,128)S(1)}, u32[]{:S(2)}, u32[]{:S(2)}) collective-permute-start(f32[112,896]{1,0:T(8,128)S(1)} %get-tuple-element.49), channel_id=1, source_target_pairs={{0,48},{16,0},{32,16},{48,32},{64,112},{80,64},{96,80},{112,96},{1... | collective-permute-start | bytes 1204232 | tf_op jit(solution)/shard_map/gather/ppermute | solution.py:24
  46.7 13.5 %collective-permute-start.17 = (f32[112,896]{1,0:T(8,128)S(1)}, f32[112,896]{1,0:T(8,128)}, u32[]{:S(2)}, u32[]{:S(2)}) collective-permute-start(f32[112,896]{1,0:T(8,128)S(1)} %get-tuple-element.50), channel_id=1, source_target_pairs={{0,16},{16,32},{32,48},{48,0},{64,80},{80,96},{96,112},{112,64},{1... | collective-permute-start | bytes 1204232 | tf_op jit(solution)/shard_map/gather/ppermute | solution.py:24
  54.5 5.8 %collective-permute-start.16 = (f32[112,896]{1,0:T(8,128)}, f32[112,896]{1,0:T(8,128)}, u32[]{:S(2)}, u32[]{:S(2)}) collective-permute-start(f32[112,896]{1,0:T(8,128)} %collective-permute-done.15.refs_6_), channel_id=1, source_target_pairs={{0,1},{1,0},{2,3},{3,2},{4,5},{5,4},{6,7},{7,6},{8,9},{9,8},{10,11... | collective-permute-start | bytes 1204232 | tf_op jit(solution)/shard_map/gather/ppermute | solution.py:34
  58.7 2.1 %collective-permute-start.13 = (f32[112,896]{1,0:T(8,128)}, f32[112,896]{1,0:T(8,128)}, u32[]{:S(2)}, u32[]{:S(2)}) collective-permute-start(f32[112,896]{1,0:T(8,128)} %collective-permute-done.1.refs_2_), channel_id=1, source_target_pairs={{0,1},{1,0},{2,3},{3,2},{4,5},{5,4},{6,7},{7,6},{8,9},{9,8},{10,11... | collective-permute-start | bytes 1204232 | tf_op jit(solution)/shard_map/gather/ppermute | solution.py:34
  58.7 2.6 %collective-permute-start.14 = (f32[112,896]{1,0:T(8,128)}, f32[112,896]{1,0:T(8,128)}, u32[]{:S(2)}, u32[]{:S(2)}) collective-permute-start(f32[112,896]{1,0:T(8,128)} %collective-permute-done.12.refs_3_), channel_id=1, source_target_pairs={{0,1},{1,0},{2,3},{3,2},{4,5},{5,4},{6,7},{7,6},{8,9},{9,8},{10,11... | collective-permute-start | bytes 1204232 | tf_op jit(solution)/shard_map/gather/ppermute | solution.py:34
  60.3 1.0 copy-start.5
  79.0 2.6 %collective-permute-start.24 = (f32[4,56,896]{2,1,0:T(8,128)}, f32[4,56,896]{2,1,0:T(8,128)S(1)}, u32[]{:S(2)}, u32[]{:S(2)}) collective-permute-start(f32[4,56,896]{2,1,0:T(8,128)} %get-tuple-element.42), channel_id=1, source_target_pairs={{0,1},{1,0},{2,3},{3,2},{4,5},{5,4},{6,7},{7,6},{8,9},{9,8},{10,11... | collective-permute-start | bytes 2408456 | tf_op jit(solution)/shard_map/reduce/ppermute | solution.py:34
  79.2 7.8 %collective-permute-start.20 = (f32[4,56,896]{2,1,0:T(8,128)}, f32[4,56,896]{2,1,0:T(8,128)S(1)}, u32[]{:S(2)}, u32[]{:S(2)}) collective-permute-start(f32[4,56,896]{2,1,0:T(8,128)} %get-tuple-element.40), channel_id=1, source_target_pairs={{0,1},{1,0},{2,3},{3,2},{4,5},{5,4},{6,7},{7,6},{8,9},{9,8},{10,11... | collective-permute-start | bytes 2408456 | tf_op jit(solution)/shard_map/reduce/ppermute | solution.py:34
  82.8 4.2 %copy-start.1 = (f32[4,56,896]{2,1,0:T(8,128)S(1)}, f32[4,56,896]{2,1,0:T(8,128)}, u32[]{:S(2)}) copy-start(f32[4,56,896]{2,1,0:T(8,128)} %get-tuple-element.39) | copy-start | bytes 2408452
  82.9 13.4 %collective-permute-start.25 = (f32[56,896]{1,0:T(8,128)S(1)}, f32[56,896]{1,0:T(8,128)S(1)}, u32[]{:S(2)}, u32[]{:S(2)}) collective-permute-start(f32[56,896]{1,0:T(8,128)S(1)} %get-tuple-element.46), channel_id=1, source_target_pairs={{0,2},{1,3},{2,4},{3,5},{4,6},{5,7},{6,0},{7,1},{8,10},{9,11},{10,... | collective-permute-start | bytes 602120 | tf_op jit(solution)/shard_map/reduce/ppermute | solution.py:34
  84.3 12.0 %collective-permute-start.27 = (f32[56,896]{1,0:T(8,128)S(1)}, f32[56,896]{1,0:T(8,128)S(1)}, u32[]{:S(2)}, u32[]{:S(2)}) collective-permute-start(f32[56,896]{1,0:T(8,128)S(1)} %get-tuple-element.47), channel_id=1, source_target_pairs={{0,6},{1,7},{2,0},{3,1},{4,2},{5,3},{6,4},{7,5},{8,14},{9,15},{10,... | collective-permute-start | bytes 602120 | tf_op jit(solution)/shard_map/reduce/ppermute | solution.py:34
  86.4 10.4 %collective-permute-start.26 = (f32[56,896]{1,0:T(8,128)S(1)}, f32[56,896]{1,0:T(8,128)S(1)}, u32[]{:S(2)}, u32[]{:S(2)}) collective-permute-start(f32[56,896]{1,0:T(8,128)S(1)} %get-tuple-element.48), channel_id=1, source_target_pairs={{0,4},{1,5},{2,6},{3,7},{4,0},{5,1},{6,2},{7,3},{8,12},{9,13},{10,... | collective-permute-start | bytes 602120 | tf_op jit(solution)/shard_map/reduce/ppermute | solution.py:34
  87.1 13.4 %collective-permute-start.21 = (f32[56,896]{1,0:T(8,128)S(1)}, f32[56,896]{1,0:T(8,128)S(1)}, u32[]{:S(2)}, u32[]{:S(2)}) collective-permute-start(f32[56,896]{1,0:T(8,128)S(1)} %get-tuple-element.43), channel_id=1, source_target_pairs={{0,2},{1,3},{2,4},{3,5},{4,6},{5,7},{6,0},{7,1},{8,10},{9,11},{10,... | collective-permute-start | bytes 602120 | tf_op jit(solution)/shard_map/reduce/ppermute | solution.py:34
  88.3 15.3 %collective-permute-start.23 = (f32[56,896]{1,0:T(8,128)S(1)}, f32[56,896]{1,0:T(8,128)S(1)}, u32[]{:S(2)}, u32[]{:S(2)}) collective-permute-start(f32[56,896]{1,0:T(8,128)S(1)} %get-tuple-element.44), channel_id=1, source_target_pairs={{0,6},{1,7},{2,0},{3,1},{4,2},{5,3},{6,4},{7,5},{8,14},{9,15},{10,... | collective-permute-start | bytes 602120 | tf_op jit(solution)/shard_map/reduce/ppermute | solution.py:34
  96.2 8.3 %collective-permute-start.22 = (f32[56,896]{1,0:T(8,128)S(1)}, f32[56,896]{1,0:T(8,128)S(1)}, u32[]{:S(2)}, u32[]{:S(2)}) collective-permute-start(f32[56,896]{1,0:T(8,128)S(1)} %get-tuple-element.45), channel_id=1, source_target_pairs={{0,4},{1,5},{2,6},{3,7},{4,0},{5,1},{6,2},{7,3},{8,12},{9,13},{10,... | collective-permute-start | bytes 602120 | tf_op jit(solution)/shard_map/reduce/ppermute | solution.py:34
  96.8 11.5 %collective-permute-start.28 = (f32[56,896]{1,0:T(8,128)S(1)}, f32[56,896]{1,0:T(8,128)S(1)}, u32[]{:S(2)}, u32[]{:S(2)}) collective-permute-start(f32[56,896]{1,0:T(8,128)S(1)} %fusion.2), channel_id=1, source_target_pairs={{0,8},{1,9},{2,10},{3,11},{4,12},{5,13},{6,14},{7,15},{8,0},{9,1},... | collective-permute-start | bytes 602120 | tf_op jit(solution)/shard_map/reduce/ppermute | solution.py:34

commit v5 on v4

--- a/solution.py
+++ b/solution.py
@@ -100,11 +100,13 @@
     fit = fit_copies(places, b32, zl, y, sem, 16)
     for copy in amp + fit:
         copy.start()
-    for copy in amp:
-        copy.wait()
-    for row in range(0, V, 128):
-        rows = slice(row, row + 128)
-        t_hi[rows], t_lo[rows] = split(t32[rows])
+    for f in (0, 1):
+        for copy in amp[8 * f : 8 * f + 8]:
+            copy.wait()
+        start = (zh + f) % NZH * HALF
+        for row in range(0, HALF, 64):
+            rows = pl.ds(pl.multiple_of(start + row, 64), 64)
+            t_hi[rows], t_lo[rows] = split(t32[rows])
     for copy in fit:
         copy.wait()
     for row in (0, HALF):
@@ -205,10 +207,10 @@
     )
 
     def reduce_x(keep, send):
-        both = keep + swap_core(send)
-        total = both[0]
+        got = swap_core(send)
+        total = keep[0] + got[0]
         for k in (1, 2, 3):
-            total = total + aux_permute(both[k], lambda zh, x, c, k=k: (zh, x + k, c))
+            total = total + aux_permute(keep[k] + got[k], lambda zh, x, c, k=k: (zh, x + k, c))
         return total
 
     with jax.named_scope("reduce"):

time: 110 us -> 110 us (level)
  no operation moved by 1% of the time
where the time goes in v5:
time: 110 us
  waiting for transfers between devices  54.8 us (50%)
  starting transfers between devices  32.2 us (29%)
  Pallas kernels  17.7 us (16%)
  local copies, waits for them, and re-layouts  2.92 us (3%)
  other arithmetic  2.53 us (2%)
    ppermute x18, waiting for transfers between devices, aux_permute(): return lax.ppermute(value, 'aux', steps)  45.2 us
    pallas_call x1, Pallas kernels, call(): pl.pallas_call(kernel, out_shape=outs, in_specs=in_specs, out_specs=out_s...  17.7 us
    ppermute x18, starting transfers between devices, aux_permute(): return lax.ppermute(value, 'aux', steps)  17.3 us
    ppermute x11, starting transfers between devices, pair_permute(): return lax.ppermute(value, 'pair', steps)  14.9 us
    ppermute x11, waiting for transfers between devices, pair_permute(): return lax.ppermute(value, 'pair', steps)  9.58 us
  transfers between devices with their start and end apart: 29, of which 18 were waited for; matrix products, arithmetic and copies ran while one was open for 2% of the time, Pallas kernels for 0%

profile of v5, /device:TPU:32, one launch (start us, length us, event | category | flops | bytes accessed | tf_op | source)
XLA Modules:
  0.0 110.3 jit_solution(18294524488580698552)
XLA Ops:
  0.0 0.9 copy.6
  0.9 0.0 copy-start
  1.0 0.1 collective-permute-start
  1.1 1.4 %collective-permute-done = f32[56,896]{1,0:T(8,128)S(1)} collective-permute-done((f32[56,896]{1,0:T(8,128)S(1)}, f32[56,896]{1,0:T(8,128)S(1)}, u32[]{:S(2)}, u32[]{:S(2)}) %collective-permute-start) | collective-permute-done | bytes 200736 | tf_op jit(solution)/shard_map/gather/ppermute | solution.py:34
  2.5 1.6 %collective-permute-start.1 = (f32[112,896]{1,0:T(8,128)S(1)}, f32[112,896]{1,0:T(8,128)}, u32[]{:S(2)}, u32[]{:S(2)}) collective-permute-start(f32[112,896]{1,0:T(8,128)S(1)} %pad_maximum_fusion.1.refs_0_), channel_id=1, source_target_pairs={{0,2},{1,7},{2,4},{3,1},{4,6},{5,3},{6,0},{7,5},{8,10},{9,15},{10,... | collective-permute-start | bytes 1204232 | tf_op jit(solution)/shard_map/gather/ppermute | solution.py:34
  4.1 3.3 %collective-permute-start.5 = (f32[56,896]{1,0:T(8,128)S(1)}, f32[56,896]{1,0:T(8,128)S(1)}, u32[]{:S(2)}, u32[]{:S(2)}) collective-permute-start(f32[56,896]{1,0:T(8,128)S(1)} %bitcast.43), channel_id=1, source_target_pairs={{0,128},{16,144},{32,160},{48,176},{64,192},{80,208},{96,224},{112... | collective-permute-start | bytes 602120 | tf_op jit(solution)/shard_map/gather/ppermute | solution.py:24
  7.4 0.1 collective-permute-start.4
  7.5 3.0 %collective-permute-start.3 = (f32[56,896]{1,0:T(8,128)S(1)}, f32[56,896]{1,0:T(8,128)S(1)}, u32[]{:S(2)}, u32[]{:S(2)}) collective-permute-start(f32[56,896]{1,0:T(8,128)S(1)} %bitcast.45), channel_id=1, source_target_pairs={{0,48},{16,0},{32,16},{48,32},{64,112},{80,64},{96,80},{112,96},{1... | collective-permute-start | bytes 602120 | tf_op jit(solution)/shard_map/gather/ppermute | solution.py:24
  10.5 6.1 %collective-permute-done.5 = f32[56,896]{1,0:T(8,128)S(1)} collective-permute-done((f32[56,896]{1,0:T(8,128)S(1)}, f32[56,896]{1,0:T(8,128)S(1)}, u32[]{:S(2)}, u32[]{:S(2)}) %collective-permute-start.5) | collective-permute-done | bytes 200736 | tf_op jit(solution)/shard_map/gather/ppermute | solution.py:24
  16.6 0.9 collective-permute-done.4
  17.5 0.0 collective-permute-done.3.refs_10_
  17.5 1.6 %collective-permute-done.2.refs_9_ = f32[56,896]{1,0:T(8,128)S(1)} collective-permute-done((f32[56,896]{1,0:T(8,128)S(1)}, f32[56,896]{1,0:T(8,128)S(1)}, u32[]{:S(2)}, u32[]{:S(2)}) %collective-permute-start.2) | collective-permute-done | bytes 200736 | tf_op jit(solution)/shard_map/gather/ppermute | solution.py:24
  19.1 0.0 collective-permute-done.1.refs_2_
  19.1 1.5 %collective-permute-start.8 = (f32[112,896]{1,0:T(8,128)S(1)}, f32[112,896]{1,0:T(8,128)S(1)}, u32[]{:S(2)}, u32[]{:S(2)}) collective-permute-start(f32[112,896]{1,0:T(8,128)S(1)} %constant_dynamic-update-slice_fusion.refs_12_), channel_id=1, source_target_pairs={{0,48},{16,0},{32,16},{48,32},{64,112},{80,64},{96,80},{112,96},{1... | collective-permute-start | bytes 1204232 | tf_op jit(solution)/shard_map/gather/ppermute | solution.py:24
  20.7 0.6 collective-permute-start.7
  21.2 1.7 %collective-permute-start.9 = (f32[56,896]{1,0:T(8,128)S(1)}, f32[56,896]{1,0:T(8,128)S(1)}, u32[]{:S(2)}, u32[]{:S(2)}) collective-permute-start(f32[56,896]{1,0:T(8,128)S(1)} %collective-permute-done.5), channel_id=1, source_target_pairs={{0,64},{16,80},{32,96},{48,112},{64,0},{80,16},{96,32},{112,48},{1... | collective-permute-start | bytes 602120 | tf_op jit(solution)/shard_map/gather/ppermute | solution.py:24
  23.0 4.5 %collective-permute-start.10 = (f32[56,896]{1,0:T(8,128)S(1)}, f32[56,896]{1,0:T(8,128)S(1)}, u32[]{:S(2)}, u32[]{:S(2)}) collective-permute-start(f32[56,896]{1,0:T(8,128)S(1)} %bitcast.50), channel_id=1, source_target_pairs={{0,8},{1,9},{2,10},{3,11},{4,12},{5,13},{6,14},{7,15},{8,0},{9,1},... | collective-permute-start | bytes 602120 | tf_op jit(solution)/shard_map/gather/ppermute | solution.py:34
  27.5 0.6 collective-permute-start.6
  28.1 12.7 %collective-permute-done.10 = f32[56,896]{1,0:T(8,128)S(1)} collective-permute-done((f32[56,896]{1,0:T(8,128)S(1)}, f32[56,896]{1,0:T(8,128)S(1)}, u32[]{:S(2)}, u32[]{:S(2)}) %collective-permute-start.10) | collective-permute-done | bytes 200736 | tf_op jit(solution)/shard_map/gather/ppermute | solution.py:34
  40.8 0.0 collective-permute-done.9.refs_15_
  40.8 0.0 collective-permute-done.6.refs_11_
  40.8 0.1 collective-permute-start.11
  41.0 0.6 collective-permute-start.15
  41.6 0.8 collective-permute-done.11
  42.4 0.3 collective-permute-start.12
  42.7 1.9 %collective-permute-start.19 = (f32[56,896]{1,0:T(8,128)S(1)}, f32[56,896]{1,0:T(8,128)S(1)}, u32[]{:S(2)}, u32[]{:S(2)}) collective-permute-start(f32[56,896]{1,0:T(8,128)S(1)} %collective-permute-done.9.refs_15_), channel_id=1, source_target_pairs={{0,32},{16,48},{32,0},{48,16},{64,96},{80,112},{96,64},{112,80},{1... | collective-permute-start | bytes 602120 | tf_op jit(solution)/shard_map/gather/ppermute | solution.py:24
  44.6 0.9 slice-done
  45.5 0.1 pad_maximum_fusion.2
  45.6 1.1 %collective-permute-start.18 = (f32[112,896]{1,0:T(8,128)S(1)}, f32[112,896]{1,0:T(8,128)S(1)}, u32[]{:S(2)}, u32[]{:S(2)}) collective-permute-start(f32[112,896]{1,0:T(8,128)S(1)} %get-tuple-element.49), channel_id=1, source_target_pairs={{0,48},{16,0},{32,16},{48,32},{64,112},{80,64},{96,80},{112,96},{1... | collective-permute-start | bytes 1204232 | tf_op jit(solution)/shard_map/gather/ppermute | solution.py:24
  46.7 1.0 collective-permute-start.17
  47.7 6.8 %collective-permute-done.15.refs_6_ = f32[112,896]{1,0:T(8,128)} collective-permute-done((f32[112,896]{1,0:T(8,128)S(1)}, f32[112,896]{1,0:T(8,128)}, u32[]{:S(2)}, u32[]{:S(2)}) %collective-permute-start.15) | collective-permute-done | bytes 401440 | tf_op jit(solution)/shard_map/gather/ppermute | solution.py:34
  54.5 0.0 collective-permute-start.16
  54.5 4.2 %collective-permute-done.12.refs_3_ = f32[112,896]{1,0:T(8,128)} collective-permute-done((f32[112,896]{1,0:T(8,128)S(1)}, f32[112,896]{1,0:T(8,128)}, u32[]{:S(2)}, u32[]{:S(2)}) %collective-permute-start.12) | collective-permute-done | bytes 401440 | tf_op jit(solution)/shard_map/gather/ppermute | solution.py:34
  58.7 0.0 collective-permute-start.13
  58.7 0.0 collective-permute-done.19.refs_18_
  58.7 0.5 collective-permute-start.14
  59.2 0.1 stack.23.place_ref
  59.3 1.0 collective-permute-done.18.refs_17_
  60.3 0.5 collective-permute-done.13.refs_4_
  60.7 0.6 collective-permute-done.14.refs_5_
  61.3 17.7 %ladder.1 = (f32[4,56,896]{2,1,0:T(8,128)}, f32[4,56,896]{2,1,0:T(8,128)}, f32[4,56,896]{2,1,0:T(8,128)}, f32[4,56,896]{2,1,0:T(8,128)}) custom-call(s32[5]{0:T(128)S(1)} %stack.23.place_ref, f32[112,896]{1,0:T(8,128)S(1)} %pad_maximum_fusion.1.refs_0_, f32[112,896]{1,0:T(8,128)S(1)} %constant_dynamic-update-slice_fusion.2.refs_1_, ...), custom_call_target="tpu_custom_call" | custom-call | flops 8631877632 | bytes 12845056 | tf_op jit(solution)/shard_map/ladder/pallas_call | solution.py:136
  79.0 0.2 collective-permute-start.24
  79.2 0.4 collective-permute-start.20
  79.6 2.0 %collective-permute-done.24 = f32[4,56,896]{2,1,0:T(8,128)S(1)} collective-permute-done((f32[4,56,896]{2,1,0:T(8,128)}, f32[4,56,896]{2,1,0:T(8,128)S(1)}, u32[]{:S(2)}, u32[]{:S(2)}) %collective-permute-start.24) | collective-permute-done | bytes 802848 | tf_op jit(solution)/shard_map/reduce/ppermute | solution.py:34
  81.6 1.3 %fusion.2 = (f32[56,896]{1,0:T(8,128)S(1)}, f32[56,896]{1,0:T(8,128)S(1)}, f32[56,896]{1,0:T(8,128)S(1)}) fusion(f32[4,56,896]{2,1,0:T(8,128)S(1)} %collective-permute-done.24, f32[4,56,896]{2,1,0:T(8,128)} %get-tuple-element.41), kind=kLoop, calls=%fused_computation.9 | loop fusion | flops 150528 | bytes 1806336 | tf_op jit(solution)/shard_map/reduce/add | solution.py:213
  82.8 1.4 %collective-permute-start.25 = (f32[56,896]{1,0:T(8,128)S(1)}, f32[56,896]{1,0:T(8,128)S(1)}, u32[]{:S(2)}, u32[]{:S(2)}) collective-permute-start(f32[56,896]{1,0:T(8,128)S(1)} %get-tuple-element.46), channel_id=1, source_target_pairs={{0,2},{1,3},{2,4},{3,5},{4,6},{5,7},{6,0},{7,1},{8,10},{9,11},{10,... | collective-permute-start | bytes 602120 | tf_op jit(solution)/shard_map/reduce/ppermute | solution.py:34
  84.3 2.1 %collective-permute-start.27 = (f32[56,896]{1,0:T(8,128)S(1)}, f32[56,896]{1,0:T(8,128)S(1)}, u32[]{:S(2)}, u32[]{:S(2)}) collective-permute-start(f32[56,896]{1,0:T(8,128)S(1)} %get-tuple-element.47), channel_id=1, source_target_pairs={{0,6},{1,7},{2,0},{3,1},{4,2},{5,3},{6,4},{7,5},{8,14},{9,15},{10,... | collective-permute-start | bytes 602120 | tf_op jit(solution)/shard_map/reduce/ppermute | solution.py:34
  86.4 0.6 collective-permute-start.26
  87.0 0.0 collective-permute-done.20
  87.0 0.1 fusion.9
  87.1 1.1 %collective-permute-start.21 = (f32[56,896]{1,0:T(8,128)S(1)}, f32[56,896]{1,0:T(8,128)S(1)}, u32[]{:S(2)}, u32[]{:S(2)}) collective-permute-start(f32[56,896]{1,0:T(8,128)S(1)} %get-tuple-element.43), channel_id=1, source_target_pairs={{0,2},{1,3},{2,4},{3,5},{4,6},{5,7},{6,0},{7,1},{8,10},{9,11},{10,... | collective-permute-start | bytes 602120 | tf_op jit(solution)/shard_map/reduce/ppermute | solution.py:34
  88.2 2.2 %collective-permute-start.23 = (f32[56,896]{1,0:T(8,128)S(1)}, f32[56,896]{1,0:T(8,128)S(1)}, u32[]{:S(2)}, u32[]{:S(2)}) collective-permute-start(f32[56,896]{1,0:T(8,128)S(1)} %get-tuple-element.44), channel_id=1, source_target_pairs={{0,6},{1,7},{2,0},{3,1},{4,2},{5,3},{6,4},{7,5},{8,14},{9,15},{10,... | collective-permute-start | bytes 602120 | tf_op jit(solution)/shard_map/reduce/ppermute | solution.py:34
  90.4 5.8 %collective-permute-done.25 = f32[56,896]{1,0:T(8,128)S(1)} collective-permute-done((f32[56,896]{1,0:T(8,128)S(1)}, f32[56,896]{1,0:T(8,128)S(1)}, u32[]{:S(2)}, u32[]{:S(2)}) %collective-permute-start.25) | collective-permute-done | bytes 200736 | tf_op jit(solution)/shard_map/reduce/ppermute | solution.py:34
  96.2 0.0 collective-permute-start.22
  96.2 0.0 collective-permute-done.27
  96.2 0.5 collective-permute-done.26
  96.8 1.0 fusion.6
  97.8 1.6 %collective-permute-start.28 = (f32[56,896]{1,0:T(8,128)S(1)}, f32[56,896]{1,0:T(8,128)S(1)}, u32[]{:S(2)}, u32[]{:S(2)}) collective-permute-start(f32[56,896]{1,0:T(8,128)S(1)} %fusion.6), channel_id=1, source_target_pairs={{0,8},{1,9},{2,10},{3,11},{4,12},{5,13},{6,14},{7,15},{8,0},{9,1},... | collective-permute-start | bytes 602120 | tf_op jit(solution)/shard_map/reduce/ppermute | solution.py:34
  99.4 1.1 %collective-permute-done.21 = f32[56,896]{1,0:T(8,128)S(1)} collective-permute-done((f32[56,896]{1,0:T(8,128)S(1)}, f32[56,896]{1,0:T(8,128)S(1)}, u32[]{:S(2)}, u32[]{:S(2)}) %collective-permute-start.21) | collective-permute-done | bytes 200736 | tf_op jit(solution)/shard_map/reduce/ppermute | solution.py:34
  100.5 3.1 %collective-permute-done.23 = f32[56,896]{1,0:T(8,128)S(1)} collective-permute-done((f32[56,896]{1,0:T(8,128)S(1)}, f32[56,896]{1,0:T(8,128)S(1)}, u32[]{:S(2)}, u32[]{:S(2)}) %collective-permute-start.23) | collective-permute-done | bytes 200736 | tf_op jit(solution)/shard_map/reduce/ppermute | solution.py:34
  103.6 1.0 collective-permute-done.22
  104.6 4.8 %collective-permute-done.28 = f32[56,896]{1,0:T(8,128)S(1)} collective-permute-done((f32[56,896]{1,0:T(8,128)S(1)}, f32[56,896]{1,0:T(8,128)S(1)}, u32[]{:S(2)}, u32[]{:S(2)}) %collective-permute-start.28) | collective-permute-done | bytes 200736 | tf_op jit(solution)/shard_map/reduce/ppermute | solution.py:34
  109.3 0.1 fusion.15
  109.4 0.9 copy.3
  (24 shorter events, 0.2 us)
Async XLA Ops:
  0.9 3.2 %copy-start = (f32[1,56,896]{2,1,0:T(8,128)S(1)}, f32[1,56,896]{2,1,0:T(8,128)}, u32[]{:S(2)}) copy-start(f32[1,56,896]{2,1,0:T(8,128)} %param.3) | copy-start | bytes 602116
  1.0 1.5 %collective-permute-start = (f32[56,896]{1,0:T(8,128)S(1)}, f32[56,896]{1,0:T(8,128)S(1)}, u32[]{:S(2)}, u32[]{:S(2)}) collective-permute-start(f32[56,896]{1,0:T(8,128)S(1)} %bitcast.48), channel_id=1, source_target_pairs={{0,1},{1,0},{2,3},{3,2},{4,5},{5,4},{6,7},{7,6},{8,9},{9,8},{10,11... | collective-permute-start | bytes 602120 | tf_op jit(solution)/shard_map/gather/ppermute | solution.py:34
  2.5 16.5 %collective-permute-start.1 = (f32[112,896]{1,0:T(8,128)S(1)}, f32[112,896]{1,0:T(8,128)}, u32[]{:S(2)}, u32[]{:S(2)}) collective-permute-start(f32[112,896]{1,0:T(8,128)S(1)} %pad_maximum_fusion.1.refs_0_), channel_id=1, source_target_pairs={{0,2},{1,7},{2,4},{3,1},{4,6},{5,3},{6,0},{7,5},{8,10},{9,15},{10,... | collective-permute-start | bytes 1204232 | tf_op jit(solution)/shard_map/gather/ppermute | solution.py:34
  4.1 12.5 %collective-permute-start.5 = (f32[56,896]{1,0:T(8,128)S(1)}, f32[56,896]{1,0:T(8,128)S(1)}, u32[]{:S(2)}, u32[]{:S(2)}) collective-permute-start(f32[56,896]{1,0:T(8,128)S(1)} %bitcast.43), channel_id=1, source_target_pairs={{0,128},{16,144},{32,160},{48,176},{64,192},{80,208},{96,224},{112... | collective-permute-start | bytes 602120 | tf_op jit(solution)/shard_map/gather/ppermute | solution.py:24
  7.4 10.1 %collective-permute-start.4 = (f32[56,896]{1,0:T(8,128)S(1)}, f32[56,896]{1,0:T(8,128)S(1)}, u32[]{:S(2)}, u32[]{:S(2)}) collective-permute-start(f32[56,896]{1,0:T(8,128)S(1)} %bitcast.44), channel_id=1, source_target_pairs={{0,64},{16,80},{32,96},{48,112},{64,0},{80,16},{96,32},{112,48},{1... | collective-permute-start | bytes 602120 | tf_op jit(solution)/shard_map/gather/ppermute | solution.py:24
  7.5 10.0 %collective-permute-start.3 = (f32[56,896]{1,0:T(8,128)S(1)}, f32[56,896]{1,0:T(8,128)S(1)}, u32[]{:S(2)}, u32[]{:S(2)}) collective-permute-start(f32[56,896]{1,0:T(8,128)S(1)} %bitcast.45), channel_id=1, source_target_pairs={{0,48},{16,0},{32,16},{48,32},{64,112},{80,64},{96,80},{112,96},{1... | collective-permute-start | bytes 602120 | tf_op jit(solution)/shard_map/gather/ppermute | solution.py:24
  10.5 8.6 %collective-permute-start.2 = (f32[56,896]{1,0:T(8,128)S(1)}, f32[56,896]{1,0:T(8,128)S(1)}, u32[]{:S(2)}, u32[]{:S(2)}) collective-permute-start(f32[56,896]{1,0:T(8,128)S(1)} %bitcast.46), channel_id=1, source_target_pairs={{0,16},{16,32},{32,48},{48,0},{64,80},{80,96},{96,112},{112,64},{1... | collective-permute-start | bytes 602120 | tf_op jit(solution)/shard_map/gather/ppermute | solution.py:24
  19.1 21.9 %copy-start.4 = (f32[112,896]{1,0:T(8,128)}, f32[112,896]{1,0:T(8,128)S(1)}, u32[]{:S(2)}) copy-start(f32[112,896]{1,0:T(8,128)S(1)} %constant_dynamic-update-slice_fusion.refs_12_) | copy-start | bytes 1204228
  19.1 21.7 %collective-permute-start.8 = (f32[112,896]{1,0:T(8,128)S(1)}, f32[112,896]{1,0:T(8,128)S(1)}, u32[]{:S(2)}, u32[]{:S(2)}) collective-permute-start(f32[112,896]{1,0:T(8,128)S(1)} %constant_dynamic-update-slice_fusion.refs_12_), channel_id=1, source_target_pairs={{0,48},{16,0},{32,16},{48,32},{64,112},{80,64},{96,80},{112,96},{1... | collective-permute-start | bytes 1204232 | tf_op jit(solution)/shard_map/gather/ppermute | solution.py:24
  20.7 20.1 %collective-permute-start.7 = (f32[112,896]{1,0:T(8,128)S(1)}, f32[112,896]{1,0:T(8,128)S(1)}, u32[]{:S(2)}, u32[]{:S(2)}) collective-permute-start(f32[112,896]{1,0:T(8,128)S(1)} %constant_dynamic-update-slice_fusion.refs_12_), channel_id=1, source_target_pairs={{0,16},{16,32},{32,48},{48,0},{64,80},{80,96},{96,112},{112,64},{1... | collective-permute-start | bytes 1204232 | tf_op jit(solution)/shard_map/gather/ppermute | solution.py:24
  21.2 19.6 %collective-permute-start.9 = (f32[56,896]{1,0:T(8,128)S(1)}, f32[56,896]{1,0:T(8,128)S(1)}, u32[]{:S(2)}, u32[]{:S(2)}) collective-permute-start(f32[56,896]{1,0:T(8,128)S(1)} %collective-permute-done.5), channel_id=1, source_target_pairs={{0,64},{16,80},{32,96},{48,112},{64,0},{80,16},{96,32},{112,48},{1... | collective-permute-start | bytes 602120 | tf_op jit(solution)/shard_map/gather/ppermute | solution.py:24
  23.0 17.8 %collective-permute-start.10 = (f32[56,896]{1,0:T(8,128)S(1)}, f32[56,896]{1,0:T(8,128)S(1)}, u32[]{:S(2)}, u32[]{:S(2)}) collective-permute-start(f32[56,896]{1,0:T(8,128)S(1)} %bitcast.50), channel_id=1, source_target_pairs={{0,8},{1,9},{2,10},{3,11},{4,12},{5,13},{6,14},{7,15},{8,0},{9,1},... | collective-permute-start | bytes 602120 | tf_op jit(solution)/shard_map/gather/ppermute | solution.py:34
  27.5 13.3 %collective-permute-start.6 = (f32[56,896]{1,0:T(8,128)S(1)}, f32[56,896]{1,0:T(8,128)S(1)}, u32[]{:S(2)}, u32[]{:S(2)}) collective-permute-start(f32[56,896]{1,0:T(8,128)S(1)} %collective-permute-done.2.refs_9_), channel_id=1, source_target_pairs={{0,16},{16,32},{32,48},{48,0},{64,80},{80,96},{96,112},{112,64},{1... | collective-permute-start | bytes 602120 | tf_op jit(solution)/shard_map/gather/ppermute | solution.py:24
  40.8 3.8 %copy-start.3 = (f32[112,896]{1,0:T(8,128)}, f32[112,896]{1,0:T(8,128)S(1)}, u32[]{:S(2)}) copy-start(f32[112,896]{1,0:T(8,128)S(1)} %collective-permute-done.8.refs_14_) | copy-start | bytes 1204228
  40.8 3.8 %copy-start.2 = (f32[112,896]{1,0:T(8,128)}, f32[112,896]{1,0:T(8,128)S(1)}, u32[]{:S(2)}) copy-start(f32[112,896]{1,0:T(8,128)S(1)} %collective-permute-done.7.refs_13_) | copy-start | bytes 1204228
  40.8 1.5 %collective-permute-start.11 = (f32[56,896]{1,0:T(8,128)S(1)}, f32[56,896]{1,0:T(8,128)S(1)}, u32[]{:S(2)}, u32[]{:S(2)}) collective-permute-start(f32[56,896]{1,0:T(8,128)S(1)} %collective-permute-done.10), channel_id=1, source_target_pairs={{0,1},{1,0},{2,3},{3,2},{4,5},{5,4},{6,7},{7,6},{8,9},{9,8},{10,11... | collective-permute-start | bytes 602120 | tf_op jit(solution)/shard_map/gather/ppermute | solution.py:34
  41.0 13.5 %collective-permute-start.15 = (f32[112,896]{1,0:T(8,128)S(1)}, f32[112,896]{1,0:T(8,128)}, u32[]{:S(2)}, u32[]{:S(2)}) collective-permute-start(f32[112,896]{1,0:T(8,128)S(1)} %pad_maximum_fusion), channel_id=1, source_target_pairs={{0,4},{1,5},{2,6},{3,7},{4,0},{5,1},{6,2},{7,3},{8,12},{9,13},{10,... | collective-permute-start | bytes 1204232 | tf_op jit(solution)/shard_map/gather/ppermute | solution.py:34
  42.4 16.3 %collective-permute-start.12 = (f32[112,896]{1,0:T(8,128)S(1)}, f32[112,896]{1,0:T(8,128)}, u32[]{:S(2)}, u32[]{:S(2)}) collective-permute-start(f32[112,896]{1,0:T(8,128)S(1)} %constant_dynamic-update-slice_fusion.2.refs_1_), channel_id=1, source_target_pairs={{0,2},{1,7},{2,4},{3,1},{4,6},{5,3},{6,0},{7,5},{8,10},{9,15},{10,... | collective-permute-start | bytes 1204232 | tf_op jit(solution)/shard_map/gather/ppermute | solution.py:34
  42.7 16.0 %collective-permute-start.19 = (f32[56,896]{1,0:T(8,128)S(1)}, f32[56,896]{1,0:T(8,128)S(1)}, u32[]{:S(2)}, u32[]{:S(2)}) collective-permute-start(f32[56,896]{1,0:T(8,128)S(1)} %collective-permute-done.9.refs_15_), channel_id=1, source_target_pairs={{0,32},{16,48},{32,0},{48,16},{64,96},{80,112},{96,64},{112,80},{1... | collective-permute-start | bytes 602120 | tf_op jit(solution)/shard_map/gather/ppermute | solution.py:24
  44.6 0.9 slice-start
  45.6 14.7 %collective-permute-start.18 = (f32[112,896]{1,0:T(8,128)S(1)}, f32[112,896]{1,0:T(8,128)S(1)}, u32[]{:S(2)}, u32[]{:S(2)}) collective-permute-start(f32[112,896]{1,0:T(8,128)S(1)} %get-tuple-element.49), channel_id=1, source_target_pairs={{0,48},{16,0},{32,16},{48,32},{64,112},{80,64},{96,80},{112,96},{1... | collective-permute-start | bytes 1204232 | tf_op jit(solution)/shard_map/gather/ppermute | solution.py:24
  46.7 13.5 %collective-permute-start.17 = (f32[112,896]{1,0:T(8,128)S(1)}, f32[112,896]{1,0:T(8,128)}, u32[]{:S(2)}, u32[]{:S(2)}) collective-permute-start(f32[112,896]{1,0:T(8,128)S(1)} %get-tuple-element.50), channel_id=1, source_target_pairs={{0,16},{16,32},{32,48},{48,0},{64,80},{80,96},{96,112},{112,64},{1... | collective-permute-start | bytes 1204232 | tf_op jit(solution)/shard_map/gather/ppermute | solution.py:24
  54.5 5.8 %collective-permute-start.16 = (f32[112,896]{1,0:T(8,128)}, f32[112,896]{1,0:T(8,128)}, u32[]{:S(2)}, u32[]{:S(2)}) collective-permute-start(f32[112,896]{1,0:T(8,128)} %collective-permute-done.15.refs_6_), channel_id=1, source_target_pairs={{0,1},{1,0},{2,3},{3,2},{4,5},{5,4},{6,7},{7,6},{8,9},{9,8},{10,11... | collective-permute-start | bytes 1204232 | tf_op jit(solution)/shard_map/gather/ppermute | solution.py:34
  58.7 2.1 %collective-permute-start.13 = (f32[112,896]{1,0:T(8,128)}, f32[112,896]{1,0:T(8,128)}, u32[]{:S(2)}, u32[]{:S(2)}) collective-permute-start(f32[112,896]{1,0:T(8,128)} %collective-permute-done.1.refs_2_), channel_id=1, source_target_pairs={{0,1},{1,0},{2,3},{3,2},{4,5},{5,4},{6,7},{7,6},{8,9},{9,8},{10,11... | collective-permute-start | bytes 1204232 | tf_op jit(solution)/shard_map/gather/ppermute | solution.py:34
  58.7 2.6 %collective-permute-start.14 = (f32[112,896]{1,0:T(8,128)}, f32[112,896]{1,0:T(8,128)}, u32[]{:S(2)}, u32[]{:S(2)}) collective-permute-start(f32[112,896]{1,0:T(8,128)} %collective-permute-done.12.refs_3_), channel_id=1, source_target_pairs={{0,1},{1,0},{2,3},{3,2},{4,5},{5,4},{6,7},{7,6},{8,9},{9,8},{10,11... | collective-permute-start | bytes 1204232 | tf_op jit(solution)/shard_map/gather/ppermute | solution.py:34
  60.3 1.0 copy-start.5
  79.0 2.6 %collective-permute-start.24 = (f32[4,56,896]{2,1,0:T(8,128)}, f32[4,56,896]{2,1,0:T(8,128)S(1)}, u32[]{:S(2)}, u32[]{:S(2)}) collective-permute-start(f32[4,56,896]{2,1,0:T(8,128)} %get-tuple-element.42), channel_id=1, source_target_pairs={{0,1},{1,0},{2,3},{3,2},{4,5},{5,4},{6,7},{7,6},{8,9},{9,8},{10,11... | collective-permute-start | bytes 2408456 | tf_op jit(solution)/shard_map/reduce/ppermute | solution.py:34
  79.2 7.8 %collective-permute-start.20 = (f32[4,56,896]{2,1,0:T(8,128)}, f32[4,56,896]{2,1,0:T(8,128)S(1)}, u32[]{:S(2)}, u32[]{:S(2)}) collective-permute-start(f32[4,56,896]{2,1,0:T(8,128)} %get-tuple-element.40), channel_id=1, source_target_pairs={{0,1},{1,0},{2,3},{3,2},{4,5},{5,4},{6,7},{7,6},{8,9},{9,8},{10,11... | collective-permute-start | bytes 2408456 | tf_op jit(solution)/shard_map/reduce/ppermute | solution.py:34
  81.6 5.4 %copy-start.1 = (f32[4,56,896]{2,1,0:T(8,128)S(1)}, f32[4,56,896]{2,1,0:T(8,128)}, u32[]{:S(2)}) copy-start(f32[4,56,896]{2,1,0:T(8,128)} %get-tuple-element.39) | copy-start | bytes 2408452
  82.8 13.4 %collective-permute-start.25 = (f32[56,896]{1,0:T(8,128)S(1)}, f32[56,896]{1,0:T(8,128)S(1)}, u32[]{:S(2)}, u32[]{:S(2)}) collective-permute-start(f32[56,896]{1,0:T(8,128)S(1)} %get-tuple-element.46), channel_id=1, source_target_pairs={{0,2},{1,3},{2,4},{3,5},{4,6},{5,7},{6,0},{7,1},{8,10},{9,11},{10,... | collective-permute-start | bytes 602120 | tf_op jit(solution)/shard_map/reduce/ppermute | solution.py:34
  84.3 12.0 %collective-permute-start.27 = (f32[56,896]{1,0:T(8,128)S(1)}, f32[56,896]{1,0:T(8,128)S(1)}, u32[]{:S(2)}, u32[]{:S(2)}) collective-permute-start(f32[56,896]{1,0:T(8,128)S(1)} %get-tuple-element.47), channel_id=1, source_target_pairs={{0,6},{1,7},{2,0},{3,1},{4,2},{5,3},{6,4},{7,5},{8,14},{9,15},{10,... | collective-permute-start | bytes 602120 | tf_op jit(solution)/shard_map/reduce/ppermute | solution.py:34
  86.4 10.4 %collective-permute-start.26 = (f32[56,896]{1,0:T(8,128)S(1)}, f32[56,896]{1,0:T(8,128)S(1)}, u32[]{:S(2)}, u32[]{:S(2)}) collective-permute-start(f32[56,896]{1,0:T(8,128)S(1)} %get-tuple-element.48), channel_id=1, source_target_pairs={{0,4},{1,5},{2,6},{3,7},{4,0},{5,1},{6,2},{7,3},{8,12},{9,13},{10,... | collective-permute-start | bytes 602120 | tf_op jit(solution)/shard_map/reduce/ppermute | solution.py:34
  87.1 13.5 %collective-permute-start.21 = (f32[56,896]{1,0:T(8,128)S(1)}, f32[56,896]{1,0:T(8,128)S(1)}, u32[]{:S(2)}, u32[]{:S(2)}) collective-permute-start(f32[56,896]{1,0:T(8,128)S(1)} %get-tuple-element.43), channel_id=1, source_target_pairs={{0,2},{1,3},{2,4},{3,5},{4,6},{5,7},{6,0},{7,1},{8,10},{9,11},{10,... | collective-permute-start | bytes 602120 | tf_op jit(solution)/shard_map/reduce/ppermute | solution.py:34
  88.2 15.4 %collective-permute-start.23 = (f32[56,896]{1,0:T(8,128)S(1)}, f32[56,896]{1,0:T(8,128)S(1)}, u32[]{:S(2)}, u32[]{:S(2)}) collective-permute-start(f32[56,896]{1,0:T(8,128)S(1)} %get-tuple-element.44), channel_id=1, source_target_pairs={{0,6},{1,7},{2,0},{3,1},{4,2},{5,3},{6,4},{7,5},{8,14},{9,15},{10,... | collective-permute-start | bytes 602120 | tf_op jit(solution)/shard_map/reduce/ppermute | solution.py:34
  96.2 8.3 %collective-permute-start.22 = (f32[56,896]{1,0:T(8,128)S(1)}, f32[56,896]{1,0:T(8,128)S(1)}, u32[]{:S(2)}, u32[]{:S(2)}) collective-permute-start(f32[56,896]{1,0:T(8,128)S(1)} %get-tuple-element.45), channel_id=1, source_target_pairs={{0,4},{1,5},{2,6},{3,7},{4,0},{5,1},{6,2},{7,3},{8,12},{9,13},{10,... | collective-permute-start | bytes 602120 | tf_op jit(solution)/shard_map/reduce/ppermute | solution.py:34
  97.8 11.5 %collective-permute-start.28 = (f32[56,896]{1,0:T(8,128)S(1)}, f32[56,896]{1,0:T(8,128)S(1)}, u32[]{:S(2)}, u32[]{:S(2)}) collective-permute-start(f32[56,896]{1,0:T(8,128)S(1)} %fusion.6), channel_id=1, source_target_pairs={{0,8},{1,9},{2,10},{3,11},{4,12},{5,13},{6,14},{7,15},{8,0},{9,1},... | collective-permute-start | bytes 602120 | tf_op jit(solution)/shard_map/reduce/ppermute | solution.py:34

commit v6 on v4

--- a/solution.py
+++ b/solution.py
@@ -137,7 +137,7 @@
         in_specs=in_specs,
         out_specs=out_specs,
         scratch_shapes=scratch,
-        compiler_params=pltpu.CompilerParams(vmem_limit_bytes=52 * 1024 * 1024),
+        compiler_params=pltpu.CompilerParams(vmem_limit_bytes=51 * 1024 * 1024),
         cost_estimate=pl.CostEstimate(flops=flops, bytes_accessed=moved, transcendentals=0),
         name=name,
     )(*args)

time: 110 us -> 110 us (level)
  Pallas kernels: 17.7 us -> 19 us
    pallas_call x1, Pallas kernels: 17.7 us -> 19 us  [call(): pl.pallas_call(kernel, out_shape=outs, in_specs=in_specs, out_specs=out_s...]
    ppermute x18, waiting for transfers between devices: 45.2 us -> 44 us  [aux_permute(): return lax.ppermute(value, 'aux', steps)]
  transfers between devices with their start and end apart: 29 -> 29, of which waited for: 18 -> 16; matrix products, arithmetic and copies ran while one was open for 2% -> 2% of each run, Pallas kernels for 0% -> 0%
where the time goes in v6:
time: 110 us
  waiting for transfers between devices  53.8 us (49%)
  starting transfers between devices  32.1 us (29%)
  Pallas kernels  19 us (17%)
  local copies, waits for them, and re-layouts  3 us (3%)
  other arithmetic  2.3 us (2%)
    ppermute x18, waiting for transfers between devices, aux_permute(): return lax.ppermute(value, 'aux', steps)  44 us
    pallas_call x1, Pallas kernels, call(): pl.pallas_call(kernel, out_shape=outs, in_specs=in_specs, out_specs=out_s...  19 us
    ppermute x18, starting transfers between devices, aux_permute(): return lax.ppermute(value, 'aux', steps)  17.3 us
    ppermute x11, starting transfers between devices, pair_permute(): return lax.ppermute(value, 'pair', steps)  14.8 us
    ppermute x11, waiting for transfers between devices, pair_permute(): return lax.ppermute(value, 'pair', steps)  9.8 us
  transfers between devices with their start and end apart: 29, of which 16 were waited for; matrix products, arithmetic and copies ran while one was open for 2% of the time, Pallas kernels for 0%

profile of v6, /device:TPU:32, one launch (start us, length us, event | category | flops | bytes accessed | tf_op | source)
XLA Modules:
  0.0 110.3 jit_solution(3771309131662398122)
XLA Ops:
  0.0 0.9 copy.6
  0.9 0.0 copy-start
  1.0 0.1 collective-permute-start
  1.1 1.4 %collective-permute-done = f32[56,896]{1,0:T(8,128)S(1)} collective-permute-done((f32[56,896]{1,0:T(8,128)S(1)}, f32[56,896]{1,0:T(8,128)S(1)}, u32[]{:S(2)}, u32[]{:S(2)}) %collective-permute-start) | collective-permute-done | bytes 200736 | tf_op jit(solution)/shard_map/gather/ppermute | solution.py:34
  2.5 1.6 %collective-permute-start.1 = (f32[112,896]{1,0:T(8,128)S(1)}, f32[112,896]{1,0:T(8,128)S(1)}, u32[]{:S(2)}, u32[]{:S(2)}) collective-permute-start(f32[112,896]{1,0:T(8,128)S(1)} %pad_maximum_fusion.1.refs_0_), channel_id=1, source_target_pairs={{0,2},{1,7},{2,4},{3,1},{4,6},{5,3},{6,0},{7,5},{8,10},{9,15},{10,... | collective-permute-start | bytes 1204232 | tf_op jit(solution)/shard_map/gather/ppermute | solution.py:34
  4.1 3.3 %collective-permute-start.5 = (f32[56,896]{1,0:T(8,128)S(1)}, f32[56,896]{1,0:T(8,128)S(1)}, u32[]{:S(2)}, u32[]{:S(2)}) collective-permute-start(f32[56,896]{1,0:T(8,128)S(1)} %bitcast.43), channel_id=1, source_target_pairs={{0,128},{16,144},{32,160},{48,176},{64,192},{80,208},{96,224},{112... | collective-permute-start | bytes 602120 | tf_op jit(solution)/shard_map/gather/ppermute | solution.py:24
  7.4 0.1 collective-permute-start.4
  7.5 3.0 %collective-permute-start.3 = (f32[56,896]{1,0:T(8,128)S(1)}, f32[56,896]{1,0:T(8,128)S(1)}, u32[]{:S(2)}, u32[]{:S(2)}) collective-permute-start(f32[56,896]{1,0:T(8,128)S(1)} %bitcast.45), channel_id=1, source_target_pairs={{0,48},{16,0},{32,16},{48,32},{64,112},{80,64},{96,80},{112,96},{1... | collective-permute-start | bytes 602120 | tf_op jit(solution)/shard_map/gather/ppermute | solution.py:24
  10.5 0.0 collective-permute-start.2
  10.5 6.1 %collective-permute-done.5 = f32[56,896]{1,0:T(8,128)S(1)} collective-permute-done((f32[56,896]{1,0:T(8,128)S(1)}, f32[56,896]{1,0:T(8,128)S(1)}, u32[]{:S(2)}, u32[]{:S(2)}) %collective-permute-start.5) | collective-permute-done | bytes 200736 | tf_op jit(solution)/shard_map/gather/ppermute | solution.py:24
  16.6 0.9 collective-permute-done.4
  17.5 0.0 collective-permute-done.3.refs_10_
  17.5 1.6 %collective-permute-done.2.refs_9_ = f32[56,896]{1,0:T(8,128)S(1)} collective-permute-done((f32[56,896]{1,0:T(8,128)S(1)}, f32[56,896]{1,0:T(8,128)S(1)}, u32[]{:S(2)}, u32[]{:S(2)}) %collective-permute-start.2) | collective-permute-done | bytes 200736 | tf_op jit(solution)/shard_map/gather/ppermute | solution.py:24
  19.1 0.0 collective-permute-done.1.refs_2_
  19.1 1.5 %collective-permute-start.8 = (f32[112,896]{1,0:T(8,128)S(1)}, f32[112,896]{1,0:T(8,128)S(1)}, u32[]{:S(2)}, u32[]{:S(2)}) collective-permute-start(f32[112,896]{1,0:T(8,128)S(1)} %constant_dynamic-update-slice_fusion.refs_12_), channel_id=1, source_target_pairs={{0,48},{16,0},{32,16},{48,32},{64,112},{80,64},{96,80},{112,96},{1... | collective-permute-start | bytes 1204232 | tf_op jit(solution)/shard_map/gather/ppermute | solution.py:24
  20.7 0.6 collective-permute-start.7
  21.2 1.7 %collective-permute-start.9 = (f32[56,896]{1,0:T(8,128)S(1)}, f32[56,896]{1,0:T(8,128)S(1)}, u32[]{:S(2)}, u32[]{:S(2)}) collective-permute-start(f32[56,896]{1,0:T(8,128)S(1)} %collective-permute-done.5), channel_id=1, source_target_pairs={{0,64},{16,80},{32,96},{48,112},{64,0},{80,16},{96,32},{112,48},{1... | collective-permute-start | bytes 602120 | tf_op jit(solution)/shard_map/gather/ppermute | solution.py:24
  23.0 4.5 %collective-permute-start.10 = (f32[56,896]{1,0:T(8,128)S(1)}, f32[56,896]{1,0:T(8,128)S(1)}, u32[]{:S(2)}, u32[]{:S(2)}) collective-permute-start(f32[56,896]{1,0:T(8,128)S(1)} %bitcast.50), channel_id=1, source_target_pairs={{0,8},{1,9},{2,10},{3,11},{4,12},{5,13},{6,14},{7,15},{8,0},{9,1},... | collective-permute-start | bytes 602120 | tf_op jit(solution)/shard_map/gather/ppermute | solution.py:34
  27.5 0.6 collective-permute-start.6
  28.1 12.7 %collective-permute-done.10 = f32[56,896]{1,0:T(8,128)S(1)} collective-permute-done((f32[56,896]{1,0:T(8,128)S(1)}, f32[56,896]{1,0:T(8,128)S(1)}, u32[]{:S(2)}, u32[]{:S(2)}) %collective-permute-start.10) | collective-permute-done | bytes 200736 | tf_op jit(solution)/shard_map/gather/ppermute | solution.py:34
  40.8 0.0 collective-permute-done.9.refs_15_
  40.8 0.0 collective-permute-done.6.refs_11_
  40.8 0.0 collective-permute-done.8.refs_14_
  40.8 0.1 collective-permute-start.11
  41.0 0.6 collective-permute-start.15
  41.6 0.8 collective-permute-done.11
  42.4 0.3 collective-permute-start.12
  42.7 1.9 %collective-permute-start.19 = (f32[56,896]{1,0:T(8,128)S(1)}, f32[56,896]{1,0:T(8,128)S(1)}, u32[]{:S(2)}, u32[]{:S(2)}) collective-permute-start(f32[56,896]{1,0:T(8,128)S(1)} %collective-permute-done.9.refs_15_), channel_id=1, source_target_pairs={{0,32},{16,48},{32,0},{48,16},{64,96},{80,112},{96,64},{112,80},{1... | collective-permute-start | bytes 602120 | tf_op jit(solution)/shard_map/gather/ppermute | solution.py:24
  44.6 0.9 slice-done
  45.5 0.8 pad_maximum_fusion.2
  46.3 1.1 collective-permute-start.18
  47.4 1.0 collective-permute-start.17
  48.4 6.1 %collective-permute-done.15.refs_6_ = f32[112,896]{1,0:T(8,128)} collective-permute-done((f32[112,896]{1,0:T(8,128)S(1)}, f32[112,896]{1,0:T(8,128)}, u32[]{:S(2)}, u32[]{:S(2)}) %collective-permute-start.15) | collective-permute-done | bytes 401440 | tf_op jit(solution)/shard_map/gather/ppermute | solution.py:34
  54.5 4.1 %collective-permute-done.12.refs_3_ = f32[112,896]{1,0:T(8,128)S(1)} collective-permute-done((f32[112,896]{1,0:T(8,128)S(1)}, f32[112,896]{1,0:T(8,128)S(1)}, u32[]{:S(2)}, u32[]{:S(2)}) %collective-permute-start.12) | collective-permute-done | bytes 401440 | tf_op jit(solution)/shard_map/gather/ppermute | solution.py:34
  58.5 0.0 collective-permute-start.13
  58.6 0.5 collective-permute-start.14
  59.1 0.1 stack.23.place_ref
  59.1 1.2 %collective-permute-done.18.refs_17_ = f32[112,896]{1,0:T(8,128)} collective-permute-done((f32[112,896]{1,0:T(8,128)}, f32[112,896]{1,0:T(8,128)}, u32[]{:S(2)}, u32[]{:S(2)}) %collective-permute-start.18) | collective-permute-done | bytes 401440 | tf_op jit(solution)/shard_map/gather/ppermute | solution.py:24
  60.4 0.0 collective-permute-done.17.refs_16_
  60.4 0.0 collective-permute-done.13.refs_4_
  60.4 0.6 collective-permute-done.14.refs_5_
  61.0 19.0 %ladder.1 = (f32[4,56,896]{2,1,0:T(8,128)}, f32[4,56,896]{2,1,0:T(8,128)}, f32[4,56,896]{2,1,0:T(8,128)}, f32[4,56,896]{2,1,0:T(8,128)}) custom-call(s32[5]{0:T(128)S(1)} %stack.23.place_ref, f32[112,896]{1,0:T(8,128)S(1)} %pad_maximum_fusion.1.refs_0_, f32[112,896]{1,0:T(8,128)S(1)} %constant_dynamic-update-slice_fusion.2.refs_1_, ...), custom_call_target="tpu_custom_call" | custom-call | flops 8631877632 | bytes 12845056 | tf_op jit(solution)/shard_map/ladder/pallas_call | solution.py:134
  80.0 0.2 collective-permute-start.24
  80.2 0.4 collective-permute-start.20
  80.6 2.0 %collective-permute-done.24 = f32[4,56,896]{2,1,0:T(8,128)S(1)} collective-permute-done((f32[4,56,896]{2,1,0:T(8,128)}, f32[4,56,896]{2,1,0:T(8,128)S(1)}, u32[]{:S(2)}, u32[]{:S(2)}) %collective-permute-start.24) | collective-permute-done | bytes 802848 | tf_op jit(solution)/shard_map/reduce/ppermute | solution.py:34
  82.6 1.2 %add.47 = f32[4,56,896]{2,1,0:T(8,128)S(1)} add(f32[4,56,896]{2,1,0:T(8,128)} %get-tuple-element.41, f32[4,56,896]{2,1,0:T(8,128)S(1)} %collective-permute-done.24) | non-fusion elementwise | flops 200704 | bytes 2408448 | tf_op jit(solution)/shard_map/reduce/add | solution.py:208
  83.8 1.1 collective-permute-start.25
  84.9 2.5 %collective-permute-start.27 = (f32[56,896]{1,0:T(8,128)S(1)}, f32[56,896]{1,0:T(8,128)S(1)}, u32[]{:S(2)}, u32[]{:S(2)}) collective-permute-start(f32[56,896]{1,0:T(8,128)S(1)} %get-tuple-element.47), channel_id=1, source_target_pairs={{0,6},{1,7},{2,0},{3,1},{4,2},{5,3},{6,4},{7,5},{8,14},{9,15},{10,... | collective-permute-start | bytes 602120 | tf_op jit(solution)/shard_map/reduce/ppermute | solution.py:34
  87.4 0.3 collective-permute-start.26
  87.7 0.0 collective-permute-done.20
  87.7 0.1 add.43
  87.8 1.1 collective-permute-start.21
  88.9 2.2 %collective-permute-start.23 = (f32[56,896]{1,0:T(8,128)S(1)}, f32[56,896]{1,0:T(8,128)S(1)}, u32[]{:S(2)}, u32[]{:S(2)}) collective-permute-start(f32[56,896]{1,0:T(8,128)S(1)} %get-tuple-element.44), channel_id=1, source_target_pairs={{0,6},{1,7},{2,0},{3,1},{4,2},{5,3},{6,4},{7,5},{8,14},{9,15},{10,... | collective-permute-start | bytes 602120 | tf_op jit(solution)/shard_map/reduce/ppermute | solution.py:34
  91.1 6.4 %collective-permute-done.25 = f32[56,896]{1,0:T(8,128)S(1)} collective-permute-done((f32[56,896]{1,0:T(8,128)S(1)}, f32[56,896]{1,0:T(8,128)S(1)}, u32[]{:S(2)}, u32[]{:S(2)}) %collective-permute-start.25) | collective-permute-done | bytes 200736 | tf_op jit(solution)/shard_map/reduce/ppermute | solution.py:34
  97.5 0.0 collective-permute-start.22
  97.5 0.0 collective-permute-done.27
  97.5 0.1 fusion.2
  97.6 1.9 %collective-permute-start.28 = (f32[56,896]{1,0:T(8,128)S(1)}, f32[56,896]{1,0:T(8,128)S(1)}, u32[]{:S(2)}, u32[]{:S(2)}) collective-permute-start(f32[56,896]{1,0:T(8,128)S(1)} %fusion.2), channel_id=1, source_target_pairs={{0,8},{1,9},{2,10},{3,11},{4,12},{5,13},{6,14},{7,15},{8,0},{9,1},... | collective-permute-start | bytes 602120 | tf_op jit(solution)/shard_map/reduce/ppermute | solution.py:34
  99.4 2.4 %collective-permute-done.21 = f32[56,896]{1,0:T(8,128)S(1)} collective-permute-done((f32[56,896]{1,0:T(8,128)S(1)}, f32[56,896]{1,0:T(8,128)S(1)}, u32[]{:S(2)}, u32[]{:S(2)}) %collective-permute-start.21) | collective-permute-done | bytes 200736 | tf_op jit(solution)/shard_map/reduce/ppermute | solution.py:34
  101.8 2.8 %collective-permute-done.23 = f32[56,896]{1,0:T(8,128)S(1)} collective-permute-done((f32[56,896]{1,0:T(8,128)S(1)}, f32[56,896]{1,0:T(8,128)S(1)}, u32[]{:S(2)}, u32[]{:S(2)}) %collective-permute-start.23) | collective-permute-done | bytes 200736 | tf_op jit(solution)/shard_map/reduce/ppermute | solution.py:34
  104.6 0.7 collective-permute-done.22
  105.3 4.0 %collective-permute-done.28 = f32[56,896]{1,0:T(8,128)S(1)} collective-permute-done((f32[56,896]{1,0:T(8,128)S(1)}, f32[56,896]{1,0:T(8,128)S(1)}, u32[]{:S(2)}, u32[]{:S(2)}) %collective-permute-start.28) | collective-permute-done | bytes 200736 | tf_op jit(solution)/shard_map/reduce/ppermute | solution.py:34
  109.3 0.1 fusion.7
  109.4 0.9 copy.3
  (24 shorter events, 0.2 us)
Async XLA Ops:
  0.9 3.1 %copy-start = (f32[1,56,896]{2,1,0:T(8,128)S(1)}, f32[1,56,896]{2,1,0:T(8,128)}, u32[]{:S(2)}) copy-start(f32[1,56,896]{2,1,0:T(8,128)} %param.3) | copy-start | bytes 602116
  1.0 1.5 %collective-permute-start = (f32[56,896]{1,0:T(8,128)S(1)}, f32[56,896]{1,0:T(8,128)S(1)}, u32[]{:S(2)}, u32[]{:S(2)}) collective-permute-start(f32[56,896]{1,0:T(8,128)S(1)} %bitcast.48), channel_id=1, source_target_pairs={{0,1},{1,0},{2,3},{3,2},{4,5},{5,4},{6,7},{7,6},{8,9},{9,8},{10,11... | collective-permute-start | bytes 602120 | tf_op jit(solution)/shard_map/gather/ppermute | solution.py:34
  2.5 16.5 %collective-permute-start.1 = (f32[112,896]{1,0:T(8,128)S(1)}, f32[112,896]{1,0:T(8,128)S(1)}, u32[]{:S(2)}, u32[]{:S(2)}) collective-permute-start(f32[112,896]{1,0:T(8,128)S(1)} %pad_maximum_fusion.1.refs_0_), channel_id=1, source_target_pairs={{0,2},{1,7},{2,4},{3,1},{4,6},{5,3},{6,0},{7,5},{8,10},{9,15},{10,... | collective-permute-start | bytes 1204232 | tf_op jit(solution)/shard_map/gather/ppermute | solution.py:34
  4.1 12.5 %collective-permute-start.5 = (f32[56,896]{1,0:T(8,128)S(1)}, f32[56,896]{1,0:T(8,128)S(1)}, u32[]{:S(2)}, u32[]{:S(2)}) collective-permute-start(f32[56,896]{1,0:T(8,128)S(1)} %bitcast.43), channel_id=1, source_target_pairs={{0,128},{16,144},{32,160},{48,176},{64,192},{80,208},{96,224},{112... | collective-permute-start | bytes 602120 | tf_op jit(solution)/shard_map/gather/ppermute | solution.py:24
  7.4 10.1 %collective-permute-start.4 = (f32[56,896]{1,0:T(8,128)S(1)}, f32[56,896]{1,0:T(8,128)S(1)}, u32[]{:S(2)}, u32[]{:S(2)}) collective-permute-start(f32[56,896]{1,0:T(8,128)S(1)} %bitcast.44), channel_id=1, source_target_pairs={{0,64},{16,80},{32,96},{48,112},{64,0},{80,16},{96,32},{112,48},{1... | collective-permute-start | bytes 602120 | tf_op jit(solution)/shard_map/gather/ppermute | solution.py:24
  7.5 10.0 %collective-permute-start.3 = (f32[56,896]{1,0:T(8,128)S(1)}, f32[56,896]{1,0:T(8,128)S(1)}, u32[]{:S(2)}, u32[]{:S(2)}) collective-permute-start(f32[56,896]{1,0:T(8,128)S(1)} %bitcast.45), channel_id=1, source_target_pairs={{0,48},{16,0},{32,16},{48,32},{64,112},{80,64},{96,80},{112,96},{1... | collective-permute-start | bytes 602120 | tf_op jit(solution)/shard_map/gather/ppermute | solution.py:24
  10.5 8.6 %collective-permute-start.2 = (f32[56,896]{1,0:T(8,128)S(1)}, f32[56,896]{1,0:T(8,128)S(1)}, u32[]{:S(2)}, u32[]{:S(2)}) collective-permute-start(f32[56,896]{1,0:T(8,128)S(1)} %bitcast.46), channel_id=1, source_target_pairs={{0,16},{16,32},{32,48},{48,0},{64,80},{80,96},{96,112},{112,64},{1... | collective-permute-start | bytes 602120 | tf_op jit(solution)/shard_map/gather/ppermute | solution.py:24
  19.1 21.9 %copy-start.4 = (f32[112,896]{1,0:T(8,128)}, f32[112,896]{1,0:T(8,128)S(1)}, u32[]{:S(2)}) copy-start(f32[112,896]{1,0:T(8,128)S(1)} %constant_dynamic-update-slice_fusion.refs_12_) | copy-start | bytes 1204228
  19.1 21.7 %collective-permute-start.8 = (f32[112,896]{1,0:T(8,128)S(1)}, f32[112,896]{1,0:T(8,128)S(1)}, u32[]{:S(2)}, u32[]{:S(2)}) collective-permute-start(f32[112,896]{1,0:T(8,128)S(1)} %constant_dynamic-update-slice_fusion.refs_12_), channel_id=1, source_target_pairs={{0,48},{16,0},{32,16},{48,32},{64,112},{80,64},{96,80},{112,96},{1... | collective-permute-start | bytes 1204232 | tf_op jit(solution)/shard_map/gather/ppermute | solution.py:24
  20.7 20.1 %collective-permute-start.7 = (f32[112,896]{1,0:T(8,128)S(1)}, f32[112,896]{1,0:T(8,128)S(1)}, u32[]{:S(2)}, u32[]{:S(2)}) collective-permute-start(f32[112,896]{1,0:T(8,128)S(1)} %constant_dynamic-update-slice_fusion.refs_12_), channel_id=1, source_target_pairs={{0,16},{16,32},{32,48},{48,0},{64,80},{80,96},{96,112},{112,64},{1... | collective-permute-start | bytes 1204232 | tf_op jit(solution)/shard_map/gather/ppermute | solution.py:24
  21.2 19.6 %collective-permute-start.9 = (f32[56,896]{1,0:T(8,128)S(1)}, f32[56,896]{1,0:T(8,128)S(1)}, u32[]{:S(2)}, u32[]{:S(2)}) collective-permute-start(f32[56,896]{1,0:T(8,128)S(1)} %collective-permute-done.5), channel_id=1, source_target_pairs={{0,64},{16,80},{32,96},{48,112},{64,0},{80,16},{96,32},{112,48},{1... | collective-permute-start | bytes 602120 | tf_op jit(solution)/shard_map/gather/ppermute | solution.py:24
  23.0 17.8 %collective-permute-start.10 = (f32[56,896]{1,0:T(8,128)S(1)}, f32[56,896]{1,0:T(8,128)S(1)}, u32[]{:S(2)}, u32[]{:S(2)}) collective-permute-start(f32[56,896]{1,0:T(8,128)S(1)} %bitcast.50), channel_id=1, source_target_pairs={{0,8},{1,9},{2,10},{3,11},{4,12},{5,13},{6,14},{7,15},{8,0},{9,1},... | collective-permute-start | bytes 602120 | tf_op jit(solution)/shard_map/gather/ppermute | solution.py:34
  27.5 13.3 %collective-permute-start.6 = (f32[56,896]{1,0:T(8,128)S(1)}, f32[56,896]{1,0:T(8,128)S(1)}, u32[]{:S(2)}, u32[]{:S(2)}) collective-permute-start(f32[56,896]{1,0:T(8,128)S(1)} %collective-permute-done.2.refs_9_), channel_id=1, source_target_pairs={{0,16},{16,32},{32,48},{48,0},{64,80},{80,96},{96,112},{112,64},{1... | collective-permute-start | bytes 602120 | tf_op jit(solution)/shard_map/gather/ppermute | solution.py:24
  40.8 3.8 %copy-start.3 = (f32[112,896]{1,0:T(8,128)}, f32[112,896]{1,0:T(8,128)S(1)}, u32[]{:S(2)}) copy-start(f32[112,896]{1,0:T(8,128)S(1)} %collective-permute-done.8.refs_14_) | copy-start | bytes 1204228
  40.8 3.8 %copy-start.2 = (f32[112,896]{1,0:T(8,128)}, f32[112,896]{1,0:T(8,128)S(1)}, u32[]{:S(2)}) copy-start(f32[112,896]{1,0:T(8,128)S(1)} %collective-permute-done.7.refs_13_) | copy-start | bytes 1204228
  40.8 1.5 %collective-permute-start.11 = (f32[56,896]{1,0:T(8,128)S(1)}, f32[56,896]{1,0:T(8,128)S(1)}, u32[]{:S(2)}, u32[]{:S(2)}) collective-permute-start(f32[56,896]{1,0:T(8,128)S(1)} %collective-permute-done.10), channel_id=1, source_target_pairs={{0,1},{1,0},{2,3},{3,2},{4,5},{5,4},{6,7},{7,6},{8,9},{9,8},{10,11... | collective-permute-start | bytes 602120 | tf_op jit(solution)/shard_map/gather/ppermute | solution.py:34
  41.0 13.5 %collective-permute-start.15 = (f32[112,896]{1,0:T(8,128)S(1)}, f32[112,896]{1,0:T(8,128)}, u32[]{:S(2)}, u32[]{:S(2)}) collective-permute-start(f32[112,896]{1,0:T(8,128)S(1)} %pad_maximum_fusion), channel_id=1, source_target_pairs={{0,4},{1,5},{2,6},{3,7},{4,0},{5,1},{6,2},{7,3},{8,12},{9,13},{10,... | collective-permute-start | bytes 1204232 | tf_op jit(solution)/shard_map/gather/ppermute | solution.py:34
  42.4 16.2 %collective-permute-start.12 = (f32[112,896]{1,0:T(8,128)S(1)}, f32[112,896]{1,0:T(8,128)S(1)}, u32[]{:S(2)}, u32[]{:S(2)}) collective-permute-start(f32[112,896]{1,0:T(8,128)S(1)} %constant_dynamic-update-slice_fusion.2.refs_1_), channel_id=1, source_target_pairs={{0,2},{1,7},{2,4},{3,1},{4,6},{5,3},{6,0},{7,5},{8,10},{9,15},{10,... | collective-permute-start | bytes 1204232 | tf_op jit(solution)/shard_map/gather/ppermute | solution.py:34
  42.7 15.9 %collective-permute-start.19 = (f32[56,896]{1,0:T(8,128)S(1)}, f32[56,896]{1,0:T(8,128)S(1)}, u32[]{:S(2)}, u32[]{:S(2)}) collective-permute-start(f32[56,896]{1,0:T(8,128)S(1)} %collective-permute-done.9.refs_15_), channel_id=1, source_target_pairs={{0,32},{16,48},{32,0},{48,16},{64,96},{80,112},{96,64},{112,80},{1... | collective-permute-start | bytes 602120 | tf_op jit(solution)/shard_map/gather/ppermute | solution.py:24
  44.6 0.9 slice-start
  46.3 14.0 %collective-permute-start.18 = (f32[112,896]{1,0:T(8,128)}, f32[112,896]{1,0:T(8,128)}, u32[]{:S(2)}, u32[]{:S(2)}) collective-permute-start(f32[112,896]{1,0:T(8,128)} %get-tuple-element.49), channel_id=1, source_target_pairs={{0,48},{16,0},{32,16},{48,32},{64,112},{80,64},{96,80},{112,96},{1... | collective-permute-start | bytes 1204232 | tf_op jit(solution)/shard_map/gather/ppermute | solution.py:24
  47.4 13.0 %collective-permute-start.17 = (f32[112,896]{1,0:T(8,128)S(1)}, f32[112,896]{1,0:T(8,128)}, u32[]{:S(2)}, u32[]{:S(2)}) collective-permute-start(f32[112,896]{1,0:T(8,128)S(1)} %get-tuple-element.50), channel_id=1, source_target_pairs={{0,16},{16,32},{32,48},{48,0},{64,80},{80,96},{96,112},{112,64},{1... | collective-permute-start | bytes 1204232 | tf_op jit(solution)/shard_map/gather/ppermute | solution.py:24
  54.5 5.9 %collective-permute-start.16 = (f32[112,896]{1,0:T(8,128)}, f32[112,896]{1,0:T(8,128)}, u32[]{:S(2)}, u32[]{:S(2)}) collective-permute-start(f32[112,896]{1,0:T(8,128)} %collective-permute-done.15.refs_6_), channel_id=1, source_target_pairs={{0,1},{1,0},{2,3},{3,2},{4,5},{5,4},{6,7},{7,6},{8,9},{9,8},{10,11... | collective-permute-start | bytes 1204232 | tf_op jit(solution)/shard_map/gather/ppermute | solution.py:34
  58.5 1.9 %collective-permute-start.13 = (f32[112,896]{1,0:T(8,128)S(1)}, f32[112,896]{1,0:T(8,128)}, u32[]{:S(2)}, u32[]{:S(2)}) collective-permute-start(f32[112,896]{1,0:T(8,128)S(1)} %collective-permute-done.1.refs_2_), channel_id=1, source_target_pairs={{0,1},{1,0},{2,3},{3,2},{4,5},{5,4},{6,7},{7,6},{8,9},{9,8},{10,11... | collective-permute-start | bytes 1204232 | tf_op jit(solution)/shard_map/gather/ppermute | solution.py:34
  58.6 2.4 %collective-permute-start.14 = (f32[112,896]{1,0:T(8,128)S(1)}, f32[112,896]{1,0:T(8,128)}, u32[]{:S(2)}, u32[]{:S(2)}) collective-permute-start(f32[112,896]{1,0:T(8,128)S(1)} %collective-permute-done.12.refs_3_), channel_id=1, source_target_pairs={{0,1},{1,0},{2,3},{3,2},{4,5},{5,4},{6,7},{7,6},{8,9},{9,8},{10,11... | collective-permute-start | bytes 1204232 | tf_op jit(solution)/shard_map/gather/ppermute | solution.py:34
  80.0 2.6 %collective-permute-start.24 = (f32[4,56,896]{2,1,0:T(8,128)}, f32[4,56,896]{2,1,0:T(8,128)S(1)}, u32[]{:S(2)}, u32[]{:S(2)}) collective-permute-start(f32[4,56,896]{2,1,0:T(8,128)} %get-tuple-element.42), channel_id=1, source_target_pairs={{0,1},{1,0},{2,3},{3,2},{4,5},{5,4},{6,7},{7,6},{8,9},{9,8},{10,11... | collective-permute-start | bytes 2408456 | tf_op jit(solution)/shard_map/reduce/ppermute | solution.py:34
  80.2 7.5 %collective-permute-start.20 = (f32[4,56,896]{2,1,0:T(8,128)}, f32[4,56,896]{2,1,0:T(8,128)S(1)}, u32[]{:S(2)}, u32[]{:S(2)}) collective-permute-start(f32[4,56,896]{2,1,0:T(8,128)} %get-tuple-element.40), channel_id=1, source_target_pairs={{0,1},{1,0},{2,3},{3,2},{4,5},{5,4},{6,7},{7,6},{8,9},{9,8},{10,11... | collective-permute-start | bytes 2408456 | tf_op jit(solution)/shard_map/reduce/ppermute | solution.py:34
  83.8 3.9 %copy-start.1 = (f32[4,56,896]{2,1,0:T(8,128)S(1)}, f32[4,56,896]{2,1,0:T(8,128)}, u32[]{:S(2)}) copy-start(f32[4,56,896]{2,1,0:T(8,128)} %get-tuple-element.39) | copy-start | bytes 2408452
  83.8 13.6 %collective-permute-start.25 = (f32[56,896]{1,0:T(8,128)S(1)}, f32[56,896]{1,0:T(8,128)S(1)}, u32[]{:S(2)}, u32[]{:S(2)}) collective-permute-start(f32[56,896]{1,0:T(8,128)S(1)} %get-tuple-element.46), channel_id=1, source_target_pairs={{0,2},{1,3},{2,4},{3,5},{4,6},{5,7},{6,0},{7,1},{8,10},{9,11},{10,... | collective-permute-start | bytes 602120 | tf_op jit(solution)/shard_map/reduce/ppermute | solution.py:34
  84.9 12.6 %collective-permute-start.27 = (f32[56,896]{1,0:T(8,128)S(1)}, f32[56,896]{1,0:T(8,128)S(1)}, u32[]{:S(2)}, u32[]{:S(2)}) collective-permute-start(f32[56,896]{1,0:T(8,128)S(1)} %get-tuple-element.47), channel_id=1, source_target_pairs={{0,6},{1,7},{2,0},{3,1},{4,2},{5,3},{6,4},{7,5},{8,14},{9,15},{10,... | collective-permute-start | bytes 602120 | tf_op jit(solution)/shard_map/reduce/ppermute | solution.py:34
  87.4 10.1 %collective-permute-start.26 = (f32[56,896]{1,0:T(8,128)S(1)}, f32[56,896]{1,0:T(8,128)S(1)}, u32[]{:S(2)}, u32[]{:S(2)}) collective-permute-start(f32[56,896]{1,0:T(8,128)S(1)} %get-tuple-element.48), channel_id=1, source_target_pairs={{0,4},{1,5},{2,6},{3,7},{4,0},{5,1},{6,2},{7,3},{8,12},{9,13},{10,... | collective-permute-start | bytes 602120 | tf_op jit(solution)/shard_map/reduce/ppermute | solution.py:34
  87.8 14.0 %collective-permute-start.21 = (f32[56,896]{1,0:T(8,128)S(1)}, f32[56,896]{1,0:T(8,128)S(1)}, u32[]{:S(2)}, u32[]{:S(2)}) collective-permute-start(f32[56,896]{1,0:T(8,128)S(1)} %get-tuple-element.43), channel_id=1, source_target_pairs={{0,2},{1,3},{2,4},{3,5},{4,6},{5,7},{6,0},{7,1},{8,10},{9,11},{10,... | collective-permute-start | bytes 602120 | tf_op jit(solution)/shard_map/reduce/ppermute | solution.py:34
  88.9 15.7 %collective-permute-start.23 = (f32[56,896]{1,0:T(8,128)S(1)}, f32[56,896]{1,0:T(8,128)S(1)}, u32[]{:S(2)}, u32[]{:S(2)}) collective-permute-start(f32[56,896]{1,0:T(8,128)S(1)} %get-tuple-element.44), channel_id=1, source_target_pairs={{0,6},{1,7},{2,0},{3,1},{4,2},{5,3},{6,4},{7,5},{8,14},{9,15},{10,... | collective-permute-start | bytes 602120 | tf_op jit(solution)/shard_map/reduce/ppermute | solution.py:34
  97.5 7.8 %collective-permute-start.22 = (f32[56,896]{1,0:T(8,128)S(1)}, f32[56,896]{1,0:T(8,128)S(1)}, u32[]{:S(2)}, u32[]{:S(2)}) collective-permute-start(f32[56,896]{1,0:T(8,128)S(1)} %get-tuple-element.45), channel_id=1, source_target_pairs={{0,4},{1,5},{2,6},{3,7},{4,0},{5,1},{6,2},{7,3},{8,12},{9,13},{10,... | collective-permute-start | bytes 602120 | tf_op jit(solution)/shard_map/reduce/ppermute | solution.py:34
  97.6 11.7 %collective-permute-start.28 = (f32[56,896]{1,0:T(8,128)S(1)}, f32[56,896]{1,0:T(8,128)S(1)}, u32[]{:S(2)}, u32[]{:S(2)}) collective-permute-start(f32[56,896]{1,0:T(8,128)S(1)} %fusion.2), channel_id=1, source_target_pairs={{0,8},{1,9},{2,10},{3,11},{4,12},{5,13},{6,14},{7,15},{8,0},{9,1},... | collective-permute-start | bytes 602120 | tf_op jit(solution)/shard_map/reduce/ppermute | solution.py:34
